TPU v7x, 32 devices: a whole 2x2x4 slice. The times are simulated.
32 devices in a mesh: energy: 8 (over y, x, core), dom: 4 (over z).
Axes of the slice: x: 2, y: 2, z: 4, core: 2. Of those that a mesh axis runs over, the one named last changes fastest.
Arguments:
- pivots: float32 [8, 32, 320, 320], P('energy', 'dom'), may hold values from -0.0125 to 1.4125
- lower_spikes: float32 [8, 32, 320, 320], P('energy', 'dom'), may hold values from -0.0125 to 1.0025
- upper_spikes: float32 [8, 32, 320, 320], P('energy', 'dom'), may hold values from -0.0125 to 1.0025
- potential: float32 [32, 320, 320], P('dom', 'energy'), may hold values from -0.3125 to 0.3125
- grain_of_slice: int32 [32], P('dom'), may hold values from 0 to 31
- grain_shift: float32 [32], replicated, may hold values from 0.5 to 1.5
- probes: float32 [32, 320, 128], P('dom'), may hold values from -6 to 6
- weights: float32 [8], P('energy'), may hold values from 0.5 to 2
Outputs:
- response: float32 [32, 320], P('dom', 'energy')
All inputs are finite; a program needn't handle non-finite values.
Results may differ from a plain program's by a relative error of at most 0.00021.
Values sent between devices are 32-bit elements; how exact they have to be, the bound alone decides.
No kernel may reach another device: no remote copies, remote signals or barrier semaphores. Data moves between devices by JAX's collectives and lax.ppermute only.
A program may use at most 128 MiB of HBM per device.

v0:
```python
import jax
import jax.numpy as jnp
from jax import lax
from jax.sharding import PartitionSpec as P

PROBES = 128


HIGHEST = lax.Precision.HIGHEST


def from_behind(x, axis, by):
    peers = lax.axis_size(axis)
    pairs = [(i, i + by) for i in range(peers) if 0 <= i + by < peers]
    return lax.ppermute(x, axis, pairs)


def sweep(blocks, given_rows, carried, backward):

    def sweep_advance(current, inputs_pair):
        matrix_block, given_value = inputs_pair
        current = given_value - jnp.dot(matrix_block, current, precision=HIGHEST)
        return (current, current)

    return lax.scan(sweep_advance, carried, (blocks, given_rows), reverse=backward)


def transfer(blocks, backward):
    orbitals = blocks.shape[1]

    def transfer_advance(current, matrix_block):
        return (-jnp.dot(matrix_block, current, precision=HIGHEST), None)

    result, _ = lax.scan(
        transfer_advance, jnp.eye(orbitals, dtype=jnp.float32), blocks, reverse=backward
    )
    return result


def boundary_value(matrix, offset, backward):
    zero_block = jnp.zeros(offset.shape, jnp.float32)
    inflow = zero_block
    direction = -1 if backward else 1
    for repeat in range(lax.axis_size("dom") - 1):
        outgoing = offset + jnp.dot(matrix, inflow, precision=HIGHEST)
        inflow = from_behind(outgoing, "dom", direction)
    return inflow


def solve(pivot_blocks, lower_blocks, upper_blocks, right_side, forward_map, backward_map):
    solved_pivot = jnp.einsum("sij,sjk->sik", pivot_blocks, right_side, precision=HIGHEST)
    zero_block = jnp.zeros(right_side.shape[1:], jnp.float32)
    last_local, _ = sweep(lower_blocks, solved_pivot, zero_block, False)
    inflow = boundary_value(forward_map, last_local, False)
    _, climbed = sweep(lower_blocks, solved_pivot, inflow, False)
    first_local, _ = sweep(upper_blocks, climbed, zero_block, True)
    outflow = boundary_value(backward_map, first_local, True)
    _, result = sweep(upper_blocks, climbed, outflow, True)
    return result


def per_device(
    pivots, lower_spikes, upper_spikes, potential, grain_of_slice, grain_shift, probes, weights
):
    pivot_blocks = pivots[0]
    lower_blocks = lower_spikes[0]
    upper_blocks = upper_spikes[0]
    grain_count = grain_shift.shape[0]
    grain_match = grain_of_slice[:, None] == jnp.arange(grain_count, dtype=jnp.int32)[None, :]
    grain_scale = jnp.sum(jnp.where(grain_match, grain_shift[None, :], 0.0), axis=1)
    gathered = lax.all_gather(potential, "energy", axis=1, tiled=True)
    perturb = gathered * grain_scale[:, None, None]
    forward_map = transfer(lower_blocks, False)
    backward_map = transfer(upper_blocks, True)
    first_solve = solve(pivot_blocks, lower_blocks, upper_blocks, probes, forward_map, backward_map)
    driven = jnp.einsum("sij,sjk->sik", perturb, first_solve, precision=HIGHEST)
    second_solve = solve(
        pivot_blocks, lower_blocks, upper_blocks, driven, forward_map, backward_map
    )
    energies = lax.axis_size("energy")
    charge_terms = weights[0] * jnp.sum(second_solve * probes, axis=2) / (PROBES * energies)
    return lax.psum_scatter(charge_terms, "energy", scatter_dimension=1, tiled=True)


def solution(mesh):
    placed = (
        P("energy", "dom", None, None),
        P("energy", "dom", None, None),
        P("energy", "dom", None, None),
        P("dom", "energy", None),
        P("dom"),
        P(),
        P("dom", None, None),
        P("energy"),
    )
    return jax.shard_map(
        per_device, mesh=mesh, in_specs=placed, out_specs=P("dom", "energy"), check_vma=False
    )
```

profile of v0, /device:TPU:0, one launch (start us, length us, event | category | flops | bytes accessed | tf_op | source)
XLA Modules:
  0.0 300.6 jit_solution(8603632055038924896)
XLA Ops:
  6.6 6.0 %fusion.48 = f32[8,320,128]{2,1,0:T(8,128)S(1)} fusion(f32[8,320,128]{2,1,0:T(8,128)} %param.34, f32[1,8,320,320]{3,2,1,0:T(8,128)} %param.28), kind=kOutput, calls=%fused_computation.62 | convolution fusion | flops 1258291200 | bytes 5898240 | tf_op jit(solution)/shard_map/sij,sjk->sik/dot_general | solution.py:51
  12.6 13.0 %while.138 = (s32[]{:T(128)}, f32[320,128]{1,0:T(8,128)S(1)}, f32[8,320,128]{2,1,0:T(8,128)S(1)}, f32[8,320,320]{2,1,0:T(8,128)}, s32[]{:T(128)}, /*index=5*/s32[]{:T(128)}) while((s32[]{:T(128)}, f32[320,128]{1,0:T(8,128)S(1)}, f32[8,320,128]{2,1,0:T(8,128)S(1)}, f32[8,320,320]{2,1,0:T(8,128)}, s32[]{:T(128)}, ...), condition=%wide.region_2.3_spmd.clone, body=%wide.region_1.2_spmd.clone.sunk | while | flops 157368320 | bytes 1311823 | solution.py:25
  26.7 17.4 %while.132 = (s32[]{:T(128)}, f32[320,320]{1,0:T(8,128)S(1)}, f32[8,320,320]{2,1,0:T(8,128)}, s32[]{:T(128)}) while((s32[]{:T(128)}, f32[320,320]{1,0:T(8,128)S(1)}, f32[8,320,320]{2,1,0:T(8,128)}, s32[]{:T(128)}) %tuple.278), condition=%wide.region_4.5_spmd, body=%wide.region_3.4_spmd.sunk | while | flops 393318400 | bytes 2130485 | solution.py:34
  44.7 4.9 %collective-permute-start = (f32[320,128]{1,0:T(8,128)S(1)}, f32[320,128]{1,0:T(8,128)S(1)}, u32[]{:S(2)}, u32[]{:S(2)}) collective-permute-start(f32[320,128]{1,0:T(8,128)S(1)} %get-tuple-element.721), channel_id=1, source_target_pairs={{0,1},{1,2},{2,3},{4,5},{5,6},{6,7},{8,9},{9,10},{10,11},{12,13},{... | collective-permute-start | bytes 491528 | tf_op jit(solution)/shard_map/ppermute | solution.py:15
  49.6 3.4 %collective-permute-done = f32[320,128]{1,0:T(8,128)S(1)} collective-permute-done((f32[320,128]{1,0:T(8,128)S(1)}, f32[320,128]{1,0:T(8,128)S(1)}, u32[]{:S(2)}, u32[]{:S(2)}) %collective-permute-start) | collective-permute-done | bytes 163872 | tf_op jit(solution)/shard_map/ppermute | solution.py:15
  53.6 4.4 %collective-permute-start.1 = (f32[320,128]{1,0:T(8,128)S(1)}, f32[320,128]{1,0:T(8,128)S(1)}, u32[]{:S(2)}, u32[]{:S(2)}) collective-permute-start(f32[320,128]{1,0:T(8,128)S(1)} %convolution_add_fusion.7), channel_id=1, source_target_pairs={{0,1},{1,2},{2,3},{4,5},{5,6},{6,7},{8,9},{9,10},{10,11},{12,13},{... | collective-permute-start | bytes 491528 | tf_op jit(solution)/shard_map/ppermute | solution.py:15
  58.0 2.8 collective-permute-done.1
  61.4 4.4 %collective-permute-start.2 = (f32[320,128]{1,0:T(8,128)S(1)}, f32[320,128]{1,0:T(8,128)S(1)}, u32[]{:S(2)}, u32[]{:S(2)}) collective-permute-start(f32[320,128]{1,0:T(8,128)S(1)} %convolution_add_fusion.6), channel_id=1, source_target_pairs={{0,1},{1,2},{2,3},{4,5},{5,6},{6,7},{8,9},{9,10},{10,11},{12,13},{... | collective-permute-start | bytes 491528 | tf_op jit(solution)/shard_map/ppermute | solution.py:15
  65.8 17.6 %while.134 = (s32[]{:T(128)}, f32[320,320]{1,0:T(8,128)S(1)}, f32[8,320,320]{2,1,0:T(8,128)}, s32[]{:T(128)}, s32[]{:T(128)}) while((s32[]{:T(128)}, f32[320,320]{1,0:T(8,128)S(1)}, f32[8,320,320]{2,1,0:T(8,128)}, s32[]{:T(128)}, s32[]{:T(128)}) %tuple.282), condition=%wide.region_10.11_spmd, body=%wide.region_9.10_spmd.sunk | while | flops 393318400 | bytes 2129997 | solution.py:34
  78.9 2.3 convolution_negate_fusion.5
  83.5 13.3 %while.133 = (s32[]{:T(128)}, f32[320,128]{1,0:T(8,128)S(1)}, f32[8,320,128]{2,1,0:T(8,128)S(1)}, f32[8,320,128]{2,1,0:T(8,128)}, f32[8,320,320]{2,1,0:T(8,128)}, /*index=5*/s32[]{:T(128)}) while((s32[]{:T(128)}, f32[320,128]{1,0:T(8,128)S(1)}, f32[8,320,128]{2,1,0:T(8,128)S(1)}, f32[8,320,128]{2,1,0:T(8,128)}, f32[8,320,320]{2,1,0:T(8,128)}, ...), condition=%wide.region_6.7_spmd, body=%wide.region_5.6_spmd.sunk | while | flops 157327360 | bytes 1475653 | solution.py:25
  96.8 13.0 %while.139 = (s32[]{:T(128)}, f32[320,128]{1,0:T(8,128)S(1)}, f32[8,320,128]{2,1,0:T(8,128)S(1)}, f32[8,320,320]{2,1,0:T(8,128)}, s32[]{:T(128)}, /*index=5*/s32[]{:T(128)}, s32[]{:T(128)}) while((s32[]{:T(128)}, f32[320,128]{1,0:T(8,128)S(1)}, f32[8,320,128]{2,1,0:T(8,128)S(1)}, f32[8,320,320]{2,1,0:T(8,128)}, s32[]{:T(128)}, ...), condition=%wide.region_8.9_spmd.clone, body=%wide.region_7.8_spmd.clone.sunk | while | flops 157368320 | bytes 1312354 | solution.py:25
  111.7 5.9 %collective-permute-done.3 = f32[320,128]{1,0:T(8,128)S(1)} collective-permute-done((f32[320,128]{1,0:T(8,128)S(1)}, f32[320,128]{1,0:T(8,128)S(1)}, u32[]{:S(2)}, u32[]{:S(2)}) %collective-permute-start.3) | collective-permute-done | bytes 163872 | tf_op jit(solution)/shard_map/ppermute | solution.py:15
  119.5 5.9 %collective-permute-done.4 = f32[320,128]{1,0:T(8,128)S(1)} collective-permute-done((f32[320,128]{1,0:T(8,128)S(1)}, f32[320,128]{1,0:T(8,128)S(1)}, u32[]{:S(2)}, u32[]{:S(2)}) %collective-permute-start.4) | collective-permute-done | bytes 163872 | tf_op jit(solution)/shard_map/ppermute | solution.py:15
  127.6 5.5 %collective-permute-done.5 = f32[320,128]{1,0:T(8,128)S(1)} collective-permute-done((f32[320,128]{1,0:T(8,128)S(1)}, f32[320,128]{1,0:T(8,128)S(1)}, u32[]{:S(2)}, u32[]{:S(2)}) %collective-permute-start.5) | collective-permute-done | bytes 163872 | tf_op jit(solution)/shard_map/ppermute | solution.py:15
  134.3 18.2 %while.135 = (s32[]{:T(128)}, f32[320,128]{1,0:T(8,128)S(1)}, f32[8,320,128]{2,1,0:T(8,128)}, f32[8,320,128]{2,1,0:T(8,128)S(1)}, f32[8,320,320]{2,1,0:T(8,128)}, /*index=5*/s32[]{:T(128)}, s32[]{:T(128)}) while((s32[]{:T(128)}, f32[320,128]{1,0:T(8,128)S(1)}, f32[8,320,128]{2,1,0:T(8,128)}, f32[8,320,128]{2,1,0:T(8,128)S(1)}, ...), condition=%wide.region_12.13_spmd, body=%wide.region_11.12_spmd.sunk | while | flops 157327360 | bytes 1475673 | solution.py:25
  134.3 2.3 bitcast_dynamic-update-slice_fusion.9
  136.6 2.2 bitcast_dynamic-update-slice_fusion.9
  138.9 2.2 bitcast_dynamic-update-slice_fusion.9
  141.1 2.3 bitcast_dynamic-update-slice_fusion.9
  143.4 2.3 bitcast_dynamic-update-slice_fusion.9
  145.7 2.3 bitcast_dynamic-update-slice_fusion.9
  148.0 2.2 bitcast_dynamic-update-slice_fusion.9
  150.2 2.3 bitcast_dynamic-update-slice_fusion.9
  152.5 6.7 %fusion.50 = f32[8,320,128]{2,1,0:T(8,128)S(1)} fusion(f32[8,320,128]{2,1,0:T(8,128)} %get-tuple-element.564, f32[8,320,320]{2,1,0:T(8,128)} %all-gather.2.cloned.1.call-done, f32[8]{0:T(128)S(1)} %select_reduce_fusion), kind=kOutput, calls=%fused_computation.64 | convolution fusion | flops 1259110400 | bytes 5898272 | tf_op jit(solution)/shard_map/sij,sjk->sik/dot_general | solution.py:76
  159.2 3.7 %fusion.53 = f32[8,320,128]{2,1,0:T(8,128)S(1)} fusion(f32[8,320,128]{2,1,0:T(8,128)S(1)} %fusion.50, f32[1,8,320,320]{3,2,1,0:T(8,128)S(1)} %copy-done), kind=kOutput, calls=%fused_computation.67 | convolution fusion | flops 1258291200 | bytes 5898240 | tf_op jit(solution)/shard_map/sij,sjk->sik/dot_general | solution.py:51
  162.8 13.0 %while.140 = (s32[]{:T(128)}, f32[320,128]{1,0:T(8,128)S(1)}, f32[8,320,128]{2,1,0:T(8,128)S(1)}, f32[8,320,320]{2,1,0:T(8,128)}, s32[]{:T(128)}, /*index=5*/s32[]{:T(128)}) while((s32[]{:T(128)}, f32[320,128]{1,0:T(8,128)S(1)}, f32[8,320,128]{2,1,0:T(8,128)S(1)}, f32[8,320,320]{2,1,0:T(8,128)}, s32[]{:T(128)}, ...), condition=%wide.region_14.15_spmd.clone, body=%wide.region_13.14_spmd.clone.sunk | while | flops 157368320 | bytes 1311823 | solution.py:25
  175.9 3.3 %collective-permute-start.6 = (f32[320,128]{1,0:T(8,128)S(1)}, f32[320,128]{1,0:T(8,128)S(1)}, u32[]{:S(2)}, u32[]{:S(2)}) collective-permute-start(f32[320,128]{1,0:T(8,128)S(1)} %add.139), channel_id=1, source_target_pairs={{0,1},{1,2},{2,3},{4,5},{5,6},{6,7},{8,9},{9,10},{10,11},{12,13},{... | collective-permute-start | bytes 491528 | tf_op jit(solution)/shard_map/ppermute | solution.py:15
  179.2 4.3 %collective-permute-done.6 = f32[320,128]{1,0:T(8,128)S(1)} collective-permute-done((f32[320,128]{1,0:T(8,128)S(1)}, f32[320,128]{1,0:T(8,128)S(1)}, u32[]{:S(2)}, u32[]{:S(2)}) %collective-permute-start.6) | collective-permute-done | bytes 163872 | tf_op jit(solution)/shard_map/ppermute | solution.py:15
  184.1 4.4 %collective-permute-start.7 = (f32[320,128]{1,0:T(8,128)S(1)}, f32[320,128]{1,0:T(8,128)S(1)}, u32[]{:S(2)}, u32[]{:S(2)}) collective-permute-start(f32[320,128]{1,0:T(8,128)S(1)} %convolution_add_fusion.3), channel_id=1, source_target_pairs={{0,1},{1,2},{2,3},{4,5},{5,6},{6,7},{8,9},{9,10},{10,11},{12,13},{... | collective-permute-start | bytes 491528 | tf_op jit(solution)/shard_map/ppermute | solution.py:15
  188.5 3.5 %collective-permute-done.7 = f32[320,128]{1,0:T(8,128)S(1)} collective-permute-done((f32[320,128]{1,0:T(8,128)S(1)}, f32[320,128]{1,0:T(8,128)S(1)}, u32[]{:S(2)}, u32[]{:S(2)}) %collective-permute-start.7) | collective-permute-done | bytes 163872 | tf_op jit(solution)/shard_map/ppermute | solution.py:15
  192.5 4.4 %collective-permute-start.8 = (f32[320,128]{1,0:T(8,128)S(1)}, f32[320,128]{1,0:T(8,128)S(1)}, u32[]{:S(2)}, u32[]{:S(2)}) collective-permute-start(f32[320,128]{1,0:T(8,128)S(1)} %convolution_add_fusion.2), channel_id=1, source_target_pairs={{0,1},{1,2},{2,3},{4,5},{5,6},{6,7},{8,9},{9,10},{10,11},{12,13},{... | collective-permute-start | bytes 491528 | tf_op jit(solution)/shard_map/ppermute | solution.py:15
  196.9 2.8 collective-permute-done.8
  199.8 13.2 %while.136 = (s32[]{:T(128)}, f32[320,128]{1,0:T(8,128)S(1)}, f32[8,320,128]{2,1,0:T(8,128)S(1)}, f32[8,320,128]{2,1,0:T(8,128)}, f32[8,320,320]{2,1,0:T(8,128)}, /*index=5*/s32[]{:T(128)}) while((s32[]{:T(128)}, f32[320,128]{1,0:T(8,128)S(1)}, f32[8,320,128]{2,1,0:T(8,128)S(1)}, f32[8,320,128]{2,1,0:T(8,128)}, f32[8,320,320]{2,1,0:T(8,128)}, ...), condition=%wide.region_16.17_spmd, body=%wide.region_15.16_spmd.sunk | while | flops 157327360 | bytes 1475653 | solution.py:25
  213.1 13.0 %while.141 = (s32[]{:T(128)}, f32[320,128]{1,0:T(8,128)S(1)}, f32[8,320,128]{2,1,0:T(8,128)S(1)}, f32[8,320,320]{2,1,0:T(8,128)}, s32[]{:T(128)}, /*index=5*/s32[]{:T(128)}, s32[]{:T(128)}) while((s32[]{:T(128)}, f32[320,128]{1,0:T(8,128)S(1)}, f32[8,320,128]{2,1,0:T(8,128)S(1)}, f32[8,320,320]{2,1,0:T(8,128)}, s32[]{:T(128)}, ...), condition=%wide.region_18.19_spmd.clone, body=%wide.region_17.18_spmd.clone.sunk | while | flops 157368320 | bytes 1312354 | solution.py:25
  227.6 6.2 %collective-permute-done.9 = f32[320,128]{1,0:T(8,128)S(1)} collective-permute-done((f32[320,128]{1,0:T(8,128)S(1)}, f32[320,128]{1,0:T(8,128)S(1)}, u32[]{:S(2)}, u32[]{:S(2)}) %collective-permute-start.9) | collective-permute-done | bytes 163872 | tf_op jit(solution)/shard_map/ppermute | solution.py:15
  235.6 5.9 %collective-permute-done.10 = f32[320,128]{1,0:T(8,128)S(1)} collective-permute-done((f32[320,128]{1,0:T(8,128)S(1)}, f32[320,128]{1,0:T(8,128)S(1)}, u32[]{:S(2)}, u32[]{:S(2)}) %collective-permute-start.10) | collective-permute-done | bytes 163872 | tf_op jit(solution)/shard_map/ppermute | solution.py:15
  245.4 3.9 %collective-permute-done.11 = f32[320,128]{1,0:T(8,128)S(1)} collective-permute-done((f32[320,128]{1,0:T(8,128)S(1)}, f32[320,128]{1,0:T(8,128)S(1)}, u32[]{:S(2)}, u32[]{:S(2)}) %collective-permute-start.11) | collective-permute-done | bytes 163872 | tf_op jit(solution)/shard_map/ppermute | solution.py:15
  250.5 18.1 %while.137 = (s32[]{:T(128)}, f32[320,128]{1,0:T(8,128)S(1)}, f32[8,320,128]{2,1,0:T(8,128)}, f32[8,320,128]{2,1,0:T(8,128)S(1)}, f32[8,320,320]{2,1,0:T(8,128)}, /*index=5*/s32[]{:T(128)}, s32[]{:T(128)}) while((s32[]{:T(128)}, f32[320,128]{1,0:T(8,128)S(1)}, f32[8,320,128]{2,1,0:T(8,128)}, f32[8,320,128]{2,1,0:T(8,128)S(1)}, ...), condition=%wide.region_20.21_spmd, body=%wide.region_19.20_spmd.sunk | while | flops 157327360 | bytes 1475673 | solution.py:25
  250.5 2.3 bitcast_dynamic-update-slice_fusion.11
  252.8 2.2 bitcast_dynamic-update-slice_fusion.11
  255.1 2.2 bitcast_dynamic-update-slice_fusion.11
  257.3 2.2 bitcast_dynamic-update-slice_fusion.11
  259.6 2.2 bitcast_dynamic-update-slice_fusion.11
  261.8 2.2 bitcast_dynamic-update-slice_fusion.11
  264.1 2.2 bitcast_dynamic-update-slice_fusion.11
  266.4 2.2 bitcast_dynamic-update-slice_fusion.11
  270.8 22.3 %all-reduce = f32[8,320]{1,0:T(8,128)S(1)} all-reduce(f32[8,320]{1,0:T(8,128)S(1)} %multiply_multiply_fusion), channel_id=2, replica_groups=mesh['energy'=8,'dom'=4] {'energy'}, use_global_device_ids=true, to_apply=%region_22.23.clone | all-reduce | flops 2560 | bytes 20480
  (192 shorter events, 130.7 us)
Async XLA Ops:
  6.5 145.9 %all-gather.2.cloned.1.call-start = ((), (), s32[]{:S(2)}) async-start(), calls=%async_computation | async-start | bytes 4423680 | tf_op jit(solution)/shard_map/all_gather | solution.py:71
  25.6 1.1 copy-start.1
  44.7 8.4 %collective-permute-start = (f32[320,128]{1,0:T(8,128)S(1)}, f32[320,128]{1,0:T(8,128)S(1)}, u32[]{:S(2)}, u32[]{:S(2)}) collective-permute-start(f32[320,128]{1,0:T(8,128)S(1)} %get-tuple-element.721), channel_id=1, source_target_pairs={{0,1},{1,2},{2,3},{4,5},{5,6},{6,7},{8,9},{9,10},{10,11},{12,13},{... | collective-permute-start | bytes 491528 | tf_op jit(solution)/shard_map/ppermute | solution.py:15
  53.6 7.2 %collective-permute-start.1 = (f32[320,128]{1,0:T(8,128)S(1)}, f32[320,128]{1,0:T(8,128)S(1)}, u32[]{:S(2)}, u32[]{:S(2)}) collective-permute-start(f32[320,128]{1,0:T(8,128)S(1)} %convolution_add_fusion.7), channel_id=1, source_target_pairs={{0,1},{1,2},{2,3},{4,5},{5,6},{6,7},{8,9},{9,10},{10,11},{12,13},{... | collective-permute-start | bytes 491528 | tf_op jit(solution)/shard_map/ppermute | solution.py:15
  61.4 22.0 %collective-permute-start.2 = (f32[320,128]{1,0:T(8,128)S(1)}, f32[320,128]{1,0:T(8,128)S(1)}, u32[]{:S(2)}, u32[]{:S(2)}) collective-permute-start(f32[320,128]{1,0:T(8,128)S(1)} %convolution_add_fusion.6), channel_id=1, source_target_pairs={{0,1},{1,2},{2,3},{4,5},{5,6},{6,7},{8,9},{9,10},{10,11},{12,13},{... | collective-permute-start | bytes 491528 | tf_op jit(solution)/shard_map/ppermute | solution.py:15
  109.8 17.6 %copy-start.3 = (f32[32]{0:T(128)S(1)}, f32[32]{0:T(128)}, u32[]{:S(2)}) copy-start(f32[32]{0:T(128)} %param.33) | copy-start | bytes 388
  109.8 17.6 %copy-start.4 = (s32[8]{0:T(128)S(1)}, s32[8]{0:T(128)}, u32[]{:S(2)}) copy-start(s32[8]{0:T(128)} %param.32) | copy-start | bytes 100
  110.4 7.2 %collective-permute-start.3 = (f32[320,128]{1,0:T(8,128)S(1)}, f32[320,128]{1,0:T(8,128)S(1)}, u32[]{:S(2)}, u32[]{:S(2)}) collective-permute-start(f32[320,128]{1,0:T(8,128)S(1)} %get-tuple-element.723), channel_id=1, source_target_pairs={{1,0},{2,1},{3,2},{5,4},{6,5},{7,6},{9,8},{10,9},{11,10},{13,12},{... | collective-permute-start | bytes 491528 | tf_op jit(solution)/shard_map/ppermute | solution.py:15
  118.2 7.2 %collective-permute-start.4 = (f32[320,128]{1,0:T(8,128)S(1)}, f32[320,128]{1,0:T(8,128)S(1)}, u32[]{:S(2)}, u32[]{:S(2)}) collective-permute-start(f32[320,128]{1,0:T(8,128)S(1)} %convolution_add_fusion.5), channel_id=1, source_target_pairs={{1,0},{2,1},{3,2},{5,4},{6,5},{7,6},{9,8},{10,9},{11,10},{13,12},{... | collective-permute-start | bytes 491528 | tf_op jit(solution)/shard_map/ppermute | solution.py:15
  125.9 7.2 %collective-permute-start.5 = (f32[320,128]{1,0:T(8,128)S(1)}, f32[320,128]{1,0:T(8,128)S(1)}, u32[]{:S(2)}, u32[]{:S(2)}) collective-permute-start(f32[320,128]{1,0:T(8,128)S(1)} %convolution_add_fusion.4), channel_id=1, source_target_pairs={{1,0},{2,1},{3,2},{5,4},{6,5},{7,6},{9,8},{10,9},{11,10},{13,12},{... | collective-permute-start | bytes 491528 | tf_op jit(solution)/shard_map/ppermute | solution.py:15
  152.5 6.7 %copy-start = (f32[1,8,320,320]{3,2,1,0:T(8,128)S(1)}, f32[1,8,320,320]{3,2,1,0:T(8,128)}, u32[]{:S(2)}) copy-start(f32[1,8,320,320]{3,2,1,0:T(8,128)} %param.28) | copy-start | bytes 9830404
  175.9 21.1 %copy-start.2 = (f32[8,320,128]{2,1,0:T(8,128)}, f32[8,320,128]{2,1,0:T(8,128)S(1)}, u32[]{:S(2)}) copy-start(f32[8,320,128]{2,1,0:T(8,128)S(1)} %get-tuple-element.1198) | copy-start | bytes 3932164
  175.9 7.7 %collective-permute-start.6 = (f32[320,128]{1,0:T(8,128)S(1)}, f32[320,128]{1,0:T(8,128)S(1)}, u32[]{:S(2)}, u32[]{:S(2)}) collective-permute-start(f32[320,128]{1,0:T(8,128)S(1)} %add.139), channel_id=1, source_target_pairs={{0,1},{1,2},{2,3},{4,5},{5,6},{6,7},{8,9},{9,10},{10,11},{12,13},{... | collective-permute-start | bytes 491528 | tf_op jit(solution)/shard_map/ppermute | solution.py:15
  184.1 7.9 %collective-permute-start.7 = (f32[320,128]{1,0:T(8,128)S(1)}, f32[320,128]{1,0:T(8,128)S(1)}, u32[]{:S(2)}, u32[]{:S(2)}) collective-permute-start(f32[320,128]{1,0:T(8,128)S(1)} %convolution_add_fusion.3), channel_id=1, source_target_pairs={{0,1},{1,2},{2,3},{4,5},{5,6},{6,7},{8,9},{9,10},{10,11},{12,13},{... | collective-permute-start | bytes 491528 | tf_op jit(solution)/shard_map/ppermute | solution.py:15
  192.5 7.2 %collective-permute-start.8 = (f32[320,128]{1,0:T(8,128)S(1)}, f32[320,128]{1,0:T(8,128)S(1)}, u32[]{:S(2)}, u32[]{:S(2)}) collective-permute-start(f32[320,128]{1,0:T(8,128)S(1)} %convolution_add_fusion.2), channel_id=1, source_target_pairs={{0,1},{1,2},{2,3},{4,5},{5,6},{6,7},{8,9},{9,10},{10,11},{12,13},{... | collective-permute-start | bytes 491528 | tf_op jit(solution)/shard_map/ppermute | solution.py:15
  226.1 18.0 %copy-start.5 = (u32[32]{0:T(128)S(1)}, u32[32]{0:T(128)}, u32[]{:S(2)}) copy-start(u32[32]{0:T(128)} %constant.230) | copy-start | bytes 388
  226.1 7.7 %collective-permute-start.9 = (f32[320,128]{1,0:T(8,128)S(1)}, f32[320,128]{1,0:T(8,128)S(1)}, u32[]{:S(2)}, u32[]{:S(2)}) collective-permute-start(f32[320,128]{1,0:T(8,128)S(1)} %add.142), channel_id=1, source_target_pairs={{1,0},{2,1},{3,2},{5,4},{6,5},{7,6},{9,8},{10,9},{11,10},{13,12},{... | collective-permute-start | bytes 491528 | tf_op jit(solution)/shard_map/ppermute | solution.py:15
  234.3 7.2 %collective-permute-start.10 = (f32[320,128]{1,0:T(8,128)S(1)}, f32[320,128]{1,0:T(8,128)S(1)}, u32[]{:S(2)}, u32[]{:S(2)}) collective-permute-start(f32[320,128]{1,0:T(8,128)S(1)} %convolution_add_fusion.1), channel_id=1, source_target_pairs={{1,0},{2,1},{3,2},{5,4},{6,5},{7,6},{9,8},{10,9},{11,10},{13,12},{... | collective-permute-start | bytes 491528 | tf_op jit(solution)/shard_map/ppermute | solution.py:15
  242.1 7.2 %collective-permute-start.11 = (f32[320,128]{1,0:T(8,128)S(1)}, f32[320,128]{1,0:T(8,128)S(1)}, u32[]{:S(2)}, u32[]{:S(2)}) collective-permute-start(f32[320,128]{1,0:T(8,128)S(1)} %convolution_add_fusion), channel_id=1, source_target_pairs={{1,0},{2,1},{3,2},{5,4},{6,5},{7,6},{9,8},{10,9},{11,10},{13,12},{... | collective-permute-start | bytes 491528 | tf_op jit(solution)/shard_map/ppermute | solution.py:15
Sparse Core Ops, SparseCore 0:
  58.2 35.8 all-gather.1
where the time goes:
time: 304 us; the launch traced here: 301 us
  matrix products  168 us (55%)
  waiting for transfers between devices  50.1 us (16%)
  starting transfers between devices  34 us (11%)
  blocking collectives  22.3 us (7%)
  between operations  15.1 us (5%)
  local copies, waits for them, and re-layouts  6.32 us (2%)
    dot_general x64, matrix products, sweep_advance(): current = given_value - jnp.dot(matrix_block, current, precision=HIGHEST)  113 us
    ppermute x12, waiting for transfers between devices, from_behind(): return lax.ppermute(x, axis, pairs)  50.1 us
    dot_general x16, matrix products, transfer_advance(): return (-jnp.dot(matrix_block, current, precision=HIGHEST), None)  34 us
    ppermute x12, starting transfers between devices, from_behind(): return lax.ppermute(x, axis, pairs)  34 us
    unnamed x1, blocking collectives  22.3 us
    dot_general x2, matrix products, solve(): jnp.einsum('sij,sjk->sik', pivot_blocks, right_side, precision=HIGHEST)  9.71 us
    dot_general x1, matrix products, per_device(): driven = jnp.einsum('sij,sjk->sik', perturb, first_solve, precision=HIGHEST)  6.65 us
  transfers between devices with their start and end apart: 13, of which 11 were waited for; matrix products, arithmetic and copies ran while one was open for 22% of the time, Pallas kernels for 0%

commit v1 on v0

v1 whole, which is shorter than its diff:
```python
import functools

import jax
import jax.numpy as jnp
from jax import lax
from jax.experimental import pallas as pl
from jax.experimental.pallas import tpu as pltpu
from jax.sharding import PartitionSpec as P

F32 = jnp.float32
BF16 = jnp.bfloat16
HIGH = lax.Precision.HIGH


def halves(x):
    high = x.astype(BF16)
    return high, (x - high.astype(F32)).astype(BF16)


def dot(a, b):
    return jnp.dot(a, b, preferred_element_type=F32)


def product(a, x):
    width = x.shape[1]
    a_high, a_low = halves(a)
    x_high, x_low = halves(x)
    if width <= 128:
        both = jnp.concatenate([x_high, x_low], axis=1)
        out = dot(jnp.concatenate([a_high, a_low], axis=1), jnp.concatenate([both, both], axis=0))
        return out[:, :width] + out[:, width:]
    return dot(
        jnp.concatenate([a_high, a_low, a_high], axis=1),
        jnp.concatenate([x_high, x_high, x_low], axis=0),
    )


def block(rows, columns, index):
    return pl.BlockSpec((1, rows, columns), index)


def whole(shape):
    return pl.BlockSpec(shape, lambda s: (0,) * len(shape))


def params():
    return pltpu.CompilerParams(vmem_limit_bytes=48 << 20)


def cost(dots, columns, orbitals, bytes_accessed):
    return pl.CostEstimate(
        flops=int(dots * 2 * 3 * orbitals * orbitals * columns),
        bytes_accessed=int(bytes_accessed),
        transcendentals=0,
    )


def forward_kernel(pivot, lower, probe, y_out, t_out, last_y, last_t, state):
    probes = probe.shape[2]
    step = pl.program_id(0)
    given = product(pivot[0], probe[0])

    @pl.when(step == 0)
    def _():
        state[:, :probes] = given
        state[:, probes:] = -lower[0]

    @pl.when(step > 0)
    def _():
        moved = product(lower[0], state[...])
        state[:, :probes] = given - moved[:, :probes]
        state[:, probes:] = -moved[:, probes:]

    y_out[0] = state[:, :probes]
    t_out[0] = state[:, probes:]
    last_y[...] = state[:, :probes]
    last_t[...] = state[:, probes:]


def forward(pivots, lower, probes):
    slices, b, k = probes.shape
    at = lambda s: (s, 0, 0)
    return pl.pallas_call(
        forward_kernel,
        grid=(slices,),
        in_specs=[block(b, b, at), block(b, b, at), block(b, k, at)],
        out_specs=[block(b, k, at), block(b, b, at), whole((b, k)), whole((b, b))],
        out_shape=[
            jax.ShapeDtypeStruct((slices, b, k), F32),
            jax.ShapeDtypeStruct((slices, b, b), F32),
            jax.ShapeDtypeStruct((b, k), F32),
            jax.ShapeDtypeStruct((b, b), F32),
        ],
        scratch_shapes=[pltpu.VMEM((b, k + b), F32)],
        compiler_params=params(),
        cost_estimate=cost(slices, 2 * k + b, b, 4 * slices * b * (3 * b + 2 * k)),
        name="forward_local",
    )(pivots, lower, probes)


def backward_kernel(upper, y, t, x_out, w_out, s_out, first_xw, first_s, state):
    k = y.shape[2]
    b = t.shape[1]
    step = pl.program_id(0)

    @pl.when(step == 0)
    def _():
        state[:, :k] = y[0]
        state[:, k : k + b] = t[0]
        state[:, k + b :] = -upper[0]

    @pl.when(step > 0)
    def _():
        moved = product(upper[0], state[...])
        state[:, :k] = y[0] - moved[:, :k]
        state[:, k : k + b] = t[0] - moved[:, k : k + b]
        state[:, k + b :] = -moved[:, k + b :]

    x_out[0] = state[:, :k]
    w_out[0] = state[:, k : k + b]
    s_out[0] = state[:, k + b :]
    first_xw[...] = state[:, : k + b]
    first_s[...] = state[:, k + b :]


def backward(upper, y, t):
    slices, b, k = y.shape
    at = lambda s: (slices - 1 - s, 0, 0)
    return pl.pallas_call(
        backward_kernel,
        grid=(slices,),
        in_specs=[block(b, b, at), block(b, k, at), block(b, b, at)],
        out_specs=[
            block(b, k, at),
            block(b, b, at),
            block(b, b, at),
            whole((b, k + b)),
            whole((b, b)),
        ],
        out_shape=[
            jax.ShapeDtypeStruct((slices, b, k), F32),
            jax.ShapeDtypeStruct((slices, b, b), F32),
            jax.ShapeDtypeStruct((slices, b, b), F32),
            jax.ShapeDtypeStruct((b, k + b), F32),
            jax.ShapeDtypeStruct((b, b), F32),
        ],
        scratch_shapes=[pltpu.VMEM((b, k + 2 * b), F32)],
        compiler_params=params(),
        cost_estimate=cost(slices, k + 2 * b, b, 4 * slices * b * (4 * b + 2 * k)),
        name="backward_local",
    )(upper, y, t)


def drive_kernel(split_rows, me, scale, pivot, w, s, x, inflow, *rest):
    pieces, out, gathered = rest[:-2], rest[-2], rest[-1]
    step = pl.program_id(0)
    if split_rows:
        rows = pieces[0].shape[1]
        for j, piece in enumerate(pieces):
            owner = lax.bitwise_xor(me[0], j)
            gathered[pl.ds(pl.multiple_of(owner * rows, 8), rows), :] = piece[0]
        potential = gathered[...]
    else:
        potential = pieces[0][0]
    base = x[0] + product(w[0], inflow[...])
    right = jnp.concatenate([base, s[0]], axis=1)
    out[0] = product(pivot[0], product(potential * scale[step], right))


def drive(me, scale, pivots, w, s, x, inflow, pieces):
    slices, b, k = x.shape
    at = lambda i: (i, 0, 0)
    scalar = pl.BlockSpec(memory_space=pltpu.SMEM)
    rows = pieces[0].shape[1]
    return pl.pallas_call(
        functools.partial(drive_kernel, len(pieces) > 1),
        grid=(slices,),
        in_specs=[
            scalar,
            scalar,
            block(b, b, at),
            block(b, b, at),
            block(b, b, at),
            block(b, k, at),
            whole((b, k)),
        ]
        + [block(rows, b, at)] * len(pieces),
        out_specs=block(b, k + b, at),
        out_shape=jax.ShapeDtypeStruct((slices, b, k + b), F32),
        scratch_shapes=[pltpu.VMEM((b, b), F32)],
        compiler_params=params(),
        cost_estimate=cost(slices, 3 * k + 2 * b, b, 4 * slices * b * (5 * b + 2 * k)),
        name="drive_blocks",
    )(me, scale, pivots, w, s, x, inflow, *pieces)


def sweep_kernel(matrix, given, out, end, state):
    step = pl.program_id(0)

    @pl.when(step == 0)
    def _():
        state[...] = given[0]

    @pl.when(step > 0)
    def _():
        state[...] = given[0] - product(matrix[0], state[...])

    out[0] = state[...]
    end[...] = state[...]


def sweep(matrices, given, reverse):
    slices, b, n = given.shape
    at = (lambda s: (slices - 1 - s, 0, 0)) if reverse else (lambda s: (s, 0, 0))
    return pl.pallas_call(
        sweep_kernel,
        grid=(slices,),
        in_specs=[block(b, b, at), block(b, n, at)],
        out_specs=[block(b, n, at), whole((b, n))],
        out_shape=[
            jax.ShapeDtypeStruct((slices, b, n), F32),
            jax.ShapeDtypeStruct((b, n), F32),
        ],
        scratch_shapes=[pltpu.VMEM((b, n), F32)],
        compiler_params=params(),
        cost_estimate=cost(slices, n, b, 4 * slices * b * (b + 2 * n)),
        name="sweep_back" if reverse else "sweep_ahead",
    )(matrices, given)


def partial_kernel(v, w, outflow, inflow, out):
    k = out.shape[2]
    wide = v[0]
    out[0] = wide[:, :k] + product(wide[:, k:], outflow[...]) + product(w[0], inflow[...])


def partial_second(v, w, outflow, inflow):
    slices, b, n = v.shape
    k = n - b
    at = lambda s: (s, 0, 0)
    return pl.pallas_call(
        partial_kernel,
        grid=(slices,),
        in_specs=[block(b, n, at), block(b, b, at), whole((b, k)), whole((b, k))],
        out_specs=block(b, k, at),
        out_shape=jax.ShapeDtypeStruct((slices, b, k), F32),
        compiler_params=params(),
        cost_estimate=cost(slices, 2 * k, b, 4 * slices * b * (2 * b + 2 * k)),
        name="second_partial",
    )(v, w, outflow, inflow)


def charge_kernel(partial, s, outflow, probe, out):
    step = pl.program_id(0)
    second = partial[0] + product(s[0], outflow[...])
    out[pl.ds(step, 1), :] = jnp.sum((second * probe[0]).T, axis=0, keepdims=True)


def charge(partial, s, outflow, probes):
    slices, b, k = probes.shape
    at = lambda i: (i, 0, 0)
    return pl.pallas_call(
        charge_kernel,
        grid=(slices,),
        in_specs=[block(b, k, at), block(b, b, at), whole((b, k)), block(b, k, at)],
        out_specs=whole((slices, b)),
        out_shape=jax.ShapeDtypeStruct((slices, b), F32),
        compiler_params=params(),
        cost_estimate=cost(slices, k, b, 4 * slices * b * (b + 2 * k)),
        name="charge_terms",
    )(partial, s, outflow, probes)


def mm(a, b):
    return jnp.dot(a, b, precision=HIGH)


def send(x, *pairs):
    return lax.ppermute(x, "dom", list(pairs))


def gather_potential(potential):
    peers = lax.axis_size("energy")
    rows = potential.shape[1]
    if peers != 8 or rows % 8:
        return (lax.all_gather(potential, "energy", axis=1, tiled=True),)
    swap = lambda x, bits: lax.ppermute(x, "energy", [(i, i ^ bits) for i in range(peers)])
    even = [potential] + [swap(potential, bits) for bits in (2, 4, 6)]
    odd = [swap(x, 1) for x in even]
    return (even[0], odd[0], even[1], odd[1], even[2], odd[2], even[3], odd[3])


def per_device(
    pivots, lower_spikes, upper_spikes, potential, grain_of_slice, grain_shift, probes, weights
):
    pivots, lower, upper = pivots[0], lower_spikes[0], upper_spikes[0]
    k = probes.shape[2]
    energies = lax.axis_size("energy")
    me = lax.axis_index("energy").astype(jnp.int32).reshape(1)
    domain = lax.axis_index("dom")
    grain_count = grain_shift.shape[0]
    grain_match = grain_of_slice[:, None] == jnp.arange(grain_count, dtype=jnp.int32)[None, :]
    grain_scale = jnp.sum(jnp.where(grain_match, grain_shift[None, :], 0.0), axis=1)
    pieces = gather_potential(potential)

    y, t, last_y, last_t = forward(pivots, lower, probes)
    in_1 = send(last_y, (0, 1))
    x, w, s, first_xw, first_s = backward(upper, y, t)
    first_x, first_w = first_xw[:, :k], first_xw[:, k:]
    from_3 = send(first_xw, (3, 2))
    x_3, w_3 = from_3[:, :k], from_3[:, k:]
    in_2 = send(last_y + mm(last_t, in_1), (1, 2))
    out_2 = last_y + mm(last_t, in_2)
    in_3 = send(out_2, (2, 3))
    inflow = in_1 + in_2 + in_3
    base_x = first_x + mm(first_w, inflow)
    outflow_2 = x_3 + mm(w_3, out_2)
    outflow_1 = send(base_x + mm(first_s, outflow_2), (2, 1))
    outflow_0 = send(base_x + mm(first_s, outflow_1), (1, 0))
    outflow = outflow_0 + outflow_1 + outflow_2

    driven = drive(me, grain_scale, pivots, w, s, x, inflow, pieces)
    ahead, ahead_end = sweep(lower, driven, False)
    back, back_end = sweep(upper, ahead, True)

    last_y = ahead_end[:, :k] + mm(ahead_end[:, k:], outflow)
    first_x = back_end[:, :k] + mm(back_end[:, k:], outflow)
    x_3 = send(first_x, (3, 2))
    in_1 = send(last_y, (0, 1))
    in_2 = send(last_y + mm(last_t, in_1), (1, 2))
    out_2 = last_y + mm(last_t, in_2)
    in_3 = send(out_2, (2, 3))
    inflow = in_1 + in_2 + in_3
    base_x = first_x + mm(first_w, inflow)
    outflow_2 = x_3 + mm(w_3, out_2)
    outflow_1 = send(base_x + mm(first_s, outflow_2), (2, 1))
    outflow_0 = send(base_x + mm(first_s, outflow_1), (1, 0))
    last_outflow = outflow_0 + outflow_1 + outflow_2

    partial = partial_second(back, w, outflow, inflow)
    terms = charge(partial, s, last_outflow, probes) * (weights[0] / (k * energies))
    slices, b = terms.shape
    split = terms.reshape(slices, energies, b // energies).transpose(1, 0, 2)
    return jnp.sum(lax.all_to_all(split, "energy", 0, 0, tiled=True), axis=0)


def solution(mesh):
    placed = (
        P("energy", "dom", None, None),
        P("energy", "dom", None, None),
        P("energy", "dom", None, None),
        P("dom", "energy", None),
        P("dom"),
        P(),
        P("dom", None, None),
        P("energy"),
    )
    return jax.shard_map(
        per_device, mesh=mesh, in_specs=placed, out_specs=P("dom", "energy"), check_vma=False
    )
```

time: 304 us -> 147 us (0.48)
  matrix products: 168 us -> 6.25 us
  Pallas kernels: 0 us -> 67.1 us
  waiting for transfers between devices: 50.1 us -> 30.5 us
  blocking collectives: 22.3 us -> 7.34 us
  between operations: 15.1 us -> 1.08 us
  starting transfers between devices: 34 us -> 26.4 us
  local copies, waits for them, and re-layouts: 6.32 us -> 2.6 us
    dot_general x93 -> x14, matrix products: 168 us -> 6.25 us  [mm(): return jnp.dot(a, b, precision=HIGH)]
    pallas_call x0 -> x7, Pallas kernels: none -> 67.1 us  [the longest x2 18.1 us: sweep(): pl.pallas_call(sweep_kernel, grid=(slices,), in_specs=[block(b, b, at), b...]
    unnamed x1 -> x0, blocking collectives: 22.3 us -> none
    ppermute x12 -> x19, waiting for transfers between devices: 50.1 us -> 30.5 us  [the longest x7 17.1 us: gather_potential(): lax.ppermute(x, 'energy', [(i, i ^ bits) for i in range(peers)])]
    ppermute x12 -> x19, starting transfers between devices: 34 us -> 26.4 us  [the longest x12 22.3 us: send(): return lax.ppermute(x, 'dom', list(pairs))]
    all_to_all x0 -> x1, blocking collectives: none -> 7.34 us  [per_device(): return jnp.sum(lax.all_to_all(split, 'energy', 0, 0, tiled=True), axis=0)]
  transfers between devices with their start and end apart: 13 -> 19, of which waited for: 11 -> 4; matrix products, arithmetic and copies ran while one was open for 22% -> 3% of each run, Pallas kernels for 0% -> 35%
where the time goes in v1:
time: 147 us; the launch traced here: 144 us
  Pallas kernels  67.1 us (46%)
  waiting for transfers between devices  30.5 us (21%)
  starting transfers between devices  26.4 us (18%)
  blocking collectives  7.34 us (5%)
  matrix products  6.25 us (4%)
  local copies, waits for them, and re-layouts  2.6 us (2%)
  other arithmetic  2.55 us (2%)
    ppermute x12, starting transfers between devices, send(): return lax.ppermute(x, 'dom', list(pairs))  22.3 us
    pallas_call x2, Pallas kernels, sweep(): pl.pallas_call(sweep_kernel, grid=(slices,), in_specs=[block(b, b, at), b...  18.1 us
    ppermute x7, waiting for transfers between devices, gather_potential(): lax.ppermute(x, 'energy', [(i, i ^ bits) for i in range(peers)])  17.1 us
    pallas_call x1, Pallas kernels, drive(): pl.pallas_call(functools.partial(drive_kernel, len(pieces) > 1), grid=(sl...  13.8 us
    ppermute x12, waiting for transfers between devices, send(): return lax.ppermute(x, 'dom', list(pairs))  13.3 us
    pallas_call x1, Pallas kernels, backward(): pl.pallas_call(backward_kernel, grid=(slices,), in_specs=[block(b, b, at)...  11.5 us
    pallas_call x1, Pallas kernels, forward(): pl.pallas_call(forward_kernel, grid=(slices,), in_specs=[block(b, b, at),...  10.4 us
    all_to_all x1, blocking collectives, per_device(): return jnp.sum(lax.all_to_all(split, 'energy', 0, 0, tiled=True), axis=0)  7.34 us
  transfers between devices with their start and end apart: 19, of which 4 were waited for; matrix products, arithmetic and copies ran while one was open for 3% of the time, Pallas kernels for 35%

profile of v1, /device:TPU:0, one launch (start us, length us, event | category | flops | bytes accessed | tf_op | source)
XLA Modules:
  0.0 143.8 jit_solution(5179704465636341205)
XLA Ops:
  0.0 1.3 copy-done.3
  1.3 10.4 %forward_local.1 = (f32[8,320,128]{2,1,0:T(8,128)S(1)}, f32[8,320,320]{2,1,0:T(8,128)}, f32[320,128]{1,0:T(8,128)S(1)}, f32[320,320]{1,0:T(8,128)S(1)}) custom-call(f32[8,320,320]{2,1,0:T(8,128)} %bitcast.33, f32[8,320,320]{2,1,0:T(8,128)} %bitcast.29, f32[8,320,128]{2,1,0:T(8,128)S(1)} %copy-done.3), custom_call_target="tpu_custom_call" | custom-call | flops 2831155200 | bytes 12451840 | tf_op jit(solution)/shard_map/forward_local/pallas_call | solution.py:83
  11.7 4.9 %collective-permute-start = (f32[320,128]{1,0:T(8,128)S(1)}, f32[320,128]{1,0:T(8,128)S(1)}, u32[]{:S(2)}, u32[]{:S(2)}) collective-permute-start(f32[320,128]{1,0:T(8,128)S(1)} %get-tuple-element.23), channel_id=1, source_target_pairs={{0,1},{4,5},{8,9},{12,13},{16,17},{20,21},{24,25},{28,29}} | collective-permute-start | bytes 491528 | tf_op jit(solution)/shard_map/ppermute | solution.py:279
  16.7 3.4 %collective-permute-done = f32[320,128]{1,0:T(8,128)S(1)} collective-permute-done((f32[320,128]{1,0:T(8,128)S(1)}, f32[320,128]{1,0:T(8,128)S(1)}, u32[]{:S(2)}, u32[]{:S(2)}) %collective-permute-start) | collective-permute-done | bytes 163872 | tf_op jit(solution)/shard_map/ppermute | solution.py:279
  20.1 0.3 convolution_add_fusion.10
  20.4 0.7 collective-permute-start.1
  21.1 0.3 convolution_add_fusion.9
  21.4 0.7 collective-permute-start.2
  22.2 11.5 %backward_local.1 = (f32[8,320,128]{2,1,0:T(8,128)S(1)}, f32[8,320,320]{2,1,0:T(8,128)}, f32[8,320,320]{2,1,0:T(8,128)}, f32[320,448]{1,0:T(8,128)S(1)}, f32[320,320]{1,0:T(8,128)S(1)}) custom-call(f32[8,320,320]{2,1,0:T(8,128)} %bitcast.31, f32[8,320,128]{2,1,0:T(8,128)S(1)} %get-tuple-element.18.y, f32[8,320,320]{2,1,0:T(8,128)} %get-tuple-element.19.t), custom_call_target="tpu_custom_call" | custom-call | flops 3774873600 | bytes 15728640 | tf_op jit(solution)/shard_map/backward_local/pallas_call | solution.py:129
  33.7 0.7 collective-permute-start.10
  34.4 1.6 %collective-permute-start.4 = (f32[8,40,320]{2,1,0:T(8,128)}, f32[8,40,320]{2,1,0:T(8,128)}, u32[]{:S(2)}, u32[]{:S(2)}) collective-permute-start(f32[8,40,320]{2,1,0:T(8,128)} %rest_0_.1), channel_id=1, source_target_pairs={{0,8},{4,12},{8,0},{12,4},{16,24},{20,28},{24,16},{28,20},{1,9},{5... | collective-permute-start | bytes 1228808 | tf_op jit(solution)/shard_map/ppermute | solution.py:287
  35.9 1.5 %collective-permute-start.6 = (f32[8,40,320]{2,1,0:T(8,128)}, f32[8,40,320]{2,1,0:T(8,128)}, u32[]{:S(2)}, u32[]{:S(2)}) collective-permute-start(f32[8,40,320]{2,1,0:T(8,128)} %rest_0_.1), channel_id=1, source_target_pairs={{0,16},{4,20},{8,24},{12,28},{16,0},{20,4},{24,8},{28,12},{1,17},{... | collective-permute-start | bytes 1228808 | tf_op jit(solution)/shard_map/ppermute | solution.py:287
  37.4 0.5 collective-permute-start.8
  37.9 0.3 convolution_add_fusion.8
  38.3 0.3 fusion.5
  38.6 0.5 copy-done.5
  39.1 1.0 convolution_add_fusion.7
  40.1 1.3 collective-permute-start.11
  41.5 7.4 %collective-permute-done.4.rest_2_ = f32[8,40,320]{2,1,0:T(8,128)} collective-permute-done((f32[8,40,320]{2,1,0:T(8,128)}, f32[8,40,320]{2,1,0:T(8,128)}, u32[]{:S(2)}, u32[]{:S(2)}) %collective-permute-start.4) | collective-permute-done | bytes 409632 | tf_op jit(solution)/shard_map/ppermute | solution.py:287
  48.9 9.7 %collective-permute-done.6.rest_4_ = f32[8,40,320]{2,1,0:T(8,128)} collective-permute-done((f32[8,40,320]{2,1,0:T(8,128)}, f32[8,40,320]{2,1,0:T(8,128)}, u32[]{:S(2)}, u32[]{:S(2)}) %collective-permute-start.6) | collective-permute-done | bytes 409632 | tf_op jit(solution)/shard_map/ppermute | solution.py:287
  58.6 0.5 collective-permute-start.9
  59.3 1.2 convolution_add_fusion.6
  60.5 1.3 collective-permute-start.12
  61.9 13.8 %drive_blocks.1.given = f32[8,320,448]{2,1,0:T(8,128)} custom-call(s32[1]{0:T(128)} %bitcast.2.me, f32[8]{0:T(128)S(1)} %select_reduce_fusion.scale, f32[8,320,320]{2,1,0:T(8,128)} %bitcast.34, f32[8,320,320]{2,1,0:T(8,128)} %get-tuple-element.20.w, f32[8,320,320]{2,1,0:T(8,128)} %get-tuple-element.21.s, f32[8,320,128]{2,1,0:T(8,128)S(1)} %get-tuple-element.22.x, ...), custom_call_target="tpu_custom_call" | custom-call | flops 5033164800 | bytes 19005440 | tf_op jit(solution)/shard_map/drive_blocks/pallas_call | solution.py:175
  75.7 9.4 %sweep_ahead.1 = (f32[8,320,448]{2,1,0:T(8,128)}, f32[320,448]{1,0:T(8,128)S(1)}) custom-call(f32[8,320,320]{2,1,0:T(8,128)S(1)} %bitcast.30, f32[8,320,448]{2,1,0:T(8,128)} %drive_blocks.1.given), custom_call_target="tpu_custom_call" | custom-call | flops 2202009600 | bytes 12451840 | tf_op jit(solution)/shard_map/sweep_ahead/pallas_call | solution.py:215
  85.1 1.0 add_add_fusion.2.outflow
  86.1 0.3 slice_add_fusion.1
  86.5 8.7 %collective-permute-start.13 = (f32[320,128]{1,0:T(8,128)S(1)}, f32[320,128]{1,0:T(8,128)S(1)}, u32[]{:S(2)}, u32[]{:S(2)}) collective-permute-start(f32[320,128]{1,0:T(8,128)S(1)} %slice_add_fusion.1), channel_id=1, source_target_pairs={{0,1},{4,5},{8,9},{12,13},{16,17},{20,21},{24,25},{28,29}} | collective-permute-start | bytes 491528 | tf_op jit(solution)/shard_map/ppermute | solution.py:279
  95.1 8.7 %sweep_back.1 = (f32[8,320,448]{2,1,0:T(8,128)}, f32[320,448]{1,0:T(8,128)S(1)}) custom-call(f32[8,320,320]{2,1,0:T(8,128)S(1)} %bitcast.32, f32[8,320,448]{2,1,0:T(8,128)} %get-tuple-element.25.given), custom_call_target="tpu_custom_call" | custom-call | flops 2202009600 | bytes 12451840 | tf_op jit(solution)/shard_map/sweep_back/pallas_call | solution.py:215
  103.8 0.3 convolution_add_fusion.5
  104.2 0.8 collective-permute-start.14
  105.0 0.3 convolution_add_fusion.3
  105.3 0.7 collective-permute-start.16
  106.0 0.3 convolution_add_fusion.4
  106.4 0.7 collective-permute-start.15
  107.0 0.3 fusion.3
  107.5 0.3 convolution_add_fusion.2
  107.8 0.3 convolution_add_fusion.1
  108.1 0.7 collective-permute-start.17
  108.8 0.3 convolution_add_fusion
  109.2 1.3 collective-permute-start.18
  111.1 6.9 %second_partial.1.partial = f32[8,320,128]{2,1,0:T(8,128)S(1)} custom-call(f32[8,320,448]{2,1,0:T(8,128)} %get-tuple-element.26.v, f32[8,320,320]{2,1,0:T(8,128)S(1)} %copy-done, f32[320,128]{1,0:T(8,128)S(1)} %add_add_fusion.2.outflow, f32[320,128]{1,0:T(8,128)S(1)} %add_add_fusion.1.inflow), custom_call_target="tpu_custom_call" | custom-call | flops 1258291200 | bytes 9175040 | tf_op jit(solution)/shard_map/second_partial/pallas_call | solution.py:241
  118.1 9.9 %collective-permute-done.18 = f32[320,128]{1,0:T(8,128)S(1)} collective-permute-done((f32[320,128]{1,0:T(8,128)S(1)}, f32[320,128]{1,0:T(8,128)S(1)}, u32[]{:S(2)}, u32[]{:S(2)}) %collective-permute-start.18) | collective-permute-done | bytes 163872 | tf_op jit(solution)/shard_map/ppermute | solution.py:279
  128.0 6.4 %charge_terms.1 = f32[8,320]{1,0:T(8,128)S(1)} custom-call(f32[8,320,128]{2,1,0:T(8,128)S(1)} %second_partial.1.partial, f32[8,320,320]{2,1,0:T(8,128)} %get-tuple-element.21.s, f32[320,128]{1,0:T(8,128)S(1)} %add_add_fusion.outflow, f32[8,320,128]{2,1,0:T(8,128)S(1)} %copy-done.4), custom_call_target="tpu_custom_call" | custom-call | flops 629145600 | bytes 5898240 | tf_op jit(solution)/shard_map/charge_terms/pallas_call | solution.py:262
  134.6 7.3 %all_to_all.5 = f32[8,1,320]{2,1,0:T(1,128)S(1)} all-to-all(f32[8,1,320]{2,1,0:T(1,128)S(1)} %reshape.12), channel_id=1, replica_groups=mesh['energy'=8,'dom'=4] {'energy'}, dimensions={0} | all-to-all | bytes 20480 | tf_op jit(solution)/shard_map/all_to_all | solution.py:344
  141.9 0.5 broadcast.2
  142.4 0.7 reduce
  143.2 0.6 reduce_sum.19
  (44 shorter events, 0.6 us)
Async XLA Ops:
  0.0 1.3 copy-start.3
  11.7 8.4 %collective-permute-start = (f32[320,128]{1,0:T(8,128)S(1)}, f32[320,128]{1,0:T(8,128)S(1)}, u32[]{:S(2)}, u32[]{:S(2)}) collective-permute-start(f32[320,128]{1,0:T(8,128)S(1)} %get-tuple-element.23), channel_id=1, source_target_pairs={{0,1},{4,5},{8,9},{12,13},{16,17},{20,21},{24,25},{28,29}} | collective-permute-start | bytes 491528 | tf_op jit(solution)/shard_map/ppermute | solution.py:279
  20.4 0.7 collective-permute-start.1
  21.4 16.5 %collective-permute-start.2 = (f32[320,128]{1,0:T(8,128)S(1)}, f32[320,128]{1,0:T(8,128)S(1)}, u32[]{:S(2)}, u32[]{:S(2)}) collective-permute-start(f32[320,128]{1,0:T(8,128)S(1)} %convolution_add_fusion.9), channel_id=1, source_target_pairs={{2,3},{6,7},{10,11},{14,15},{18,19},{22,23},{26,27},{30,31}} | collective-permute-start | bytes 491528 | tf_op jit(solution)/shard_map/ppermute | solution.py:279
  22.1 37.0 %copy-start.7 = (f32[32]{0:T(128)S(1)}, f32[32]{0:T(128)}, u32[]{:S(2)}) copy-start(f32[32]{0:T(128)} %param.13) | copy-start | bytes 388
  22.1 36.9 %copy-start.8 = (s32[8]{0:T(128)S(1)}, s32[8]{0:T(128)}, u32[]{:S(2)}) copy-start(s32[8]{0:T(128)} %param.12) | copy-start | bytes 100
  33.7 4.6 %collective-permute-start.10 = (f32[320,448]{1,0:T(8,128)S(1)}, f32[320,448]{1,0:T(8,128)S(1)}, u32[]{:S(2)}, u32[]{:S(2)}) collective-permute-start(f32[320,448]{1,0:T(8,128)S(1)} %get-tuple-element.27), channel_id=1, source_target_pairs={{3,2},{7,6},{11,10},{15,14},{19,18},{23,22},{27,26},{31,30}} | collective-permute-start | bytes 1720328 | tf_op jit(solution)/shard_map/ppermute | solution.py:279
  34.4 14.5 %collective-permute-start.4 = (f32[8,40,320]{2,1,0:T(8,128)}, f32[8,40,320]{2,1,0:T(8,128)}, u32[]{:S(2)}, u32[]{:S(2)}) collective-permute-start(f32[8,40,320]{2,1,0:T(8,128)} %rest_0_.1), channel_id=1, source_target_pairs={{0,8},{4,12},{8,0},{12,4},{16,24},{20,28},{24,16},{28,20},{1,9},{5... | collective-permute-start | bytes 1228808 | tf_op jit(solution)/shard_map/ppermute | solution.py:287
  35.9 22.7 %collective-permute-start.6 = (f32[8,40,320]{2,1,0:T(8,128)}, f32[8,40,320]{2,1,0:T(8,128)}, u32[]{:S(2)}, u32[]{:S(2)}) collective-permute-start(f32[8,40,320]{2,1,0:T(8,128)} %rest_0_.1), channel_id=1, source_target_pairs={{0,16},{4,20},{8,24},{12,28},{16,0},{20,4},{24,8},{28,12},{1,17},{... | collective-permute-start | bytes 1228808 | tf_op jit(solution)/shard_map/ppermute | solution.py:287
  37.4 21.1 %collective-permute-start.8 = (f32[8,40,320]{2,1,0:T(8,128)}, f32[8,40,320]{2,1,0:T(8,128)}, u32[]{:S(2)}, u32[]{:S(2)}) collective-permute-start(f32[8,40,320]{2,1,0:T(8,128)} %rest_0_.1), channel_id=1, source_target_pairs={{0,24},{4,28},{8,16},{12,20},{16,8},{20,12},{24,0},{28,4},{1,25},{... | collective-permute-start | bytes 1228808 | tf_op jit(solution)/shard_map/ppermute | solution.py:287
  38.3 0.8 copy-start.5
  40.1 19.1 %collective-permute-start.11 = (f32[320,128]{1,0:T(8,128)}, f32[320,128]{1,0:T(8,128)}, u32[]{:S(2)}, u32[]{:S(2)}) collective-permute-start(f32[320,128]{1,0:T(8,128)} %convolution_add_fusion.7), channel_id=1, source_target_pairs={{2,1},{6,5},{10,9},{14,13},{18,17},{22,21},{26,25},{30,29}} | collective-permute-start | bytes 491528 | tf_op jit(solution)/shard_map/ppermute | solution.py:279
  41.5 20.4 %collective-permute-start.3 = (f32[8,40,320]{2,1,0:T(8,128)}, f32[8,40,320]{2,1,0:T(8,128)}, u32[]{:S(2)}, u32[]{:S(2)}) collective-permute-start(f32[8,40,320]{2,1,0:T(8,128)} %rest_0_.1), channel_id=1, source_target_pairs={{0,4},{4,0},{8,12},{12,8},{16,20},{20,16},{24,28},{28,24},{1,5},{5... | collective-permute-start | bytes 1228808 | tf_op jit(solution)/shard_map/ppermute | solution.py:287
  48.9 12.9 %collective-permute-start.5 = (f32[8,40,320]{2,1,0:T(8,128)}, f32[8,40,320]{2,1,0:T(8,128)}, u32[]{:S(2)}, u32[]{:S(2)}) collective-permute-start(f32[8,40,320]{2,1,0:T(8,128)} %collective-permute-done.4.rest_2_), channel_id=1, source_target_pairs={{0,4},{4,0},{8,12},{12,8},{16,20},{20,16},{24,28},{28,24},{1,5},{5... | collective-permute-start | bytes 1228808 | tf_op jit(solution)/shard_map/ppermute | solution.py:287
  58.6 3.3 %collective-permute-start.7 = (f32[8,40,320]{2,1,0:T(8,128)}, f32[8,40,320]{2,1,0:T(8,128)}, u32[]{:S(2)}, u32[]{:S(2)}) collective-permute-start(f32[8,40,320]{2,1,0:T(8,128)} %collective-permute-done.6.rest_4_), channel_id=1, source_target_pairs={{0,4},{4,0},{8,12},{12,8},{16,20},{20,16},{24,28},{28,24},{1,5},{5... | collective-permute-start | bytes 1228808 | tf_op jit(solution)/shard_map/ppermute | solution.py:287
  58.6 3.3 %collective-permute-start.9 = (f32[8,40,320]{2,1,0:T(8,128)}, f32[8,40,320]{2,1,0:T(8,128)}, u32[]{:S(2)}, u32[]{:S(2)}) collective-permute-start(f32[8,40,320]{2,1,0:T(8,128)} %collective-permute-done.8.rest_6_), channel_id=1, source_target_pairs={{0,4},{4,0},{8,12},{12,8},{16,20},{20,16},{24,28},{28,24},{1,5},{5... | collective-permute-start | bytes 1228808 | tf_op jit(solution)/shard_map/ppermute | solution.py:287
  60.5 24.6 %collective-permute-start.12 = (f32[320,128]{1,0:T(8,128)S(1)}, f32[320,128]{1,0:T(8,128)S(1)}, u32[]{:S(2)}, u32[]{:S(2)}) collective-permute-start(f32[320,128]{1,0:T(8,128)S(1)} %convolution_add_fusion.6), channel_id=1, source_target_pairs={{1,0},{5,4},{9,8},{13,12},{17,16},{21,20},{25,24},{29,28}} | collective-permute-start | bytes 491528 | tf_op jit(solution)/shard_map/ppermute | solution.py:279
  61.9 13.8 %copy-start.1 = (f32[1,8,320,320]{3,2,1,0:T(8,128)S(1)}, f32[1,8,320,320]{3,2,1,0:T(8,128)}, u32[]{:S(2)}) copy-start(f32[1,8,320,320]{3,2,1,0:T(8,128)} %param.9) | copy-start | bytes 9830404
  75.7 9.4 %copy-start.6 = (f32[320,448]{1,0:T(8,128)S(1)}, f32[320,448]{1,0:T(8,128)}, u32[]{:S(2)}) copy-start(f32[320,448]{1,0:T(8,128)} %copy-done.5) | copy-start | bytes 1720324
  75.7 19.4 %copy-start.2 = (f32[1,8,320,320]{3,2,1,0:T(8,128)S(1)}, f32[1,8,320,320]{3,2,1,0:T(8,128)}, u32[]{:S(2)}) copy-start(f32[1,8,320,320]{3,2,1,0:T(8,128)} %param.10) | copy-start | bytes 9830404
  86.5 17.4 %collective-permute-start.13 = (f32[320,128]{1,0:T(8,128)S(1)}, f32[320,128]{1,0:T(8,128)S(1)}, u32[]{:S(2)}, u32[]{:S(2)}) collective-permute-start(f32[320,128]{1,0:T(8,128)S(1)} %slice_add_fusion.1), channel_id=1, source_target_pairs={{0,1},{4,5},{8,9},{12,13},{16,17},{20,21},{24,25},{28,29}} | collective-permute-start | bytes 491528 | tf_op jit(solution)/shard_map/ppermute | solution.py:279
  103.8 7.3 %copy-start = (f32[8,320,320]{2,1,0:T(8,128)S(1)}, f32[8,320,320]{2,1,0:T(8,128)}, u32[]{:S(2)}) copy-start(f32[8,320,320]{2,1,0:T(8,128)} %get-tuple-element.20.w) | copy-start | bytes 9830404
  104.2 1.8 %collective-permute-start.14 = (f32[320,128]{1,0:T(8,128)S(1)}, f32[320,128]{1,0:T(8,128)S(1)}, u32[]{:S(2)}, u32[]{:S(2)}) collective-permute-start(f32[320,128]{1,0:T(8,128)S(1)} %convolution_add_fusion.5), channel_id=1, source_target_pairs={{1,2},{5,6},{9,10},{13,14},{17,18},{21,22},{25,26},{29,30}} | collective-permute-start | bytes 491528 | tf_op jit(solution)/shard_map/ppermute | solution.py:279
  105.3 2.1 %collective-permute-start.16 = (f32[320,128]{1,0:T(8,128)S(1)}, f32[320,128]{1,0:T(8,128)S(1)}, u32[]{:S(2)}, u32[]{:S(2)}) collective-permute-start(f32[320,128]{1,0:T(8,128)S(1)} %convolution_add_fusion.3), channel_id=1, source_target_pairs={{3,2},{7,6},{11,10},{15,14},{19,18},{23,22},{27,26},{31,30}} | collective-permute-start | bytes 491528 | tf_op jit(solution)/shard_map/ppermute | solution.py:279
  106.4 1.1 collective-permute-start.15
  108.1 0.7 collective-permute-start.17
  109.2 18.8 %collective-permute-start.18 = (f32[320,128]{1,0:T(8,128)S(1)}, f32[320,128]{1,0:T(8,128)S(1)}, u32[]{:S(2)}, u32[]{:S(2)}) collective-permute-start(f32[320,128]{1,0:T(8,128)S(1)} %convolution_add_fusion), channel_id=1, source_target_pairs={{1,0},{5,4},{9,8},{13,12},{17,16},{21,20},{25,24},{29,28}} | collective-permute-start | bytes 491528 | tf_op jit(solution)/shard_map/ppermute | solution.py:279
  111.1 16.8 %copy-start.4 = (f32[8,320,128]{2,1,0:T(8,128)S(1)}, f32[8,320,128]{2,1,0:T(8,128)}, u32[]{:S(2)}) copy-start(f32[8,320,128]{2,1,0:T(8,128)} %probe.3) | copy-start | bytes 3932164

commit v2 on v0

v2 whole, which is shorter than its diff:
```python
import functools

import jax
import jax.numpy as jnp
from jax import lax
from jax.experimental import pallas as pl
from jax.experimental.pallas import tpu as pltpu
from jax.sharding import PartitionSpec as P

F32 = jnp.float32
BF16 = jnp.bfloat16
HIGH = lax.Precision.HIGH
MIB = 1 << 20


def halves(x):
    high = x.astype(BF16)
    return high, (x - high.astype(F32)).astype(BF16)


def dot(a, b):
    return jnp.dot(a, b, preferred_element_type=F32)


def left_two(a):
    return jnp.concatenate(halves(a), axis=1)


def left_three(a):
    high, low = halves(a)
    return jnp.concatenate([high, low, high], axis=1)


def apply_two(a, x):
    width = x.shape[1]
    both = jnp.concatenate(halves(x), axis=1)
    out = dot(a, jnp.concatenate([both, both], axis=0))
    return out[:, :width] + out[:, width:]


def apply_three(a, high, low):
    return dot(a, jnp.concatenate([high, high, low], axis=0))


def shapes(*entries):
    return [jax.ShapeDtypeStruct(shape, kind) for shape, kind in entries]


def params(mib):
    return pltpu.CompilerParams(vmem_limit_bytes=mib * MIB)


HBM = pl.BlockSpec(memory_space=pltpu.HBM)
VMEM = pl.BlockSpec(memory_space=pltpu.VMEM)
SMEM = pl.BlockSpec(memory_space=pltpu.SMEM)


def pinned(*entries):
    return [pltpu.VMEM(shape, kind) for shape, kind in entries]


def in_vmem(*arrays):
    return [pltpu.with_memory_space_constraint(x, pltpu.VMEM) for x in arrays]


def in_hbm(*arrays):
    return [pltpu.with_memory_space_constraint(x, pltpu.HBM) for x in arrays]


def local_kernel(
    pivot, lower, upper, probe,
    x_out, high_out, low_out, last_y, last_t, first_xw, first_x, first_w, first_s,
    d, l, u, z, left_a, left_b, given_a, given_b, h, x, high, low, sem, sem_out,
):
    n, b, k = z.shape
    kb = k + b
    wide = h.shape[2]
    lefts, givens = (left_a, left_b), (given_a, given_b)

    def load(which, i):
        src, dst = ((probe, z), (pivot, d), (lower, l), (upper, u))[which]
        return pltpu.make_async_copy(src.at[i], dst.at[i], sem.at[which, i])

    def store(which, i):
        src, dst = ((x, x_out), (high, high_out), (low, low_out))[which]
        return pltpu.make_async_copy(src.at[i], dst.at[i], sem_out.at[which, i])

    def begin(i, c):
        load(0, i).start()
        load(1, i).start()
        load(2, i).start()
        return c

    def begin_upper(i, c):
        load(3, n - 1 - i).start()
        return c

    lax.fori_loop(0, n, begin, 0)
    lax.fori_loop(0, n, begin_upper, 0)

    def arrive(i):
        load(0, i).wait()
        load(1, i).wait()
        load(2, i).wait()

    def prepare(i, slot):
        givens[slot][...] = apply_two(left_two(d[i]), z[i])
        lefts[slot][...] = left_three(l[i])

    def ahead(i, slot):
        moved = apply_three(lefts[slot][...], *halves(h[i - 1]))
        h[i, :, :k] = givens[slot][...] - moved[:, :k]
        h[i, :, k:] = -moved[:, k:]

    arrive(0)
    prepare(0, 0)
    h[0] = jnp.concatenate([given_a[...], -l[0], jnp.zeros((b, wide - kb), F32)], axis=1)
    arrive(1)
    prepare(1, 1)

    def ahead_pair(j, c):
        i = 2 * j + 1
        arrive(i + 1)
        ahead(i, 1)
        prepare(i + 1, 0)
        arrive(i + 2)
        ahead(i + 1, 0)
        prepare(i + 2, 1)
        return c

    lax.fori_loop(0, n // 2 - 1, ahead_pair, 0)

    def prepare_back(i, slot):
        lefts[slot][...] = left_three(u[i])

    def keep(i, value):
        value_high, value_low = halves(value)
        x[i] = value[:, :k]
        high[i] = value_high
        low[i] = value_low
        for which in range(3):
            store(which, i).start()

    def step_back(i, slot):
        moved = apply_three(lefts[slot][...], high[i + 1], low[i + 1])
        value = jnp.concatenate([h[i] - moved[:, :wide], -moved[:, wide:]], axis=1)
        keep(i, value)
        return value

    load(3, n - 1).wait()
    load(3, n - 2).wait()
    ahead(n - 1, 1)
    prepare_back(n - 1, 0)
    last_y[...] = h[n - 1, :, :k]
    last_t[...] = h[n - 1, :, k:kb]
    keep(n - 1, jnp.concatenate([h[n - 1, :, :kb], -u[n - 1]], axis=1))
    prepare_back(n - 2, 0)

    def back_pair(j, c):
        i = n - 2 - 2 * j
        load(3, i - 1).wait()
        step_back(i, 0)
        prepare_back(i - 1, 1)
        load(3, i - 2).wait()
        step_back(i - 1, 1)
        prepare_back(i - 2, 0)
        return c

    lax.fori_loop(0, n // 2 - 1, back_pair, 0)
    value = step_back(0, 0)
    first_xw[...] = value[:, :kb]
    first_x[...] = value[:, :k]
    first_w[...] = value[:, k:kb]
    first_s[...] = value[:, kb:]

    def drain(i, c):
        for which in range(3):
            store(which, i).wait()
        return c

    lax.fori_loop(0, n, drain, 0)


def local_maps(pivots, lower, upper, probes):
    n, b, k = probes.shape
    wide = -(-(k + b) // 128) * 128
    full = k + 2 * b
    v = pltpu.VMEM
    return pl.pallas_call(
        local_kernel,
        in_specs=[HBM] * 4,
        out_specs=[HBM] * 3 + [VMEM] * 6,
        out_shape=[
            pltpu.HBM((n, b, k), F32),
            pltpu.HBM((n, b, full), BF16),
            pltpu.HBM((n, b, full), BF16),
        ]
        + pinned(
            ((b, k), F32),
            ((b, b), F32),
            ((b, k + b), F32),
            ((b, k), F32),
            ((b, b), F32),
            ((b, b), F32),
        ),
        scratch_shapes=[
            v((n, b, b), F32),
            v((n, b, b), F32),
            v((n, b, b), F32),
            v((n, b, k), F32),
            v((b, 3 * b), BF16),
            v((b, 3 * b), BF16),
            v((b, k), F32),
            v((b, k), F32),
            v((n, b, wide), F32),
            v((n, b, k), F32),
            v((n, b, full), BF16),
            v((n, b, full), BF16),
            pltpu.SemaphoreType.DMA((4, n)),
            pltpu.SemaphoreType.DMA((3, n)),
        ],
        compiler_params=params(52),
        name="local_maps",
    )(*in_hbm(pivots, lower, upper, probes))


def drive_kernel(start, count, me, scale, pivot, lower, upper, *rest):
    pieces, rest = rest[:count], rest[count:]
    out, lower_out, upper_out, gathered = rest[-4:]
    step = pl.program_id(0) + start
    if count > 1:
        rows = pieces[0].shape[1]
        for j, piece in enumerate(pieces):
            owner = lax.bitwise_xor(me[0], j)
            gathered[pl.ds(pl.multiple_of(owner * rows, 8), rows), :] = piece[0]
        potential = gathered[...]
    else:
        potential = pieces[0][0]
    out[0] = left_two(apply_three(left_three(pivot[0]), *halves(potential * scale[step])))
    lower_out[0] = left_two(lower[0])
    upper_out[0] = left_two(upper[0])


def drive(start, stop, me, scale, pivots, lower, upper, pieces, done=()):
    n, b, _ = pivots.shape
    rows = pieces[0].shape[1]
    at = lambda i: (i + start, 0, 0)
    inputs = (me, scale, *in_hbm(pivots, lower, upper), *pieces)
    return pl.pallas_call(
        functools.partial(drive_kernel, start, len(pieces)),
        grid=(stop - start,),
        in_specs=[SMEM, SMEM]
        + [pl.BlockSpec((1, b, b), at)] * 3
        + [pl.BlockSpec((1, rows, b), at)] * len(pieces)
        + [pl.BlockSpec(memory_space=pl.ANY)] * len(done),
        out_specs=[pl.BlockSpec((1, b, 2 * b), at)] * 3,
        out_shape=pinned(*[((n, b, 2 * b), BF16)] * 3),
        scratch_shapes=[pltpu.VMEM((b, b), F32)],
        input_output_aliases={len(inputs) + i: i for i in range(len(done))},
        compiler_params=params(12),
        name="drive_maps",
    )(*inputs, *done)


def apply_maps(high, low, i, flows):
    k = flows.shape[1] // 2
    skip = high.shape[2] - flows.shape[0]
    maps = jnp.concatenate([high[i, :, skip:], low[i, :, skip:]], axis=1)
    out = dot(maps, jnp.concatenate([flows, flows], axis=0))
    return out[:, :k] + out[:, k:]


def second_kernel(
    x, high, low, driver, lower, upper, probes, inflow, outflow, out, last, first, y
):
    n, b, k = x.shape
    flows = jnp.concatenate(halves(jnp.concatenate([inflow[...], outflow[...]], axis=0)), axis=1)

    def given(i, c):
        out[i] = apply_two(driver[i], x[i] + apply_maps(high, low, i, flows))
        return c

    lax.fori_loop(0, n, given, 0)
    y[0] = out[0]

    def ahead(i, c):
        y[i] = out[i] - apply_two(lower[i], y[i - 1])
        return c

    lax.fori_loop(1, n, ahead, 0)
    last[...] = y[n - 1]
    out[n - 1] = y[n - 1]

    def back(r, c):
        i = n - 1 - r
        out[i] = y[i] - apply_two(upper[i], out[i + 1])
        return c

    lax.fori_loop(1, n, back, 0)
    first[...] = out[0]


def second(x, high, low, driver, lower, upper, probes, inflow, outflow):
    n, b, k = x.shape
    return pl.pallas_call(
        second_kernel,
        in_specs=[VMEM] * 9,
        out_specs=[VMEM] * 3,
        out_shape=pinned(((n, b, k), F32), ((b, k), F32), ((b, k), F32)),
        scratch_shapes=[pltpu.VMEM((n, b, k), F32)],
        compiler_params=params(10),
        name="second_local",
    )(*in_vmem(x, high, low, driver, lower, upper, probes), inflow, outflow)


def charge_kernel(places, weight, x, high, low, probe, in_1, in_2, out_1, out_2, ended, *outs):
    n, b, k = x.shape
    at, energy = places[0], places[1]
    none = jnp.zeros_like(ended)
    inflow = jnp.where(at == 1, in_1[...], jnp.where(at == 2, in_2[...], none))
    inflow = jnp.where(at == 3, ended[...], inflow)
    outflow = jnp.where(at == 1, out_1[...], jnp.where(at == 2, out_2[...], none))
    outflow = jnp.where(at == 0, ended[...], outflow)
    flows = jnp.concatenate(halves(jnp.concatenate([inflow, outflow], axis=0)), axis=1)
    terms = outs[-1]
    for i in range(n):
        value = x[i] + apply_maps(high, low, i, flows)
        terms[i : i + 1, :] = jnp.sum((value * probe[i]).T, axis=0, keepdims=True) * weight[0]
    if len(outs) > 1:
        blocks = outs[0]
        owners, _, rows = blocks.shape
        for owner in range(owners):
            j = lax.bitwise_xor(energy, owner)
            blocks[lax.div(j, 2) + lax.rem(j, 2) * (owners // 2)] = terms[:, owner * rows : (owner + 1) * rows]


def charge(places, weight, energies, x, high, low, probes, *flows):
    n, b, k = probes.shape
    by_swaps = energies == 8
    return pl.pallas_call(
        charge_kernel,
        in_specs=[SMEM] * 2 + [VMEM] * (4 + len(flows)),
        out_specs=VMEM,
        out_shape=pltpu.VMEM((energies, n, b // energies) if by_swaps else (n, b), F32),
        scratch_shapes=[pltpu.VMEM((n, b), F32)] if by_swaps else [],
        compiler_params=params(10),
        name="charge_terms",
    )(places, weight, *in_vmem(x, high, low, probes), *flows)


def mm(a, b):
    return jnp.dot(a, b, precision=HIGH)


def send(x, *pairs):
    return lax.ppermute(x, "dom", list(pairs))


def near(x, ways):
    peers = lax.axis_size("energy")
    return [lax.ppermute(x, "energy", [(i, i ^ way) for i in range(peers)]) for way in ways]


def together(*values):
    return lax.optimization_barrier(values)


def per_device(
    pivots, lower_spikes, upper_spikes, potential, grain_of_slice, grain_shift, probes, weights
):
    pivots, lower, upper = pivots[0], lower_spikes[0], upper_spikes[0]
    k = probes.shape[2]
    energies = lax.axis_size("energy")
    me = lax.axis_index("energy").astype(jnp.int32).reshape(1)
    domain = lax.axis_index("dom")
    grain_count = grain_shift.shape[0]
    grain_match = grain_of_slice[:, None] == jnp.arange(grain_count, dtype=jnp.int32)[None, :]
    grain_scale = jnp.sum(jnp.where(grain_match, grain_shift[None, :], 0.0), axis=1)
    by_swaps = energies == 8 and potential.shape[1] % 8 == 0

    places = jnp.stack([domain, lax.axis_index("energy")]).astype(jnp.int32)
    n, b = pivots.shape[:2]

    even = near(potential, (2, 4, 6)) if by_swaps else []
    x, high, low, last_y, last_t, first_xw, first_x, first_w, first_s = local_maps(
        pivots, lower, upper, probes
    )

    if by_swaps:
        last_y, first_xw, even[0], even[1] = together(last_y, first_xw, even[0], even[1])
    in_1 = send(last_y, (0, 1))
    from_3 = send(first_xw, (3, 2))
    if by_swaps:
        in_1, even[2] = together(in_1, even[2])
    out_1 = last_y + mm(last_t, in_1)
    in_2 = send(out_1, (1, 2))
    if by_swaps:
        even = [potential] + even
        odd = [near(block, (1,))[0] for block in even]
        pieces = [block for pair in zip(even, odd) for block in pair]
    else:
        pieces = [lax.all_gather(potential, "energy", axis=1, tiled=True)]
    out_2 = last_y + mm(last_t, in_2)
    in_3 = send(out_2, (2, 3))
    scale, _ = together(grain_scale, out_2)
    driven = drive(0, n // 2, me, scale, pivots, lower, upper, pieces)
    from_3, *driven = together(from_3, *driven)
    x_3, w_3 = from_3[:, :k], from_3[:, k:]
    inflow = in_1 + in_2 + in_3
    outflow_2 = x_3 + mm(w_3, out_2)
    turn = first_x + mm(first_w, in_1 + in_2) + mm(first_s, outflow_2)
    outflow_1 = send(turn, (2, 1))
    scale, _ = together(scale, turn)
    driven = drive(n // 2, n, me, scale, pivots, lower, upper, pieces, driven)
    outflow_1, *driven = together(outflow_1, *driven)
    outflow_0 = send(first_x + mm(first_w, in_1) + mm(first_s, outflow_1), (1, 0))
    outflow_0, w_3 = together(outflow_0, w_3)
    around = send(first_w + mm(first_s, mm(w_3, last_t)), (2, 1))
    outflow = outflow_0 + outflow_1 + outflow_2

    x, last_y, first_x = second(x, high, low, *driven, probes, inflow, outflow)

    last_y, first_x, around = together(last_y, first_x, around)
    x_3 = send(first_x, (3, 2))
    in_1 = send(last_y, (0, 1))
    joined = jnp.where(
        domain == 1,
        last_y + mm(last_t, in_1),
        first_x + mm(first_s, x_3 + mm(w_3, last_y)),
    )
    swapped = send(joined, (1, 2), (2, 1))
    own = swapped + mm(around, joined)
    out_2 = last_y + mm(last_t, swapped)
    crossing = jnp.where(
        domain == 1, first_x + mm(first_w, in_1) + mm(first_s, own), out_2
    )
    ended = send(crossing, (1, 0), (2, 3))
    out_2, _ = together(out_2, crossing)
    beyond = x_3 + mm(w_3, out_2)

    weight = weights / (k * energies)
    terms = charge(places, weight, energies, x, high, low, probes, in_1, swapped, own, beyond, ended)
    if energies == 8:
        half = energies // 2
        total = terms[:half] + near(terms[half:], (1,))[0]
        parts = [near(total[j], (2 * j,))[0] for j in range(1, half)]
        return total[0] + parts[0] + parts[1] + parts[2]
    split = terms.reshape(n, energies, b // energies).transpose(1, 0, 2)
    return jnp.sum(lax.all_to_all(split, "energy", 0, 0, tiled=True), axis=0)


def solution(mesh):
    placed = (
        P("energy", "dom", None, None),
        P("energy", "dom", None, None),
        P("energy", "dom", None, None),
        P("dom", "energy", None),
        P("dom"),
        P(),
        P("dom", None, None),
        P("energy"),
    )
    return jax.shard_map(
        per_device, mesh=mesh, in_specs=placed, out_specs=P("dom", "energy"), check_vma=False
    )
```

time: 304 us -> 118 us (0.39)
  matrix products: 168 us -> 13.3 us
  Pallas kernels: 0 us -> 39.3 us
  blocking collectives: 22.3 us -> 0 us
  waiting for transfers between devices: 50.1 us -> 31.6 us
  between operations: 15.1 us -> 1.18 us
  starting transfers between devices: 34 us -> 24.6 us
    dot_general x93 -> x17, matrix products: 168 us -> 13.3 us  [mm(): return jnp.dot(a, b, precision=HIGH)]
    pallas_call x0 -> x5, Pallas kernels: none -> 39.3 us  [the longest x1 15.5 us: local_maps(): pl.pallas_call(local_kernel, in_specs=[HBM] * 4, out_specs=[HBM] * 3 + [V...]
    unnamed x1 -> x0, blocking collectives: 22.3 us -> none
    ppermute x12 -> x22, waiting for transfers between devices: 50.1 us -> 31.6 us  [the longest x11 23.5 us: send(): return lax.ppermute(x, 'dom', list(pairs))]
    ppermute x12 -> x22, starting transfers between devices: 34 us -> 24.6 us  [the longest x11 15.5 us: send(): return lax.ppermute(x, 'dom', list(pairs))]
  transfers between devices with their start and end apart: 13 -> 22, of which waited for: 11 -> 11; matrix products, arithmetic and copies ran while one was open for 22% -> 8% of each run, Pallas kernels for 0% -> 31%
where the time goes in v2:
time: 118 us; the launch traced here: 117 us
  Pallas kernels  39.3 us (33%)
  waiting for transfers between devices  31.6 us (27%)
  starting transfers between devices  24.6 us (21%)
  matrix products  13.3 us (11%)
  local copies, waits for them, and re-layouts  4.38 us (4%)
  other arithmetic  2.78 us (2%)
  between operations  1.18 us (1%)
    ppermute x11, waiting for transfers between devices, send(): return lax.ppermute(x, 'dom', list(pairs))  23.5 us
    pallas_call x1, Pallas kernels, local_maps(): pl.pallas_call(local_kernel, in_specs=[HBM] * 4, out_specs=[HBM] * 3 + [V...  15.5 us
    ppermute x11, starting transfers between devices, send(): return lax.ppermute(x, 'dom', list(pairs))  15.5 us
    dot_general x17, matrix products, mm(): return jnp.dot(a, b, precision=HIGH)  13.3 us
    pallas_call x1, Pallas kernels, second(): pl.pallas_call(second_kernel, in_specs=[VMEM] * 9, out_specs=[VMEM] * 3,...  11.2 us
    pallas_call x2, Pallas kernels, drive(): pl.pallas_call(functools.partial(drive_kernel, start, len(pieces)), grid=...  10 us
    ppermute x11, starting transfers between devices, near(): lax.ppermute(x, 'energy', [(i, i ^ way) for i in range(peers)])  9.1 us
    ppermute x11, waiting for transfers between devices, near(): lax.ppermute(x, 'energy', [(i, i ^ way) for i in range(peers)])  8.15 us
  transfers between devices with their start and end apart: 22, of which 11 were waited for; matrix products, arithmetic and copies ran while one was open for 8% of the time, Pallas kernels for 31%

profile of v2, /device:TPU:0, one launch (start us, length us, event | category | flops | bytes accessed | tf_op | source)
XLA Modules:
  0.0 117.2 jit_solution(9142674634254054480)
XLA Ops:
  0.0 3.0 %collective-permute-start.1 = (f32[8,40,320]{2,1,0:T(8,128)}, f32[8,40,320]{2,1,0:T(8,128)S(1)}, u32[]{:S(2)}, u32[]{:S(2)}) collective-permute-start(f32[8,40,320]{2,1,0:T(8,128)} %rest_0_.3), channel_id=1, source_target_pairs={{0,16},{4,20},{8,24},{12,28},{16,0},{20,4},{24,8},{28,12},{1,17},{... | collective-permute-start | bytes 1228808 | tf_op jit(solution)/shard_map/ppermute | solution.py:361
  3.0 1.5 %collective-permute-start = (f32[8,40,320]{2,1,0:T(8,128)}, f32[8,40,320]{2,1,0:T(8,128)S(1)}, u32[]{:S(2)}, u32[]{:S(2)}) collective-permute-start(f32[8,40,320]{2,1,0:T(8,128)} %rest_0_.3), channel_id=1, source_target_pairs={{0,8},{4,12},{8,0},{12,4},{16,24},{20,28},{24,16},{28,20},{1,9},{5... | collective-permute-start | bytes 1228808 | tf_op jit(solution)/shard_map/ppermute | solution.py:361
  4.5 15.5 %local_maps.1 = (f32[8,320,128]{2,1,0:T(8,128)}, bf16[8,320,768]{2,1,0:T(8,128)(2,1)}, bf16[8,320,768]{2,1,0:T(8,128)(2,1)}, f32[320,128]{1,0:T(8,128)S(1)}, f32...) custom-call(f32[8,320,320]{2,1,0:T(8,128)} %bitcast.50, ...), custom_call_target="tpu_custom_call" | custom-call | tf_op jit(solution)/shard_map/local_maps/pallas_call | solution.py:189
  20.0 4.0 %collective-permute-start.2 = (f32[320,128]{1,0:T(8,128)S(1)}, f32[320,128]{1,0:T(8,128)S(1)}, u32[]{:S(2)}, u32[]{:S(2)}) collective-permute-start(f32[320,128]{1,0:T(8,128)S(1)} %get-tuple-element.52), channel_id=1, source_target_pairs={{0,1},{4,5},{8,9},{12,13},{16,17},{20,21},{24,25},{28,29}} | collective-permute-start | bytes 491528 | tf_op jit(solution)/shard_map/ppermute | solution.py:356
  24.0 2.2 %collective-permute-done.3.rest_6_ = f32[8,40,320]{2,1,0:T(8,128)} collective-permute-done((f32[8,40,320]{2,1,0:T(8,128)}, f32[8,40,320]{2,1,0:T(8,128)}, u32[]{:S(2)}, u32[]{:S(2)}) %collective-permute-start.3) | collective-permute-done | bytes 409632 | tf_op jit(solution)/shard_map/ppermute | solution.py:361
  26.2 0.6 collective-permute-done.2
  27.1 1.3 %collective-permute-start.4 = (f32[320,128]{1,0:T(8,128)S(1)}, f32[320,128]{1,0:T(8,128)}, u32[]{:S(2)}, u32[]{:S(2)}) collective-permute-start(f32[320,128]{1,0:T(8,128)S(1)} %convolution_add_fusion.11), channel_id=1, source_target_pairs={{1,2},{5,6},{9,10},{13,14},{17,18},{21,22},{25,26},{29,30}} | collective-permute-start | bytes 491528 | tf_op jit(solution)/shard_map/ppermute | solution.py:356
  28.4 1.5 %collective-permute-start.5 = (f32[320,448]{1,0:T(8,128)}, f32[320,448]{1,0:T(8,128)}, u32[]{:S(2)}, u32[]{:S(2)}) collective-permute-start(f32[320,448]{1,0:T(8,128)} %get-tuple-element.56), channel_id=1, source_target_pairs={{3,2},{7,6},{11,10},{15,14},{19,18},{23,22},{27,26},{31,30}} | collective-permute-start | bytes 1720328 | tf_op jit(solution)/shard_map/ppermute | solution.py:356
  29.9 0.5 collective-permute-start.7
  30.4 0.5 collective-permute-start.9
  31.1 1.2 %convolution_add_fusion.9 = f32[320,128]{1,0:T(8,128)S(1)} fusion(f32[320,128]{1,0:T(8,128)S(1)} %get-tuple-element.52, f32[320,320]{1,0:T(8,128)S(1)} %get-tuple-element.54, f32[320,128]{1,0:T(8,128)} %collective-permute-done.4), kind=kOutput, calls=%fused_computation.12 | convolution fusion | flops 78684160 | bytes 901120 | tf_op jit(solution)/shard_map/dot_general | solution.py:352
  32.4 0.9 collective-permute-done.7.rest_3_
  33.3 0.7 collective-permute-done.8.rest_5_
  34.0 4.9 %drive_maps.2 = (bf16[8,320,640]{2,1,0:T(8,128)(2,1)S(1)}, bf16[8,320,640]{2,1,0:T(8,128)(2,1)S(1)}, bf16[8,320,640]{2,1,0:T(8,128)(2,1)S(1)}) custom-call(s32[1]{0:T(128)} %bitcast.1.me, f32[8]{0:T(128)S(1)} %select_reduce_fusion.scale, f32[8,320,320]{2,1,0:T(8,128)} %bitcast.51, f32[8,320,320]{2,1,0:T(8,128)} %bitcast.54, f32[8,320,320]{2,1,0:T(8,128)} %bitcast.57, ...), custom_call_target="tpu_custom_call" | custom-call | tf_op jit(solution)/shard_map/drive_maps/pallas_call | solution.py:249
  39.0 1.4 %fusion.10 = f32[320,128]{1,0:T(8,128)S(1)} fusion(f32[320,128]{1,0:T(8,128)S(1)} %convolution_add_fusion.9, f32[320,448]{1,0:T(8,128)} %collective-permute-done.5), kind=kOutput, calls=%fused_computation.33 | convolution fusion | flops 78643200 | bytes 819200 | tf_op jit(solution)/shard_map/dot_general | solution.py:352
  40.5 1.3 %fusion.6 = f32[320,128]{1,0:T(8,128)S(1)} fusion(f32[320,320]{1,0:T(8,128)S(1)} %get-tuple-element.55, f32[320,128]{1,0:T(8,128)S(1)} %fusion.10, f32[320,448]{1,0:T(8,128)} %collective-permute-done.5), kind=kOutput, calls=%fused_computation.21 | convolution fusion | flops 78684160 | bytes 901120 | tf_op jit(solution)/shard_map/dot_general | solution.py:352
  41.8 1.3 %fusion.3 = f32[320,128]{1,0:T(8,128)S(1)} fusion(f32[320,128]{1,0:T(8,128)S(1)} %fusion.6, f32[320,128]{1,0:T(8,128)S(1)} %get-tuple-element.48, f32[320,320]{1,0:T(8,128)S(1)} %get-tuple-element.49, f32[320,128]{1,0:T(8,128)S(1)} %collective-permute-done.2, f32[320,128]{1,0:T(8,128)} %collective-permute-done.4), kind=kOutput, calls=%fused_computation.14 | convolution fusion | flops 78766080 | bytes 1228800 | tf_op jit(solution)/shard_map/dot_general | solution.py:352
  43.0 0.8 collective-permute-start.10
  43.9 5.1 %drive_maps.3 = (bf16[8,320,640]{2,1,0:T(8,128)(2,1)S(1)}, bf16[8,320,640]{2,1,0:T(8,128)(2,1)S(1)}, bf16[8,320,640]{2,1,0:T(8,128)(2,1)S(1)}) custom-call(s32[1]{0:T(128)} %bitcast.1.me, f32[8]{0:T(128)S(1)} %select_reduce_fusion.scale, f32[8,320,320]{2,1,0:T(8,128)} %bitcast.52, ...), custom_call_target="tpu_custom_call", output_to_operand_aliasing={{0}: (13, {}), {1}: (14, {}), {2}: (15, {})} | custom-call | tf_op jit(solution)/shard_map/drive_maps/pallas_call | solution.py:249
  49.7 1.6 %collective-permute-start.12 = (f32[320,128]{1,0:T(8,128)S(1)}, f32[320,128]{1,0:T(8,128)S(1)}, u32[]{:S(2)}, u32[]{:S(2)}) collective-permute-start(f32[320,128]{1,0:T(8,128)S(1)} %fusion.2), channel_id=1, source_target_pairs={{1,0},{5,4},{9,8},{13,12},{17,16},{21,20},{25,24},{29,28}} | collective-permute-start | bytes 491528 | tf_op jit(solution)/shard_map/ppermute | solution.py:356
  51.3 0.8 collective-permute-start.11
  52.1 1.1 slice.25
  53.2 9.8 %collective-permute-done.12 = f32[320,128]{1,0:T(8,128)S(1)} collective-permute-done((f32[320,128]{1,0:T(8,128)S(1)}, f32[320,128]{1,0:T(8,128)S(1)}, u32[]{:S(2)}, u32[]{:S(2)}) %collective-permute-start.12) | collective-permute-done | bytes 163872 | tf_op jit(solution)/shard_map/ppermute | solution.py:356
  63.0 0.6 fusion.13
  63.6 0.6 convolution_add_fusion
  64.2 0.9 collective-permute-start.13
  65.1 1.0 add_add_fusion.1.inflow
  66.1 1.0 add_add_fusion.outflow
  67.1 11.2 %second_local.1 = (f32[8,320,128]{2,1,0:T(8,128)S(1)}, f32[320,128]{1,0:T(8,128)S(1)}, f32[320,128]{1,0:T(8,128)S(1)}) custom-call(f32[8,320,128]{2,1,0:T(8,128)S(1)} %copy-done.10, bf16[8,320,768]{2,1,0:T(8,128)(2,1)S(1)} %copy-done, bf16[8,320,768]{2,1,0:T(8,128)(2,1)S(1)} %copy-done.2, bf16[8,320,640]{2,1,0:T(8,128)(2,1)S(1)} %get-tuple-element.72.driver, ...), custom_call_target="tpu_custom_call" | custom-call | tf_op jit(solution)/shard_map/second_local/pallas_call | solution.py:305
  78.3 1.1 copy-done.11
  79.4 0.8 copy-done.16
  80.2 0.7 collective-permute-start.15
  80.9 2.1 %collective-permute-start.14 = (f32[320,128]{1,0:T(8,128)S(1)}, f32[320,128]{1,0:T(8,128)S(1)}, u32[]{:S(2)}, u32[]{:S(2)}) collective-permute-start(f32[320,128]{1,0:T(8,128)S(1)} %get-tuple-element.81), channel_id=1, source_target_pairs={{0,1},{4,5},{8,9},{12,13},{16,17},{20,21},{24,25},{28,29}} | collective-permute-start | bytes 491528 | tf_op jit(solution)/shard_map/ppermute | solution.py:356
  83.0 1.5 %convolution_add_fusion.6 = f32[320,128]{1,0:T(8,128)S(1)} fusion(f32[320,128]{1,0:T(8,128)S(1)} %collective-permute-done.15, f32[320,320]{1,0:T(8,128)} %copy-done.13, f32[320,128]{1,0:T(8,128)S(1)} %get-tuple-element.81), kind=kOutput, calls=%fused_computation.7 | convolution fusion | flops 78684160 | bytes 901120 | tf_op jit(solution)/shard_map/dot_general | solution.py:352
  84.8 0.9 collective-permute-done.14.in_1
  86.1 0.7 collective-permute-start.16
  87.5 1.4 %convolution_add_fusion.4.out_1 = f32[320,128]{1,0:T(8,128)S(1)} fusion(f32[320,128]{1,0:T(8,128)S(1)} %collective-permute-done.16.in_2, f32[320,320]{1,0:T(8,128)} %copy-done.16, f32[320,128]{1,0:T(8,128)S(1)} %fusion.1), kind=kOutput, calls=%fused_computation.5 | convolution fusion | flops 78684160 | bytes 901120 | tf_op jit(solution)/shard_map/dot_general | solution.py:352
  89.9 1.3 %collective-permute-start.17 = (f32[320,128]{1,0:T(8,128)S(1)}, f32[320,128]{1,0:T(8,128)S(1)}, u32[]{:S(2)}, u32[]{:S(2)}) collective-permute-start(f32[320,128]{1,0:T(8,128)S(1)} %fusion.4), channel_id=1, source_target_pairs={{1,0},{2,3},{5,4},{6,7},{9,8},{10,11},{13,12},{14,15},{17,16},{18,... | collective-permute-start | bytes 491528 | tf_op jit(solution)/shard_map/ppermute | solution.py:356
  91.2 1.4 %convolution_add_fusion.1.out_2 = f32[320,128]{1,0:T(8,128)S(1)} fusion(f32[320,128]{1,0:T(8,128)S(1)} %collective-permute-done.15, f32[320,320]{1,0:T(8,128)} %copy-done.13, f32[320,128]{1,0:T(8,128)S(1)} %convolution_add_fusion.3), kind=kOutput, calls=%fused_computation.1 | convolution fusion | flops 78684160 | bytes 901120 | tf_op jit(solution)/shard_map/dot_general | solution.py:352
  92.6 12.2 %collective-permute-done.17.ended = f32[320,128]{1,0:T(8,128)S(1)} collective-permute-done((f32[320,128]{1,0:T(8,128)S(1)}, f32[320,128]{1,0:T(8,128)S(1)}, u32[]{:S(2)}, u32[]{:S(2)}) %collective-permute-start.17) | collective-permute-done | bytes 163872 | tf_op jit(solution)/shard_map/ppermute | solution.py:356
  104.7 1.3 %copy-done.12 = f32[8,320,128]{2,1,0:T(8,128)S(1)} copy-done((f32[8,320,128]{2,1,0:T(8,128)S(1)}, f32[8,320,128]{2,1,0:T(8,128)}, u32[]{:S(2)}) %copy-start.12) | copy-done | bytes 1310744
  106.1 2.6 %charge_terms.1 = f32[8,8,40]{2,1,0:T(8,128)S(1)} custom-call(s32[2]{0:T(128)S(1)} %pad_add_fusion.places, f32[1]{0:T(128)S(6)} %div.3.weight, f32[8,320,128]{2,1,0:T(8,128)S(1)} %copy-done.12, bf16[8,320,768]{2,1,0:T(8,128)(2,1)S(1)} %copy-done.1, bf16[8,320,768]{2,1,0:T(8,128)(2,1)S(1)} %copy-done.3, f32[8,320,128]{2,1,0:T(8,128)S(1)} %copy-done.4, ...), custom_call_target="tpu_custom_call" | custom-call | tf_op jit(solution)/shard_map/charge_terms/pallas_call | solution.py:340
  108.8 1.2 collective-permute-done.18
  110.0 1.5 %collective-permute-start.19 = (f32[8,40]{1,0:T(8,128)S(1)}, f32[8,40]{1,0:T(8,128)S(1)}, u32[]{:S(2)}, u32[]{:S(2)}) collective-permute-start(f32[8,40]{1,0:T(8,128)S(1)} %get-tuple-element.85), channel_id=1, source_target_pairs={{0,8},{4,12},{8,0},{12,4},{16,24},{20,28},{24,16},{28,20},{1,9},{5... | collective-permute-start | bytes 3848 | tf_op jit(solution)/shard_map/ppermute | solution.py:361
  111.5 1.5 %collective-permute-start.21 = (f32[8,40]{1,0:T(8,128)S(1)}, f32[8,40]{1,0:T(8,128)S(1)}, u32[]{:S(2)}, u32[]{:S(2)}) collective-permute-start(f32[8,40]{1,0:T(8,128)S(1)} %get-tuple-element.86), channel_id=1, source_target_pairs={{0,24},{4,28},{8,16},{12,20},{16,8},{20,12},{24,0},{28,4},{1,25},{... | collective-permute-start | bytes 3848 | tf_op jit(solution)/shard_map/ppermute | solution.py:361
  113.6 2.4 %collective-permute-done.21 = f32[8,40]{1,0:T(8,128)S(1)} collective-permute-done((f32[8,40]{1,0:T(8,128)S(1)}, f32[8,40]{1,0:T(8,128)S(1)}, u32[]{:S(2)}, u32[]{:S(2)}) %collective-permute-start.21) | collective-permute-done | bytes 1312 | tf_op jit(solution)/shard_map/ppermute | solution.py:361
  116.0 0.6 collective-permute-done.20
  116.6 0.6 fusion.9
  (65 shorter events, 3.7 us)
Async XLA Ops:
  0.0 20.0 %collective-permute-start.1 = (f32[8,40,320]{2,1,0:T(8,128)}, f32[8,40,320]{2,1,0:T(8,128)S(1)}, u32[]{:S(2)}, u32[]{:S(2)}) collective-permute-start(f32[8,40,320]{2,1,0:T(8,128)} %rest_0_.3), channel_id=1, source_target_pairs={{0,16},{4,20},{8,24},{12,28},{16,0},{20,4},{24,8},{28,12},{1,17},{... | collective-permute-start | bytes 1228808 | tf_op jit(solution)/shard_map/ppermute | solution.py:361
  3.0 17.0 %collective-permute-start = (f32[8,40,320]{2,1,0:T(8,128)}, f32[8,40,320]{2,1,0:T(8,128)S(1)}, u32[]{:S(2)}, u32[]{:S(2)}) collective-permute-start(f32[8,40,320]{2,1,0:T(8,128)} %rest_0_.3), channel_id=1, source_target_pairs={{0,8},{4,12},{8,0},{12,4},{16,24},{20,28},{24,16},{28,20},{1,9},{5... | collective-permute-start | bytes 1228808 | tf_op jit(solution)/shard_map/ppermute | solution.py:361
  4.5 21.8 %collective-permute-start.3 = (f32[8,40,320]{2,1,0:T(8,128)}, f32[8,40,320]{2,1,0:T(8,128)}, u32[]{:S(2)}, u32[]{:S(2)}) collective-permute-start(f32[8,40,320]{2,1,0:T(8,128)} %rest_0_.3), channel_id=1, source_target_pairs={{0,24},{4,28},{8,16},{12,20},{16,8},{20,12},{24,0},{28,4},{1,25},{... | collective-permute-start | bytes 1228808 | tf_op jit(solution)/shard_map/ppermute | solution.py:361
  4.5 25.5 %copy-start.5 = (f32[8,40,320]{2,1,0:T(8,128)S(1)}, f32[8,40,320]{2,1,0:T(8,128)}, u32[]{:S(2)}) copy-start(f32[8,40,320]{2,1,0:T(8,128)} %rest_0_.3) | copy-start | bytes 1228804
  4.5 26.5 %copy-start.17 = (f32[32]{0:T(128)S(1)}, f32[32]{0:T(128)}, u32[]{:S(2)}) copy-start(f32[32]{0:T(128)} %param.13) | copy-start | bytes 388
  4.5 26.5 %copy-start.18 = (s32[8]{0:T(128)S(1)}, s32[8]{0:T(128)}, u32[]{:S(2)}) copy-start(s32[8]{0:T(128)} %param.12) | copy-start | bytes 100
  20.0 19.0 %copy-start.6 = (f32[8,40,320]{2,1,0:T(8,128)}, f32[8,40,320]{2,1,0:T(8,128)S(1)}, u32[]{:S(2)}) copy-start(f32[8,40,320]{2,1,0:T(8,128)S(1)} %collective-permute-done.1.rest_4_) | copy-start | bytes 1228804
  20.0 19.0 %copy-start.8 = (f32[8,40,320]{2,1,0:T(8,128)}, f32[8,40,320]{2,1,0:T(8,128)S(1)}, u32[]{:S(2)}) copy-start(f32[8,40,320]{2,1,0:T(8,128)S(1)} %collective-permute-done.rest_2_) | copy-start | bytes 1228804
  20.0 6.8 %collective-permute-start.2 = (f32[320,128]{1,0:T(8,128)S(1)}, f32[320,128]{1,0:T(8,128)S(1)}, u32[]{:S(2)}, u32[]{:S(2)}) collective-permute-start(f32[320,128]{1,0:T(8,128)S(1)} %get-tuple-element.52), channel_id=1, source_target_pairs={{0,1},{4,5},{8,9},{12,13},{16,17},{20,21},{24,25},{28,29}} | collective-permute-start | bytes 491528 | tf_op jit(solution)/shard_map/ppermute | solution.py:356
  26.8 15.0 %copy-start.14 = (f32[320,128]{1,0:T(8,128)}, f32[320,128]{1,0:T(8,128)S(1)}, u32[]{:S(2)}) copy-start(f32[320,128]{1,0:T(8,128)S(1)} %collective-permute-done.2) | copy-start | bytes 491524
  27.1 3.3 %collective-permute-start.4 = (f32[320,128]{1,0:T(8,128)S(1)}, f32[320,128]{1,0:T(8,128)}, u32[]{:S(2)}, u32[]{:S(2)}) collective-permute-start(f32[320,128]{1,0:T(8,128)S(1)} %convolution_add_fusion.11), channel_id=1, source_target_pairs={{1,2},{5,6},{9,10},{13,14},{17,18},{21,22},{25,26},{29,30}} | collective-permute-start | bytes 491528 | tf_op jit(solution)/shard_map/ppermute | solution.py:356
  28.4 10.6 %collective-permute-start.5 = (f32[320,448]{1,0:T(8,128)}, f32[320,448]{1,0:T(8,128)}, u32[]{:S(2)}, u32[]{:S(2)}) collective-permute-start(f32[320,448]{1,0:T(8,128)} %get-tuple-element.56), channel_id=1, source_target_pairs={{3,2},{7,6},{11,10},{15,14},{19,18},{23,22},{27,26},{31,30}} | collective-permute-start | bytes 1720328 | tf_op jit(solution)/shard_map/ppermute | solution.py:356
  29.9 2.5 %collective-permute-start.6 = (f32[8,40,320]{2,1,0:T(8,128)S(1)}, f32[8,40,320]{2,1,0:T(8,128)}, u32[]{:S(2)}, u32[]{:S(2)}) collective-permute-start(f32[8,40,320]{2,1,0:T(8,128)S(1)} %copy-done.5), channel_id=1, source_target_pairs={{0,4},{4,0},{8,12},{12,8},{16,20},{20,16},{24,28},{28,24},{1,5},{5... | collective-permute-start | bytes 1228808 | tf_op jit(solution)/shard_map/ppermute | solution.py:361
  29.9 3.4 %collective-permute-start.7 = (f32[8,40,320]{2,1,0:T(8,128)S(1)}, f32[8,40,320]{2,1,0:T(8,128)}, u32[]{:S(2)}, u32[]{:S(2)}) collective-permute-start(f32[8,40,320]{2,1,0:T(8,128)S(1)} %collective-permute-done.rest_2_), channel_id=1, source_target_pairs={{0,4},{4,0},{8,12},{12,8},{16,20},{20,16},{24,28},{28,24},{1,5},{5... | collective-permute-start | bytes 1228808 | tf_op jit(solution)/shard_map/ppermute | solution.py:361
  30.4 3.6 %collective-permute-start.8 = (f32[8,40,320]{2,1,0:T(8,128)S(1)}, f32[8,40,320]{2,1,0:T(8,128)}, u32[]{:S(2)}, u32[]{:S(2)}) collective-permute-start(f32[8,40,320]{2,1,0:T(8,128)S(1)} %collective-permute-done.1.rest_4_), channel_id=1, source_target_pairs={{0,4},{4,0},{8,12},{12,8},{16,20},{20,16},{24,28},{28,24},{1,5},{5... | collective-permute-start | bytes 1228808 | tf_op jit(solution)/shard_map/ppermute | solution.py:361
  30.4 3.6 %collective-permute-start.9 = (f32[8,40,320]{2,1,0:T(8,128)}, f32[8,40,320]{2,1,0:T(8,128)}, u32[]{:S(2)}, u32[]{:S(2)}) collective-permute-start(f32[8,40,320]{2,1,0:T(8,128)} %collective-permute-done.3.rest_6_), channel_id=1, source_target_pairs={{0,4},{4,0},{8,12},{12,8},{16,20},{20,16},{24,28},{28,24},{1,5},{5... | collective-permute-start | bytes 1228808 | tf_op jit(solution)/shard_map/ppermute | solution.py:361
  39.0 4.8 %copy-start.7 = (f32[8,40,320]{2,1,0:T(8,128)S(1)}, f32[8,40,320]{2,1,0:T(8,128)}, u32[]{:S(2)}) copy-start(f32[8,40,320]{2,1,0:T(8,128)} %copy-done.6) | copy-start | bytes 1228804
  39.0 4.8 %copy-start.9 = (f32[8,40,320]{2,1,0:T(8,128)S(1)}, f32[8,40,320]{2,1,0:T(8,128)}, u32[]{:S(2)}) copy-start(f32[8,40,320]{2,1,0:T(8,128)} %copy-done.8) | copy-start | bytes 1228804
  43.0 6.3 %copy-start.15 = (f32[320,128]{1,0:T(8,128)S(1)}, f32[320,128]{1,0:T(8,128)}, u32[]{:S(2)}) copy-start(f32[320,128]{1,0:T(8,128)} %copy-done.14) | copy-start | bytes 491524
  43.0 6.0 %collective-permute-start.10 = (f32[320,128]{1,0:T(8,128)S(1)}, f32[320,128]{1,0:T(8,128)S(1)}, u32[]{:S(2)}, u32[]{:S(2)}) collective-permute-start(f32[320,128]{1,0:T(8,128)S(1)} %fusion.3), channel_id=1, source_target_pairs={{2,1},{6,5},{10,9},{14,13},{18,17},{22,21},{26,25},{30,29}} | collective-permute-start | bytes 491528 | tf_op jit(solution)/shard_map/ppermute | solution.py:356
  43.9 23.2 %copy-start.4 = (f32[8,320,128]{2,1,0:T(8,128)S(1)}, f32[8,320,128]{2,1,0:T(8,128)}, u32[]{:S(2)}) copy-start(f32[8,320,128]{2,1,0:T(8,128)} %probe.3) | copy-start | bytes 3932164
  43.9 23.2 %copy-start.10 = (f32[8,320,128]{2,1,0:T(8,128)S(1)}, f32[8,320,128]{2,1,0:T(8,128)}, u32[]{:S(2)}) copy-start(f32[8,320,128]{2,1,0:T(8,128)} %get-tuple-element.45.x) | copy-start | bytes 3932164
  49.0 18.1 %copy-start.2 = (bf16[8,320,768]{2,1,0:T(8,128)(2,1)S(1)}, bf16[8,320,768]{2,1,0:T(8,128)(2,1)}, u32[]{:S(2)}) copy-start(bf16[8,320,768]{2,1,0:T(8,128)(2,1)} %get-tuple-element.47.low) | copy-start | bytes 11796484
  49.4 17.7 %copy-start = (bf16[8,320,768]{2,1,0:T(8,128)(2,1)S(1)}, bf16[8,320,768]{2,1,0:T(8,128)(2,1)}, u32[]{:S(2)}) copy-start(bf16[8,320,768]{2,1,0:T(8,128)(2,1)} %get-tuple-element.46.high) | copy-start | bytes 11796484
  49.7 13.3 %collective-permute-start.12 = (f32[320,128]{1,0:T(8,128)S(1)}, f32[320,128]{1,0:T(8,128)S(1)}, u32[]{:S(2)}, u32[]{:S(2)}) collective-permute-start(f32[320,128]{1,0:T(8,128)S(1)} %fusion.2), channel_id=1, source_target_pairs={{1,0},{5,4},{9,8},{13,12},{17,16},{21,20},{25,24},{29,28}} | collective-permute-start | bytes 491528 | tf_op jit(solution)/shard_map/ppermute | solution.py:356
  51.3 13.8 %collective-permute-start.11 = (f32[320,128]{1,0:T(8,128)S(1)}, f32[320,128]{1,0:T(8,128)S(1)}, u32[]{:S(2)}, u32[]{:S(2)}) collective-permute-start(f32[320,128]{1,0:T(8,128)S(1)} %convolution_add_fusion.9), channel_id=1, source_target_pairs={{2,3},{6,7},{10,11},{14,15},{18,19},{22,23},{26,27},{30,31}} | collective-permute-start | bytes 491528 | tf_op jit(solution)/shard_map/ppermute | solution.py:356
  53.2 12.0 %copy-start.13 = (f32[320,320]{1,0:T(8,128)}, f32[320,320]{1,0:T(8,128)S(1)}, u32[]{:S(2)}) copy-start(f32[320,320]{1,0:T(8,128)S(1)} %slice.25) | copy-start | bytes 1228804
  64.2 15.2 %collective-permute-start.13 = (f32[320,320]{1,0:T(8,128)S(1)}, f32[320,320]{1,0:T(8,128)S(1)}, u32[]{:S(2)}, u32[]{:S(2)}) collective-permute-start(f32[320,320]{1,0:T(8,128)S(1)} %convolution_add_fusion), channel_id=1, source_target_pairs={{2,1},{6,5},{10,9},{14,13},{18,17},{22,21},{26,25},{30,29}} | collective-permute-start | bytes 1228808 | tf_op jit(solution)/shard_map/ppermute | solution.py:356
  78.3 1.2 copy-start.11
  79.4 0.8 copy-start.16
  80.2 2.7 %collective-permute-start.15 = (f32[320,128]{1,0:T(8,128)S(1)}, f32[320,128]{1,0:T(8,128)S(1)}, u32[]{:S(2)}, u32[]{:S(2)}) collective-permute-start(f32[320,128]{1,0:T(8,128)S(1)} %get-tuple-element.82), channel_id=1, source_target_pairs={{3,2},{7,6},{11,10},{15,14},{19,18},{23,22},{27,26},{31,30}} | collective-permute-start | bytes 491528 | tf_op jit(solution)/shard_map/ppermute | solution.py:356
  80.9 4.9 %collective-permute-start.14 = (f32[320,128]{1,0:T(8,128)S(1)}, f32[320,128]{1,0:T(8,128)S(1)}, u32[]{:S(2)}, u32[]{:S(2)}) collective-permute-start(f32[320,128]{1,0:T(8,128)S(1)} %get-tuple-element.81), channel_id=1, source_target_pairs={{0,1},{4,5},{8,9},{12,13},{16,17},{20,21},{24,25},{28,29}} | collective-permute-start | bytes 491528 | tf_op jit(solution)/shard_map/ppermute | solution.py:356
  82.9 21.8 %copy-start.3 = (bf16[8,320,768]{2,1,0:T(8,128)(2,1)S(1)}, bf16[8,320,768]{2,1,0:T(8,128)(2,1)}, u32[]{:S(2)}) copy-start(bf16[8,320,768]{2,1,0:T(8,128)(2,1)} %get-tuple-element.47.low) | copy-start | bytes 11796484
  84.8 19.9 %copy-start.1 = (bf16[8,320,768]{2,1,0:T(8,128)(2,1)S(1)}, bf16[8,320,768]{2,1,0:T(8,128)(2,1)}, u32[]{:S(2)}) copy-start(bf16[8,320,768]{2,1,0:T(8,128)(2,1)} %get-tuple-element.46.high) | copy-start | bytes 11796484
  86.1 1.4 %collective-permute-start.16 = (f32[320,128]{1,0:T(8,128)S(1)}, f32[320,128]{1,0:T(8,128)S(1)}, u32[]{:S(2)}, u32[]{:S(2)}) collective-permute-start(f32[320,128]{1,0:T(8,128)S(1)} %fusion.1), channel_id=1, source_target_pairs={{1,2},{2,1},{5,6},{6,5},{9,10},{10,9},{13,14},{14,13},{17,18},{18,... | collective-permute-start | bytes 491528 | tf_op jit(solution)/shard_map/ppermute | solution.py:356
  89.9 14.8 %collective-permute-start.17 = (f32[320,128]{1,0:T(8,128)S(1)}, f32[320,128]{1,0:T(8,128)S(1)}, u32[]{:S(2)}, u32[]{:S(2)}) collective-permute-start(f32[320,128]{1,0:T(8,128)S(1)} %fusion.4), channel_id=1, source_target_pairs={{1,0},{2,3},{5,4},{6,7},{9,8},{10,11},{13,12},{14,15},{17,16},{18,... | collective-permute-start | bytes 491528 | tf_op jit(solution)/shard_map/ppermute | solution.py:356
  104.7 1.3 %copy-start.12 = (f32[8,320,128]{2,1,0:T(8,128)S(1)}, f32[8,320,128]{2,1,0:T(8,128)}, u32[]{:S(2)}) copy-start(f32[8,320,128]{2,1,0:T(8,128)} %copy-done.11) | copy-start | bytes 3932164
  108.7 1.2 %collective-permute-start.18 = (f32[4,8,40]{2,1,0:T(8,128)S(1)}, f32[4,8,40]{2,1,0:T(8,128)S(1)}, u32[]{:S(2)}, u32[]{:S(2)}) collective-permute-start(f32[4,8,40]{2,1,0:T(8,128)S(1)} %slice.33), channel_id=1, source_target_pairs={{0,4},{4,0},{8,12},{12,8},{16,20},{20,16},{24,28},{28,24},{1,5},{5... | collective-permute-start | bytes 15368 | tf_op jit(solution)/shard_map/ppermute | solution.py:361
  110.0 3.7 %collective-permute-start.19 = (f32[8,40]{1,0:T(8,128)S(1)}, f32[8,40]{1,0:T(8,128)S(1)}, u32[]{:S(2)}, u32[]{:S(2)}) collective-permute-start(f32[8,40]{1,0:T(8,128)S(1)} %get-tuple-element.85), channel_id=1, source_target_pairs={{0,8},{4,12},{8,0},{12,4},{16,24},{20,28},{24,16},{28,20},{1,9},{5... | collective-permute-start | bytes 3848 | tf_op jit(solution)/shard_map/ppermute | solution.py:361
  111.5 4.5 %collective-permute-start.21 = (f32[8,40]{1,0:T(8,128)S(1)}, f32[8,40]{1,0:T(8,128)S(1)}, u32[]{:S(2)}, u32[]{:S(2)}) collective-permute-start(f32[8,40]{1,0:T(8,128)S(1)} %get-tuple-element.86), channel_id=1, source_target_pairs={{0,24},{4,28},{8,16},{12,20},{16,8},{20,12},{24,0},{28,4},{1,25},{... | collective-permute-start | bytes 3848 | tf_op jit(solution)/shard_map/ppermute | solution.py:361
  113.0 3.6 %collective-permute-start.20 = (f32[8,40]{1,0:T(8,128)S(1)}, f32[8,40]{1,0:T(8,128)S(1)}, u32[]{:S(2)}, u32[]{:S(2)}) collective-permute-start(f32[8,40]{1,0:T(8,128)S(1)} %get-tuple-element.87), channel_id=1, source_target_pairs={{0,16},{4,20},{8,24},{12,28},{16,0},{20,4},{24,8},{28,12},{1,17},{... | collective-permute-start | bytes 3848 | tf_op jit(solution)/shard_map/ppermute | solution.py:361

commit v3 on v2

--- a/solution.py
+++ b/solution.py
@@ -1,5 +1,3 @@
-import functools
-
 import jax
 import jax.numpy as jnp
 from jax import lax
@@ -44,6 +42,10 @@
 
 def shapes(*entries):
     return [jax.ShapeDtypeStruct(shape, kind) for shape, kind in entries]
+
+
+def cost(us):
+    return pl.CostEstimate(flops=int(us * 1e9), bytes_accessed=0, transcendentals=0)
 
 
 def params(mib):
@@ -220,15 +222,15 @@
             pltpu.SemaphoreType.DMA((3, n)),
         ],
         compiler_params=params(52),
+        cost_estimate=cost(15),
         name="local_maps",
     )(*in_hbm(pivots, lower, upper, probes))
 
 
-def drive_kernel(start, count, me, scale, pivot, lower, upper, *rest):
-    pieces, rest = rest[:count], rest[count:]
-    out, lower_out, upper_out, gathered = rest[-4:]
-    step = pl.program_id(0) + start
-    if count > 1:
+def drive_kernel(me, scale, pivot, *rest):
+    pieces, out, gathered = rest[:-2], rest[-2], rest[-1]
+    step = pl.program_id(0)
+    if len(pieces) > 1:
         rows = pieces[0].shape[1]
         for j, piece in enumerate(pieces):
             owner = lax.bitwise_xor(me[0], j)
@@ -236,30 +238,25 @@
         potential = gathered[...]
     else:
         potential = pieces[0][0]
-    out[0] = left_two(apply_three(left_three(pivot[0]), *halves(potential * scale[step])))
-    lower_out[0] = left_two(lower[0])
-    upper_out[0] = left_two(upper[0])
-
-
-def drive(start, stop, me, scale, pivots, lower, upper, pieces, done=()):
+    out[step] = left_two(apply_three(left_three(pivot[0]), *halves(potential * scale[step])))
+
+
+def drive(me, scale, pivots, pieces):
     n, b, _ = pivots.shape
     rows = pieces[0].shape[1]
-    at = lambda i: (i + start, 0, 0)
-    inputs = (me, scale, *in_hbm(pivots, lower, upper), *pieces)
+    at = lambda i: (i, 0, 0)
     return pl.pallas_call(
-        functools.partial(drive_kernel, start, len(pieces)),
-        grid=(stop - start,),
-        in_specs=[SMEM, SMEM]
-        + [pl.BlockSpec((1, b, b), at)] * 3
-        + [pl.BlockSpec((1, rows, b), at)] * len(pieces)
-        + [pl.BlockSpec(memory_space=pl.ANY)] * len(done),
-        out_specs=[pl.BlockSpec((1, b, 2 * b), at)] * 3,
-        out_shape=pinned(*[((n, b, 2 * b), BF16)] * 3),
+        drive_kernel,
+        grid=(n,),
+        in_specs=[SMEM, SMEM, pl.BlockSpec((1, b, b), at)]
+        + [pl.BlockSpec((1, rows, b), at)] * len(pieces),
+        out_specs=VMEM,
+        out_shape=pltpu.VMEM((n, b, 2 * b), BF16),
         scratch_shapes=[pltpu.VMEM((b, b), F32)],
-        input_output_aliases={len(inputs) + i: i for i in range(len(done))},
-        compiler_params=params(12),
+        compiler_params=params(10),
+        cost_estimate=cost(0.01),
         name="drive_maps",
-    )(*inputs, *done)
+    )(me, scale, *in_hbm(pivots, *pieces))
 
 
 def apply_maps(high, low, i, flows):
@@ -270,47 +267,97 @@
     return out[:, :k] + out[:, k:]
 
 
-def second_kernel(
-    x, high, low, driver, lower, upper, probes, inflow, outflow, out, last, first, y
+def second_ahead_kernel(
+    lower, upper, x, high, low, driver, probes, in_1, in_2, in_3, out_0, out_1, out_2,
+    y, last, left_u, l, u, left_l, out, sem,
 ):
     n, b, k = x.shape
-    flows = jnp.concatenate(halves(jnp.concatenate([inflow[...], outflow[...]], axis=0)), axis=1)
+    load_l = lambda i: pltpu.make_async_copy(lower.at[i], l.at[i], sem.at[0, i])
+    load_u = lambda i: pltpu.make_async_copy(upper.at[i], u.at[i], sem.at[1, i])
+
+    def begin(i, c):
+        load_l(i).start()
+        load_u(i).start()
+        return c
+
+    lax.fori_loop(0, n, begin, 0)
+    inflow = in_1[...] + in_2[...] + in_3[...]
+    outflow = out_0[...] + out_1[...] + out_2[...]
+    flows = jnp.concatenate(halves(jnp.concatenate([inflow, outflow], axis=0)), axis=1)
 
     def given(i, c):
+        load_l(i).wait()
+        load_u(i).wait()
         out[i] = apply_two(driver[i], x[i] + apply_maps(high, low, i, flows))
+        left_l[i] = left_two(l[i])
+        left_u[i] = left_two(u[i])
         return c
 
     lax.fori_loop(0, n, given, 0)
     y[0] = out[0]
 
     def ahead(i, c):
-        y[i] = out[i] - apply_two(lower[i], y[i - 1])
+        y[i] = out[i] - apply_two(left_l[i], y[i - 1])
         return c
 
     lax.fori_loop(1, n, ahead, 0)
     last[...] = y[n - 1]
+
+
+def second_ahead(lower, upper, x, high, low, driver, probes, *flows):
+    n, b, k = x.shape
+    return pl.pallas_call(
+        second_ahead_kernel,
+        in_specs=[HBM] * 2 + [VMEM] * (5 + len(flows)),
+        out_specs=[VMEM] * 3,
+        out_shape=pinned(((n, b, k), F32), ((b, k), F32), ((n, b, 2 * b), BF16)),
+        scratch_shapes=[
+            pltpu.VMEM((n, b, b), F32),
+            pltpu.VMEM((n, b, b), F32),
+            pltpu.VMEM((n, b, 2 * b), BF16),
+            pltpu.VMEM((n, b, k), F32),
+            pltpu.SemaphoreType.DMA((2, n)),
+        ],
+        compiler_params=params(18),
+        cost_estimate=cost(9),
+        name="second_ahead",
+    )(*in_hbm(lower, upper), *in_vmem(x, high, low, driver, probes), *flows)
+
+
+def second_back_kernel(y, left_u, x_out, first, out, sem):
+    n = y.shape[0]
+    store = lambda i: pltpu.make_async_copy(out.at[i], x_out.at[i], sem.at[i])
     out[n - 1] = y[n - 1]
+    store(n - 1).start()
 
     def back(r, c):
         i = n - 1 - r
-        out[i] = y[i] - apply_two(upper[i], out[i + 1])
+        out[i] = y[i] - apply_two(left_u[i], out[i + 1])
+        store(i).start()
         return c
 
     lax.fori_loop(1, n, back, 0)
     first[...] = out[0]
 
-
-def second(x, high, low, driver, lower, upper, probes, inflow, outflow):
-    n, b, k = x.shape
+    def drain(i, c):
+        store(i).wait()
+        return c
+
+    lax.fori_loop(0, n, drain, 0)
+
+
+def second_back(y, left_u):
+    n, b, k = y.shape
     return pl.pallas_call(
-        second_kernel,
-        in_specs=[VMEM] * 9,
-        out_specs=[VMEM] * 3,
-        out_shape=pinned(((n, b, k), F32), ((b, k), F32), ((b, k), F32)),
-        scratch_shapes=[pltpu.VMEM((n, b, k), F32)],
-        compiler_params=params(10),
-        name="second_local",
-    )(*in_vmem(x, high, low, driver, lower, upper, probes), inflow, outflow)
+        second_back_kernel,
+        in_specs=[VMEM] * 2,
+        out_specs=[HBM, VMEM],
+        out_shape=[pltpu.HBM((n, b, k), F32), pltpu.VMEM((b, k), F32)],
+        scratch_shapes=[pltpu.VMEM((n, b, k), F32), pltpu.SemaphoreType.DMA((n,))],
+        compiler_params=params(4),
+        cost_estimate=cost(4),
+        name="second_back",
+    )(*in_vmem(y, left_u))
 
 
 def charge_kernel(places, weight, x, high, low, probe, in_1, in_2, out_1, out_2, ended, *outs):
@@ -386,12 +433,10 @@
         pivots, lower, upper, probes
     )
 
-    if by_swaps:
-        last_y, first_xw, even[0], even[1] = together(last_y, first_xw, even[0], even[1])
     in_1 = send(last_y, (0, 1))
     from_3 = send(first_xw, (3, 2))
     if by_swaps:
-        in_1, even[2] = together(in_1, even[2])
+        in_1, *even = together(in_1, *even)
     out_1 = last_y + mm(last_t, in_1)
     in_2 = send(out_1, (1, 2))
     if by_swaps:
@@ -400,46 +445,46 @@
         pieces = [block for pair in zip(even, odd) for block in pair]
     else:
         pieces = [lax.all_gather(potential, "energy", axis=1, tiled=True)]
+    driver = drive(me, grain_scale, pivots, pieces)
+    in_2, from_3, driver = together(in_2, from_3, driver)
     out_2 = last_y + mm(last_t, in_2)
+    base = first_x + mm(first_w, in_1 + in_2)
+    outflow_2 = from_3[:, :k] + mm(from_3[:, k:], out_2)
+    turn = base + mm(first_s, outflow_2)
+    outflow_1 = send(turn, (2, 1))
+    from_3, out_2, _ = together(from_3, out_2, turn)
     in_3 = send(out_2, (2, 3))
-    scale, _ = together(grain_scale, out_2)
-    driven = drive(0, n // 2, me, scale, pivots, lower, upper, pieces)
-    from_3, *driven = together(from_3, *driven)
-    x_3, w_3 = from_3[:, :k], from_3[:, k:]
-    inflow = in_1 + in_2 + in_3
-    outflow_2 = x_3 + mm(w_3, out_2)
-    turn = first_x + mm(first_w, in_1 + in_2) + mm(first_s, outflow_2)
-    outflow_1 = send(turn, (2, 1))
-    scale, _ = together(scale, turn)
-    driven = drive(n // 2, n, me, scale, pivots, lower, upper, pieces, driven)
-    outflow_1, *driven = together(outflow_1, *driven)
-    outflow_0 = send(first_x + mm(first_w, in_1) + mm(first_s, outflow_1), (1, 0))
-    outflow_0, w_3 = together(outflow_0, w_3)
-    around = send(first_w + mm(first_s, mm(w_3, last_t)), (2, 1))
-    outflow = outflow_0 + outflow_1 + outflow_2
-
-    x, last_y, first_x = second(x, high, low, *driven, probes, inflow, outflow)
-
-    last_y, first_x, around = together(last_y, first_x, around)
+    w_3 = from_3[:, k:]
+    around = first_w + mm(first_s, mm(w_3, last_t))
+    outflow_1, around = together(outflow_1, around)
+    around = send(around, (2, 1))
+    outflow_0 = send(base + mm(first_s, outflow_1), (1, 0))
+
+    ahead, last_y, left_u = second_ahead(
+        lower, upper, x, high, low, driver, probes,
+        in_1, in_2, in_3, outflow_0, outflow_1, outflow_2,
+    )
+
+    in_1 = send(last_y, (0, 1))
+    x, first_x = second_back(ahead, left_u)
+    in_1, first_x, around = together(in_1, first_x, around)
     x_3 = send(first_x, (3, 2))
-    in_1 = send(last_y, (0, 1))
-    joined = jnp.where(
-        domain == 1,
-        last_y + mm(last_t, in_1),
-        first_x + mm(first_s, x_3 + mm(w_3, last_y)),
+    base = first_x + mm(first_s, mm(w_3, last_y))
+    x_3, base = together(x_3, base)
+    joined = jnp.where(domain == 1, last_y + mm(last_t, in_1), base + mm(first_s, x_3))
+    swapped = send(joined, (1, 2), (2, 1))
+    past = mm(around, joined)
+    base = jnp.where(
+        domain == 1, first_x + mm(first_w, in_1) + mm(first_s, past), last_y
     )
-    swapped = send(joined, (1, 2), (2, 1))
-    own = swapped + mm(around, joined)
-    out_2 = last_y + mm(last_t, swapped)
-    crossing = jnp.where(
-        domain == 1, first_x + mm(first_w, in_1) + mm(first_s, own), out_2
-    )
+    across = jnp.where(domain == 1, first_s, last_t)
+    swapped, base, across, past = together(swapped, base, across, past)
+    crossing = base + mm(across, swapped)
     ended = send(crossing, (1, 0), (2, 3))
-    out_2, _ = together(out_2, crossing)
-    beyond = x_3 + mm(w_3, out_2)
+    beyond = x_3 + mm(w_3, crossing)
 
     weight = weights / (k * energies)
-    terms = charge(places, weight, energies, x, high, low, probes, in_1, swapped, own, beyond, ended)
+    terms = charge(places, weight, energies, x, high, low, probes, in_1, swapped, swapped + past, beyond, ended)
     if energies == 8:
         half = energies // 2
         total = terms[:half] + near(terms[half:], (1,))[0]

time: 118 us -> 103 us (0.87)
  matrix products: 13.3 us -> 6.87 us
  local copies, waits for them, and re-layouts: 4.38 us -> 0.84 us
  starting transfers between devices: 24.6 us -> 22.1 us
  other arithmetic: 2.78 us -> 0.96 us
    dot_general x17, matrix products: 13.3 us -> 6.87 us  [mm(): return jnp.dot(a, b, precision=HIGH)]
    ppermute x11, waiting for transfers between devices: 23.5 us -> 27.1 us  [send(): return lax.ppermute(x, 'dom', list(pairs))]
    ppermute x11, waiting for transfers between devices: 8.15 us -> 4.81 us  [near(): lax.ppermute(x, 'energy', [(i, i ^ way) for i in range(peers)])]
    unnamed x38 -> x18, local copies, waits for them, and re-layouts: 3.31 us -> 0.83 us
    ppermute x11, starting transfers between devices: 15.5 us -> 13.3 us  [send(): return lax.ppermute(x, 'dom', list(pairs))]
    add x2, other arithmetic: 1.92 us -> 0.05 us  [the longest x1 0.02 us: per_device(): crossing = base + mm(across, swapped)]
  transfers between devices with their start and end apart: 22 -> 22, of which waited for: 11 -> 8; matrix products, arithmetic and copies ran while one was open for 8% -> 5% of each run, Pallas kernels for 31% -> 35%
where the time goes in v3:
time: 103 us; the launch traced here: 102 us
  Pallas kernels  38.7 us (38%)
  waiting for transfers between devices  31.9 us (31%)
  starting transfers between devices  22.1 us (21%)
  matrix products  6.87 us (7%)
  between operations  1.13 us (1%)
    ppermute x11, waiting for transfers between devices, send(): return lax.ppermute(x, 'dom', list(pairs))  27.1 us
    pallas_call x1, Pallas kernels, local_maps(): pl.pallas_call(local_kernel, in_specs=[HBM] * 4, out_specs=[HBM] * 3 + [V...  14.6 us
    ppermute x11, starting transfers between devices, send(): return lax.ppermute(x, 'dom', list(pairs))  13.3 us
    pallas_call x1, Pallas kernels, second_ahead(): pl.pallas_call(second_ahead_kernel, in_specs=[HBM] * 2 + [VMEM] * (5 + le...  10.3 us
    ppermute x11, starting transfers between devices, near(): lax.ppermute(x, 'energy', [(i, i ^ way) for i in range(peers)])  8.79 us
    pallas_call x1, Pallas kernels, drive(): pl.pallas_call(drive_kernel, grid=(n,), in_specs=[SMEM, SMEM, pl.BlockSpe...  8.14 us
    dot_general x17, matrix products, mm(): return jnp.dot(a, b, precision=HIGH)  6.87 us
    ppermute x11, waiting for transfers between devices, near(): lax.ppermute(x, 'energy', [(i, i ^ way) for i in range(peers)])  4.81 us
  transfers between devices with their start and end apart: 22, of which 8 were waited for; matrix products, arithmetic and copies ran while one was open for 5% of the time, Pallas kernels for 35%

profile of v3, /device:TPU:0, one launch (start us, length us, event | category | flops | bytes accessed | tf_op | source)
XLA Modules:
  0.0 102.5 jit_solution(10810765511695521582)
XLA Ops:
  0.0 2.9 %collective-permute-start.1 = (f32[8,40,320]{2,1,0:T(8,128)}, f32[8,40,320]{2,1,0:T(8,128)}, u32[]{:S(2)}, u32[]{:S(2)}) collective-permute-start(f32[8,40,320]{2,1,0:T(8,128)} %rest_0_.1), channel_id=1, source_target_pairs={{0,8},{4,12},{8,0},{12,4},{16,24},{20,28},{24,16},{28,20},{1,9},{5... | collective-permute-start | bytes 1228808 | tf_op jit(solution)/shard_map/ppermute | solution.py:408
  2.9 1.5 %collective-permute-start.2 = (f32[8,40,320]{2,1,0:T(8,128)}, f32[8,40,320]{2,1,0:T(8,128)}, u32[]{:S(2)}, u32[]{:S(2)}) collective-permute-start(f32[8,40,320]{2,1,0:T(8,128)} %rest_0_.1), channel_id=1, source_target_pairs={{0,16},{4,20},{8,24},{12,28},{16,0},{20,4},{24,8},{28,12},{1,17},{... | collective-permute-start | bytes 1228808 | tf_op jit(solution)/shard_map/ppermute | solution.py:408
  4.5 14.6 %local_maps.1 = (f32[8,320,128]{2,1,0:T(8,128)}, bf16[8,320,768]{2,1,0:T(8,128)(2,1)}, bf16[8,320,768]{2,1,0:T(8,128)(2,1)}, f32[320,128]{1,0:T(8,128)S(1)}, f32...) custom-call(f32[8,320,320]{2,1,0:T(8,128)} %bitcast.48, ...), custom_call_target="tpu_custom_call" | custom-call | flops 15000000512 | tf_op jit(solution)/shard_map/local_maps/pallas_call | solution.py:191
  19.1 4.0 %collective-permute-start = (f32[320,128]{1,0:T(8,128)S(1)}, f32[320,128]{1,0:T(8,128)S(1)}, u32[]{:S(2)}, u32[]{:S(2)}) collective-permute-start(f32[320,128]{1,0:T(8,128)S(1)} %get-tuple-element.42), channel_id=1, source_target_pairs={{0,1},{4,5},{8,9},{12,13},{16,17},{20,21},{24,25},{28,29}} | collective-permute-start | bytes 491528 | tf_op jit(solution)/shard_map/ppermute | solution.py:403
  23.2 2.7 %collective-permute-done.in_1 = f32[320,128]{1,0:T(8,128)S(1)} collective-permute-done((f32[320,128]{1,0:T(8,128)S(1)}, f32[320,128]{1,0:T(8,128)S(1)}, u32[]{:S(2)}, u32[]{:S(2)}) %collective-permute-start) | collective-permute-done | bytes 163872 | tf_op jit(solution)/shard_map/ppermute | solution.py:403
  25.9 0.7 collective-permute-start.5
  26.7 0.5 collective-permute-start.8
  27.3 1.0 convolution_add_fusion.9
  28.3 0.8 copy-done.6
  29.1 0.7 collective-permute-start.4
  30.0 0.3 collective-permute-done.9.rest_7_
  30.3 8.1 %drive_maps.1.driver = bf16[8,320,640]{2,1,0:T(8,128)(2,1)S(1)} custom-call(s32[1]{0:T(128)} %bitcast.1.me, f32[8]{0:T(128)S(1)} %select_reduce_fusion.scale, f32[8,320,320]{2,1,0:T(8,128)} %bitcast.49, f32[8,40,320]{2,1,0:T(8,128)} %rest_0_.1, f32[8,40,320]{2,1,0:T(8,128)} %copy-done.6, f32[8,40,320]{2,1,0:T(8,128)} %collective-permute-done.1.rest_2_, ...), custom_call_target="tpu_custom_call" | custom-call | flops 10000000 | tf_op jit(solution)/shard_map/drive_maps/pallas_call | solution.py:248
  38.5 0.3 convolution_add_fusion.8
  38.8 0.3 slice_add_fusion.out_2
  39.2 0.3 convolution_add_fusion.7
  39.5 0.3 convolution_add_fusion.6
  39.9 0.8 collective-permute-start.11
  40.7 0.6 fusion.8
  41.3 0.8 collective-permute-start.10
  42.1 0.6 convolution_add_fusion
  42.7 0.3 convolution_add_fusion.5
  43.1 1.3 %collective-permute-start.12 = (f32[320,128]{1,0:T(8,128)S(1)}, f32[320,128]{1,0:T(8,128)S(1)}, u32[]{:S(2)}, u32[]{:S(2)}) collective-permute-start(f32[320,128]{1,0:T(8,128)S(1)} %convolution_add_fusion.5), channel_id=1, source_target_pairs={{1,0},{5,4},{9,8},{13,12},{17,16},{21,20},{25,24},{29,28}} | collective-permute-start | bytes 491528 | tf_op jit(solution)/shard_map/ppermute | solution.py:403
  45.1 0.7 collective-permute-start.14
  45.8 11.7 %collective-permute-done.12.out_0 = f32[320,128]{1,0:T(8,128)S(1)} collective-permute-done((f32[320,128]{1,0:T(8,128)S(1)}, f32[320,128]{1,0:T(8,128)S(1)}, u32[]{:S(2)}, u32[]{:S(2)}) %collective-permute-start.12) | collective-permute-done | bytes 163872 | tf_op jit(solution)/shard_map/ppermute | solution.py:403
  57.6 10.3 %second_ahead.1 = (f32[8,320,128]{2,1,0:T(8,128)S(1)}, f32[320,128]{1,0:T(8,128)S(1)}, bf16[8,320,640]{2,1,0:T(8,128)(2,1)S(1)}) custom-call(f32[8,320,320]{2,1,0:T(8,128)} %bitcast.51, f32[8,320,320]{2,1,0:T(8,128)} %bitcast.53, f32[8,320,128]{2,1,0:T(8,128)S(1)} %copy-done.4, bf16[8,320,768]{2,1,0:T(8,128)(2,1)S(1)} %copy-done, ...), custom_call_target="tpu_custom_call" | custom-call | flops 8999999488 | tf_op jit(solution)/shard_map/second_ahead/pallas_call | solution.py:309
  67.9 1.5 %collective-permute-start.13 = (f32[320,128]{1,0:T(8,128)S(1)}, f32[320,128]{1,0:T(8,128)S(1)}, u32[]{:S(2)}, u32[]{:S(2)}) collective-permute-start(f32[320,128]{1,0:T(8,128)S(1)} %get-tuple-element.61), channel_id=1, source_target_pairs={{0,1},{4,5},{8,9},{12,13},{16,17},{20,21},{24,25},{28,29}} | collective-permute-start | bytes 491528 | tf_op jit(solution)/shard_map/ppermute | solution.py:403
  69.4 2.9 %second_back.1 = (f32[8,320,128]{2,1,0:T(8,128)}, f32[320,128]{1,0:T(8,128)S(1)}) custom-call(f32[8,320,128]{2,1,0:T(8,128)S(1)} %get-tuple-element.58.y, bf16[8,320,640]{2,1,0:T(8,128)(2,1)S(1)} %get-tuple-element.59.left_u), custom_call_target="tpu_custom_call" | custom-call | flops 4000000000 | tf_op jit(solution)/shard_map/second_back/pallas_call | solution.py:351
  72.3 0.3 fusion.6
  72.6 0.9 collective-permute-start.15
  73.5 0.3 convolution_add_fusion.3
  73.8 0.3 fusion.14
  74.2 0.3 fusion.1
  74.5 0.8 collective-permute-start.16
  75.3 0.3 fusion.15
  75.7 0.3 fusion.16
  76.0 0.3 fusion.2
  76.4 0.3 fusion.17
  76.8 1.3 %collective-permute-start.17 = (f32[320,128]{1,0:T(8,128)S(1)}, f32[320,128]{1,0:T(8,128)S(1)}, u32[]{:S(2)}, u32[]{:S(2)}) collective-permute-start(f32[320,128]{1,0:T(8,128)S(1)} %add.74), channel_id=1, source_target_pairs={{1,0},{2,3},{5,4},{6,7},{9,8},{10,11},{13,12},{14,15},{17,16},{18,... | collective-permute-start | bytes 491528 | tf_op jit(solution)/shard_map/ppermute | solution.py:403
  78.1 0.3 convolution_add_fusion.1.out_2
  78.4 12.6 %collective-permute-done.17.ended = f32[320,128]{1,0:T(8,128)S(1)} collective-permute-done((f32[320,128]{1,0:T(8,128)S(1)}, f32[320,128]{1,0:T(8,128)S(1)}, u32[]{:S(2)}, u32[]{:S(2)}) %collective-permute-start.17) | collective-permute-done | bytes 163872 | tf_op jit(solution)/shard_map/ppermute | solution.py:403
  91.1 2.7 %charge_terms.1 = f32[8,8,40]{2,1,0:T(8,128)S(1)} custom-call(s32[2]{0:T(128)S(1)} %pad_add_fusion.places, f32[1]{0:T(128)S(6)} %div.3.weight, f32[8,320,128]{2,1,0:T(8,128)S(1)} %copy-done.3, bf16[8,320,768]{2,1,0:T(8,128)(2,1)S(1)} %copy-done, bf16[8,320,768]{2,1,0:T(8,128)(2,1)S(1)} %copy-done.1, f32[8,320,128]{2,1,0:T(8,128)S(1)} %copy-done.2, ...), custom_call_target="tpu_custom_call" | custom-call | tf_op jit(solution)/shard_map/charge_terms/pallas_call | solution.py:387
  93.8 1.2 %collective-permute-done.18 = f32[4,8,40]{2,1,0:T(8,128)S(1)} collective-permute-done((f32[4,8,40]{2,1,0:T(8,128)S(1)}, f32[4,8,40]{2,1,0:T(8,128)S(1)}, u32[]{:S(2)}, u32[]{:S(2)}) %collective-permute-start.18) | collective-permute-done | bytes 5152 | tf_op jit(solution)/shard_map/ppermute | solution.py:408
  95.0 1.3 %collective-permute-start.19 = (f32[8,40]{1,0:T(8,128)S(1)}, f32[8,40]{1,0:T(8,128)S(1)}, u32[]{:S(2)}, u32[]{:S(2)}) collective-permute-start(f32[8,40]{1,0:T(8,128)S(1)} %get-tuple-element.73), channel_id=1, source_target_pairs={{0,8},{4,12},{8,0},{12,4},{16,24},{20,28},{24,16},{28,20},{1,9},{5... | collective-permute-start | bytes 3848 | tf_op jit(solution)/shard_map/ppermute | solution.py:408
  96.3 1.0 %collective-permute-start.20 = (f32[8,40]{1,0:T(8,128)S(1)}, f32[8,40]{1,0:T(8,128)S(1)}, u32[]{:S(2)}, u32[]{:S(2)}) collective-permute-start(f32[8,40]{1,0:T(8,128)S(1)} %get-tuple-element.75), channel_id=1, source_target_pairs={{0,16},{4,20},{8,24},{12,28},{16,0},{20,4},{24,8},{28,12},{1,17},{... | collective-permute-start | bytes 3848 | tf_op jit(solution)/shard_map/ppermute | solution.py:408
  97.4 1.2 %collective-permute-start.21 = (f32[8,40]{1,0:T(8,128)S(1)}, f32[8,40]{1,0:T(8,128)S(1)}, u32[]{:S(2)}, u32[]{:S(2)}) collective-permute-start(f32[8,40]{1,0:T(8,128)S(1)} %get-tuple-element.74), channel_id=1, source_target_pairs={{0,24},{4,28},{8,16},{12,20},{16,8},{20,12},{24,0},{28,4},{1,25},{... | collective-permute-start | bytes 3848 | tf_op jit(solution)/shard_map/ppermute | solution.py:408
  98.7 1.2 %collective-permute-done.20 = f32[8,40]{1,0:T(8,128)S(1)} collective-permute-done((f32[8,40]{1,0:T(8,128)S(1)}, f32[8,40]{1,0:T(8,128)S(1)}, u32[]{:S(2)}, u32[]{:S(2)}) %collective-permute-start.20) | collective-permute-done | bytes 1312 | tf_op jit(solution)/shard_map/ppermute | solution.py:408
  99.9 1.9 %collective-permute-done.21 = f32[8,40]{1,0:T(8,128)S(1)} collective-permute-done((f32[8,40]{1,0:T(8,128)S(1)}, f32[8,40]{1,0:T(8,128)S(1)}, u32[]{:S(2)}, u32[]{:S(2)}) %collective-permute-start.21) | collective-permute-done | bytes 1312 | tf_op jit(solution)/shard_map/ppermute | solution.py:408
  101.9 0.6 fusion.13
  (45 shorter events, 0.9 us)
Async XLA Ops:
  0.0 26.6 %collective-permute-start.1 = (f32[8,40,320]{2,1,0:T(8,128)}, f32[8,40,320]{2,1,0:T(8,128)}, u32[]{:S(2)}, u32[]{:S(2)}) collective-permute-start(f32[8,40,320]{2,1,0:T(8,128)} %rest_0_.1), channel_id=1, source_target_pairs={{0,8},{4,12},{8,0},{12,4},{16,24},{20,28},{24,16},{28,20},{1,9},{5... | collective-permute-start | bytes 1228808 | tf_op jit(solution)/shard_map/ppermute | solution.py:408
  2.9 23.7 %collective-permute-start.2 = (f32[8,40,320]{2,1,0:T(8,128)}, f32[8,40,320]{2,1,0:T(8,128)}, u32[]{:S(2)}, u32[]{:S(2)}) collective-permute-start(f32[8,40,320]{2,1,0:T(8,128)} %rest_0_.1), channel_id=1, source_target_pairs={{0,16},{4,20},{8,24},{12,28},{16,0},{20,4},{24,8},{28,12},{1,17},{... | collective-permute-start | bytes 1228808 | tf_op jit(solution)/shard_map/ppermute | solution.py:408
  4.5 22.2 %collective-permute-start.3 = (f32[8,40,320]{2,1,0:T(8,128)}, f32[8,40,320]{2,1,0:T(8,128)}, u32[]{:S(2)}, u32[]{:S(2)}) collective-permute-start(f32[8,40,320]{2,1,0:T(8,128)} %rest_0_.1), channel_id=1, source_target_pairs={{0,24},{4,28},{8,16},{12,20},{16,8},{20,12},{24,0},{28,4},{1,25},{... | collective-permute-start | bytes 1228808 | tf_op jit(solution)/shard_map/ppermute | solution.py:408
  4.5 18.6 %copy-start.5 = (f32[8,40,320]{2,1,0:T(8,128)S(1)}, f32[8,40,320]{2,1,0:T(8,128)}, u32[]{:S(2)}) copy-start(f32[8,40,320]{2,1,0:T(8,128)} %rest_0_.1) | copy-start | bytes 1228804
  4.5 25.3 %copy-start.7 = (f32[32]{0:T(128)S(1)}, f32[32]{0:T(128)}, u32[]{:S(2)}) copy-start(f32[32]{0:T(128)} %param.13) | copy-start | bytes 388
  4.5 25.3 %copy-start.8 = (s32[8]{0:T(128)S(1)}, s32[8]{0:T(128)}, u32[]{:S(2)}) copy-start(s32[8]{0:T(128)} %param.12) | copy-start | bytes 100
  19.1 6.8 %collective-permute-start = (f32[320,128]{1,0:T(8,128)S(1)}, f32[320,128]{1,0:T(8,128)S(1)}, u32[]{:S(2)}, u32[]{:S(2)}) collective-permute-start(f32[320,128]{1,0:T(8,128)S(1)} %get-tuple-element.42), channel_id=1, source_target_pairs={{0,1},{4,5},{8,9},{12,13},{16,17},{20,21},{24,25},{28,29}} | collective-permute-start | bytes 491528 | tf_op jit(solution)/shard_map/ppermute | solution.py:403
  23.1 5.2 %collective-permute-start.6 = (f32[8,40,320]{2,1,0:T(8,128)S(1)}, f32[8,40,320]{2,1,0:T(8,128)S(1)}, u32[]{:S(2)}, u32[]{:S(2)}) collective-permute-start(f32[8,40,320]{2,1,0:T(8,128)S(1)} %copy-done.5), channel_id=1, source_target_pairs={{0,4},{4,0},{8,12},{12,8},{16,20},{20,16},{24,28},{28,24},{1,5},{5... | collective-permute-start | bytes 1228808 | tf_op jit(solution)/shard_map/ppermute | solution.py:408
  25.9 12.6 %collective-permute-start.5 = (f32[320,448]{1,0:T(8,128)S(1)}, f32[320,448]{1,0:T(8,128)S(1)}, u32[]{:S(2)}, u32[]{:S(2)}) collective-permute-start(f32[320,448]{1,0:T(8,128)S(1)} %get-tuple-element.45), channel_id=1, source_target_pairs={{3,2},{7,6},{11,10},{15,14},{19,18},{23,22},{27,26},{31,30}} | collective-permute-start | bytes 1720328 | tf_op jit(solution)/shard_map/ppermute | solution.py:403
  26.6 3.3 %collective-permute-start.7 = (f32[8,40,320]{2,1,0:T(8,128)}, f32[8,40,320]{2,1,0:T(8,128)}, u32[]{:S(2)}, u32[]{:S(2)}) collective-permute-start(f32[8,40,320]{2,1,0:T(8,128)} %collective-permute-done.1.rest_2_), channel_id=1, source_target_pairs={{0,4},{4,0},{8,12},{12,8},{16,20},{20,16},{24,28},{28,24},{1,5},{5... | collective-permute-start | bytes 1228808 | tf_op jit(solution)/shard_map/ppermute | solution.py:408
  26.7 3.3 %collective-permute-start.8 = (f32[8,40,320]{2,1,0:T(8,128)}, f32[8,40,320]{2,1,0:T(8,128)}, u32[]{:S(2)}, u32[]{:S(2)}) collective-permute-start(f32[8,40,320]{2,1,0:T(8,128)} %collective-permute-done.2.rest_4_), channel_id=1, source_target_pairs={{0,4},{4,0},{8,12},{12,8},{16,20},{20,16},{24,28},{28,24},{1,5},{5... | collective-permute-start | bytes 1228808 | tf_op jit(solution)/shard_map/ppermute | solution.py:408
  27.2 3.1 %collective-permute-start.9 = (f32[8,40,320]{2,1,0:T(8,128)}, f32[8,40,320]{2,1,0:T(8,128)}, u32[]{:S(2)}, u32[]{:S(2)}) collective-permute-start(f32[8,40,320]{2,1,0:T(8,128)} %collective-permute-done.3.rest_6_), channel_id=1, source_target_pairs={{0,4},{4,0},{8,12},{12,8},{16,20},{20,16},{24,28},{28,24},{1,5},{5... | collective-permute-start | bytes 1228808 | tf_op jit(solution)/shard_map/ppermute | solution.py:408
  28.3 0.8 copy-start.6
  29.1 9.4 %collective-permute-start.4 = (f32[320,128]{1,0:T(8,128)}, f32[320,128]{1,0:T(8,128)S(1)}, u32[]{:S(2)}, u32[]{:S(2)}) collective-permute-start(f32[320,128]{1,0:T(8,128)} %convolution_add_fusion.9), channel_id=1, source_target_pairs={{1,2},{5,6},{9,10},{13,14},{17,18},{21,22},{25,26},{29,30}} | collective-permute-start | bytes 491528 | tf_op jit(solution)/shard_map/ppermute | solution.py:403
  30.3 27.3 %copy-start.4 = (f32[8,320,128]{2,1,0:T(8,128)S(1)}, f32[8,320,128]{2,1,0:T(8,128)}, u32[]{:S(2)}) copy-start(f32[8,320,128]{2,1,0:T(8,128)} %get-tuple-element.39.x) | copy-start | bytes 3932164
  38.5 19.1 %copy-start.2 = (f32[8,320,128]{2,1,0:T(8,128)S(1)}, f32[8,320,128]{2,1,0:T(8,128)}, u32[]{:S(2)}) copy-start(f32[8,320,128]{2,1,0:T(8,128)} %probe.3) | copy-start | bytes 3932164
  39.2 18.4 %copy-start.1 = (bf16[8,320,768]{2,1,0:T(8,128)(2,1)S(1)}, bf16[8,320,768]{2,1,0:T(8,128)(2,1)}, u32[]{:S(2)}) copy-start(bf16[8,320,768]{2,1,0:T(8,128)(2,1)} %get-tuple-element.41.low) | copy-start | bytes 11796484
  39.5 18.0 %copy-start = (bf16[8,320,768]{2,1,0:T(8,128)(2,1)S(1)}, bf16[8,320,768]{2,1,0:T(8,128)(2,1)}, u32[]{:S(2)}) copy-start(bf16[8,320,768]{2,1,0:T(8,128)(2,1)} %get-tuple-element.40.high) | copy-start | bytes 11796484
  39.9 2.8 %collective-permute-start.11 = (f32[320,128]{1,0:T(8,128)S(1)}, f32[320,128]{1,0:T(8,128)S(1)}, u32[]{:S(2)}, u32[]{:S(2)}) collective-permute-start(f32[320,128]{1,0:T(8,128)S(1)} %convolution_add_fusion.6), channel_id=1, source_target_pairs={{2,1},{6,5},{10,9},{14,13},{18,17},{22,21},{26,25},{30,29}} | collective-permute-start | bytes 491528 | tf_op jit(solution)/shard_map/ppermute | solution.py:403
  41.3 4.6 %collective-permute-start.10 = (f32[320,128]{1,0:T(8,128)S(1)}, f32[320,128]{1,0:T(8,128)S(1)}, u32[]{:S(2)}, u32[]{:S(2)}) collective-permute-start(f32[320,128]{1,0:T(8,128)S(1)} %convolution_add_fusion.8), channel_id=1, source_target_pairs={{2,3},{6,7},{10,11},{14,15},{18,19},{22,23},{26,27},{30,31}} | collective-permute-start | bytes 491528 | tf_op jit(solution)/shard_map/ppermute | solution.py:403
  43.1 14.5 %collective-permute-start.12 = (f32[320,128]{1,0:T(8,128)S(1)}, f32[320,128]{1,0:T(8,128)S(1)}, u32[]{:S(2)}, u32[]{:S(2)}) collective-permute-start(f32[320,128]{1,0:T(8,128)S(1)} %convolution_add_fusion.5), channel_id=1, source_target_pairs={{1,0},{5,4},{9,8},{13,12},{17,16},{21,20},{25,24},{29,28}} | collective-permute-start | bytes 491528 | tf_op jit(solution)/shard_map/ppermute | solution.py:403
  45.1 27.5 %collective-permute-start.14 = (f32[320,320]{1,0:T(8,128)S(1)}, f32[320,320]{1,0:T(8,128)S(1)}, u32[]{:S(2)}, u32[]{:S(2)}) collective-permute-start(f32[320,320]{1,0:T(8,128)S(1)} %convolution_add_fusion), channel_id=1, source_target_pairs={{2,1},{6,5},{10,9},{14,13},{18,17},{22,21},{26,25},{30,29}} | collective-permute-start | bytes 1228808 | tf_op jit(solution)/shard_map/ppermute | solution.py:403
  67.9 4.7 %collective-permute-start.13 = (f32[320,128]{1,0:T(8,128)S(1)}, f32[320,128]{1,0:T(8,128)S(1)}, u32[]{:S(2)}, u32[]{:S(2)}) collective-permute-start(f32[320,128]{1,0:T(8,128)S(1)} %get-tuple-element.61), channel_id=1, source_target_pairs={{0,1},{4,5},{8,9},{12,13},{16,17},{20,21},{24,25},{28,29}} | collective-permute-start | bytes 491528 | tf_op jit(solution)/shard_map/ppermute | solution.py:403
  72.6 1.2 %collective-permute-start.15 = (f32[320,128]{1,0:T(8,128)S(1)}, f32[320,128]{1,0:T(8,128)S(1)}, u32[]{:S(2)}, u32[]{:S(2)}) collective-permute-start(f32[320,128]{1,0:T(8,128)S(1)} %get-tuple-element.65), channel_id=1, source_target_pairs={{3,2},{7,6},{11,10},{15,14},{19,18},{23,22},{27,26},{31,30}} | collective-permute-start | bytes 491528 | tf_op jit(solution)/shard_map/ppermute | solution.py:403
  74.2 16.9 %copy-start.3 = (f32[8,320,128]{2,1,0:T(8,128)S(1)}, f32[8,320,128]{2,1,0:T(8,128)}, u32[]{:S(2)}) copy-start(f32[8,320,128]{2,1,0:T(8,128)} %get-tuple-element.60.x) | copy-start | bytes 3932164
  74.5 1.8 %collective-permute-start.16 = (f32[320,128]{1,0:T(8,128)S(1)}, f32[320,128]{1,0:T(8,128)S(1)}, u32[]{:S(2)}, u32[]{:S(2)}) collective-permute-start(f32[320,128]{1,0:T(8,128)S(1)} %fusion.1), channel_id=1, source_target_pairs={{1,2},{2,1},{5,6},{6,5},{9,10},{10,9},{13,14},{14,13},{17,18},{18,... | collective-permute-start | bytes 491528 | tf_op jit(solution)/shard_map/ppermute | solution.py:403
  76.8 14.3 %collective-permute-start.17 = (f32[320,128]{1,0:T(8,128)S(1)}, f32[320,128]{1,0:T(8,128)S(1)}, u32[]{:S(2)}, u32[]{:S(2)}) collective-permute-start(f32[320,128]{1,0:T(8,128)S(1)} %add.74), channel_id=1, source_target_pairs={{1,0},{2,3},{5,4},{6,7},{9,8},{10,11},{13,12},{14,15},{17,16},{18,... | collective-permute-start | bytes 491528 | tf_op jit(solution)/shard_map/ppermute | solution.py:403
  93.8 1.2 %collective-permute-start.18 = (f32[4,8,40]{2,1,0:T(8,128)S(1)}, f32[4,8,40]{2,1,0:T(8,128)S(1)}, u32[]{:S(2)}, u32[]{:S(2)}) collective-permute-start(f32[4,8,40]{2,1,0:T(8,128)S(1)} %slice.37), channel_id=1, source_target_pairs={{0,4},{4,0},{8,12},{12,8},{16,20},{20,16},{24,28},{28,24},{1,5},{5... | collective-permute-start | bytes 15368 | tf_op jit(solution)/shard_map/ppermute | solution.py:408
  95.0 3.7 %collective-permute-start.19 = (f32[8,40]{1,0:T(8,128)S(1)}, f32[8,40]{1,0:T(8,128)S(1)}, u32[]{:S(2)}, u32[]{:S(2)}) collective-permute-start(f32[8,40]{1,0:T(8,128)S(1)} %get-tuple-element.73), channel_id=1, source_target_pairs={{0,8},{4,12},{8,0},{12,4},{16,24},{20,28},{24,16},{28,20},{1,9},{5... | collective-permute-start | bytes 3848 | tf_op jit(solution)/shard_map/ppermute | solution.py:408
  96.3 3.6 %collective-permute-start.20 = (f32[8,40]{1,0:T(8,128)S(1)}, f32[8,40]{1,0:T(8,128)S(1)}, u32[]{:S(2)}, u32[]{:S(2)}) collective-permute-start(f32[8,40]{1,0:T(8,128)S(1)} %get-tuple-element.75), channel_id=1, source_target_pairs={{0,16},{4,20},{8,24},{12,28},{16,0},{20,4},{24,8},{28,12},{1,17},{... | collective-permute-start | bytes 3848 | tf_op jit(solution)/shard_map/ppermute | solution.py:408
  97.4 4.5 %collective-permute-start.21 = (f32[8,40]{1,0:T(8,128)S(1)}, f32[8,40]{1,0:T(8,128)S(1)}, u32[]{:S(2)}, u32[]{:S(2)}) collective-permute-start(f32[8,40]{1,0:T(8,128)S(1)} %get-tuple-element.74), channel_id=1, source_target_pairs={{0,24},{4,28},{8,16},{12,20},{16,8},{20,12},{24,0},{28,4},{1,25},{... | collective-permute-start | bytes 3848 | tf_op jit(solution)/shard_map/ppermute | solution.py:408

commit v4 on v3

--- a/solution.py
+++ b/solution.py
@@ -1,3 +1,5 @@
+import functools
+
 import jax
 import jax.numpy as jnp
 from jax import lax
@@ -227,7 +229,7 @@
     )(*in_hbm(pivots, lower, upper, probes))
 
 
-def drive_kernel(me, scale, pivot, *rest):
+def drive_kernel(start, me, scale, pivot, *rest):
     pieces, out, gathered = rest[:-2], rest[-2], rest[-1]
     step = pl.program_id(0)
     if len(pieces) > 1:
@@ -238,20 +240,20 @@
         potential = gathered[...]
     else:
         potential = pieces[0][0]
-    out[step] = left_two(apply_three(left_three(pivot[0]), *halves(potential * scale[step])))
-
-
-def drive(me, scale, pivots, pieces):
-    n, b, _ = pivots.shape
+    out[step] = left_two(apply_three(left_three(pivot[0]), *halves(potential * scale[step + start])))
+
+
+def drive(start, stop, me, scale, pivots, pieces):
+    b = pivots.shape[1]
     rows = pieces[0].shape[1]
-    at = lambda i: (i, 0, 0)
+    at = lambda i: (i + start, 0, 0)
     return pl.pallas_call(
-        drive_kernel,
-        grid=(n,),
+        functools.partial(drive_kernel, start),
+        grid=(stop - start,),
         in_specs=[SMEM, SMEM, pl.BlockSpec((1, b, b), at)]
         + [pl.BlockSpec((1, rows, b), at)] * len(pieces),
         out_specs=VMEM,
-        out_shape=pltpu.VMEM((n, b, 2 * b), BF16),
+        out_shape=pltpu.VMEM((stop - start, b, 2 * b), BF16),
         scratch_shapes=[pltpu.VMEM((b, b), F32)],
         compiler_params=params(10),
         cost_estimate=cost(0.01),
@@ -259,19 +261,20 @@
     )(me, scale, *in_hbm(pivots, *pieces))
 
 
-def apply_maps(high, low, i, flows):
-    k = flows.shape[1] // 2
+def add_flows(x, high, low, i, flows):
+    n, b, k = x.shape
     skip = high.shape[2] - flows.shape[0]
-    maps = jnp.concatenate([high[i, :, skip:], low[i, :, skip:]], axis=1)
-    out = dot(maps, jnp.concatenate([flows, flows], axis=0))
-    return out[:, :k] + out[:, k:]
-
-
-def second_ahead_kernel(
-    lower, upper, x, high, low, driver, probes, in_1, in_2, in_3, out_0, out_1, out_2,
-    y, last, left_u, l, u, left_l, out, sem,
+    rows = lambda ref: ref[pl.ds(i, 2), :, skip:].reshape(2 * b, flows.shape[0])
+    out = dot(rows(high), flows) + dot(rows(low), flows)
+    out = out[:, :k] + out[:, k:]
+    return x[i] + out[:b], x[i + 1] + out[b:]
+
+
+def sweep_ahead(
+    lower, upper, x, high, low, drive_a, drive_b, inflow, outflow, y, u, l, left_a, left_b, sem
 ):
     n, b, k = x.shape
+    lefts = (left_a, left_b)
     load_l = lambda i: pltpu.make_async_copy(lower.at[i], l.at[i], sem.at[0, i])
     load_u = lambda i: pltpu.make_async_copy(upper.at[i], u.at[i], sem.at[1, i])
 
@@ -281,83 +284,183 @@
         return c
 
     lax.fori_loop(0, n, begin, 0)
-    inflow = in_1[...] + in_2[...] + in_3[...]
-    outflow = out_0[...] + out_1[...] + out_2[...]
     flows = jnp.concatenate(halves(jnp.concatenate([inflow, outflow], axis=0)), axis=1)
-
-    def given(i, c):
+    half = drive_a.shape[0]
+    for start, driver in ((0, drive_a), (half, drive_b)):
+
+        def given(r, c):
+            j = 2 * r
+            i = j + start
+            ahead_0, ahead_1 = add_flows(x, high, low, i, flows)
+            y[i] = apply_two(driver[j], ahead_0)
+            y[i + 1] = apply_two(driver[j + 1], ahead_1)
+            return c
+
+        lax.fori_loop(0, driver.shape[0] // 2, given, 0)
+
+    def arrive(i, c):
         load_l(i).wait()
         load_u(i).wait()
-        out[i] = apply_two(driver[i], x[i] + apply_maps(high, low, i, flows))
-        left_l[i] = left_two(l[i])
-        left_u[i] = left_two(u[i])
-        return c
-
-    lax.fori_loop(0, n, given, 0)
-    y[0] = out[0]
-
-    def ahead(i, c):
-        y[i] = out[i] - apply_two(left_l[i], y[i - 1])
-        return c
-
-    lax.fori_loop(1, n, ahead, 0)
-    last[...] = y[n - 1]
-
-
-def second_ahead(lower, upper, x, high, low, driver, probes, *flows):
+        return c
+
+    lax.fori_loop(0, n, arrive, 0)
+    left_b[...] = left_two(l[1])
+
+    def step(i, slot):
+        y[i] = y[i] - apply_two(lefts[slot][...], y[i - 1])
+
+    def pair(j, c):
+        i = 2 * j + 1
+        step(i, 1)
+        left_a[...] = left_two(l[i + 1])
+        step(i + 1, 0)
+        left_b[...] = left_two(l[i + 2])
+        return c
+
+    lax.fori_loop(0, n // 2 - 1, pair, 0)
+    step(n - 1, 1)
+
+
+def sweep_back(y, u, x_out, out, left_a, left_b, sem):
+    n = y.shape[0]
+    lefts = (left_a, left_b)
+    store = lambda i: pltpu.make_async_copy(out.at[i], x_out.at[i], sem.at[i])
+    left_a[...] = left_two(u[n - 2])
+    out[n - 1] = y[n - 1]
+    store(n - 1).start()
+
+    def step(i, slot):
+        out[i] = y[i] - apply_two(lefts[slot][...], out[i + 1])
+        store(i).start()
+
+    def pair(j, c):
+        i = n - 2 - 2 * j
+        step(i, 0)
+        left_b[...] = left_two(u[i - 1])
+        step(i - 1, 1)
+        left_a[...] = left_two(u[i - 2])
+        return c
+
+    lax.fori_loop(0, n // 2 - 1, pair, 0)
+    step(0, 0)
+
+    def drain(i, c):
+        store(i).wait()
+        return c
+
+    lax.fori_loop(0, n, drain, 0)
+
+
+def second_of_3_kernel(
+    places, lower, upper, x, high, low, drive_a, drive_b, probes, in_3,
+    x_out, first, y, u, out, l, left_a, left_b, sem, sem_out,
+):
+    @pl.when(places[0] == 3)
+    def _():
+        inflow = in_3[...]
+        sweep_ahead(
+            lower, upper, x, high, low, drive_a, drive_b, inflow, jnp.zeros_like(inflow),
+            y, u, l, left_a, left_b, sem,
+        )
+        sweep_back(y, u, x_out, out, left_a, left_b, sem_out)
+        first[...] = out[0]
+
+    @pl.when(places[0] != 3)
+    def _():
+        first[...] = jnp.zeros_like(first)
+
+
+def second_of_3(places, lower, upper, x, high, low, drive_a, drive_b, probes, in_3):
+    n, b, k = x.shape
+    v = pltpu.VMEM
+    return pl.pallas_call(
+        second_of_3_kernel,
+        in_specs=[SMEM] + [HBM] * 2 + [VMEM] * 7,
+        out_specs=[HBM, VMEM],
+        out_shape=[pltpu.HBM((n, b, k), F32), pltpu.VMEM((b, k), F32)],
+        scratch_shapes=[
+            v((n, b, k), F32),
+            v((n, b, b), F32),
+            v((n, b, k), F32),
+            v((n, b, b), F32),
+            v((b, 2 * b), BF16),
+            v((b, 2 * b), BF16),
+            pltpu.SemaphoreType.DMA((2, n)),
+            pltpu.SemaphoreType.DMA((n,)),
+        ],
+        compiler_params=params(18),
+        cost_estimate=cost(0.01),
+        name="second_of_3",
+    )(places, *in_hbm(lower, upper), *in_vmem(x, high, low, drive_a, drive_b, probes), in_3)
+
+
+def second_ahead_kernel(
+    places, lower, upper, x, high, low, drive_a, drive_b, in_1, in_2, out_0, out_1, out_2,
+    y, u, last, l, left_a, left_b, sem,
+):
+    @pl.when(places[0] != 3)
+    def _():
+        inflow = in_1[...] + in_2[...]
+        outflow = out_0[...] + out_1[...] + out_2[...]
+        sweep_ahead(
+            lower, upper, x, high, low, drive_a, drive_b, inflow, outflow,
+            y, u, l, left_a, left_b, sem,
+        )
+        last[...] = y[y.shape[0] - 1]
+
+    @pl.when(places[0] == 3)
+    def _():
+        last[...] = jnp.zeros_like(last)
+
+
+def second_ahead(places, lower, upper, x, high, low, drive_a, drive_b, *flows):
     n, b, k = x.shape
     return pl.pallas_call(
         second_ahead_kernel,
-        in_specs=[HBM] * 2 + [VMEM] * (5 + len(flows)),
+        in_specs=[SMEM] + [HBM] * 2 + [VMEM] * (5 + len(flows)),
         out_specs=[VMEM] * 3,
-        out_shape=pinned(((n, b, k), F32), ((b, k), F32), ((n, b, 2 * b), BF16)),
+        out_shape=pinned(((n, b, k), F32), ((n, b, b), F32), ((b, k), F32)),
         scratch_shapes=[
             pltpu.VMEM((n, b, b), F32),
-            pltpu.VMEM((n, b, b), F32),
-            pltpu.VMEM((n, b, 2 * b), BF16),
-            pltpu.VMEM((n, b, k), F32),
+            pltpu.VMEM((b, 2 * b), BF16),
+            pltpu.VMEM((b, 2 * b), BF16),
             pltpu.SemaphoreType.DMA((2, n)),
         ],
-        compiler_params=params(18),
-        cost_estimate=cost(9),
+        compiler_params=params(12),
+        cost_estimate=cost(0.01),
         name="second_ahead",
-    )(*in_hbm(lower, upper), *in_vmem(x, high, low, driver, probes), *flows)
-
-
-def second_back_kernel(y, left_u, x_out, first, out, sem):
-    n = y.shape[0]
-    store = lambda i: pltpu.make_async_copy(out.at[i], x_out.at[i], sem.at[i])
-    out[n - 1] = y[n - 1]
-    store(n - 1).start()
-
-    def back(r, c):
-        i = n - 1 - r
-        out[i] = y[i] - apply_two(left_u[i], out[i + 1])
-        store(i).start()
-        return c
-
-    lax.fori_loop(1, n, back, 0)
-    first[...] = out[0]
-
-    def drain(i, c):
-        store(i).wait()
-        return c
-
-    lax.fori_loop(0, n, drain, 0)
-
-
-def second_back(y, left_u):
+    )(places, *in_hbm(lower, upper), *in_vmem(x, high, low, drive_a, drive_b), *flows)
+
+
+def second_back_kernel(places, y, u, x_of_3, x_out, first, out, left_a, left_b, sem):
+    @pl.when(places[0] != 3)
+    def _():
+        sweep_back(y, u, x_out, out, left_a, left_b, sem)
+        first[...] = out[0]
+
+    @pl.when(places[0] == 3)
+    def _():
+        first[...] = jnp.zeros_like(first)
+
+
+def second_back(places, y, u, x_of_3):
     n, b, k = y.shape
     return pl.pallas_call(
         second_back_kernel,
-        in_specs=[VMEM] * 2,
+        in_specs=[SMEM] + [VMEM] * 2 + [HBM],
         out_specs=[HBM, VMEM],
         out_shape=[pltpu.HBM((n, b, k), F32), pltpu.VMEM((b, k), F32)],
-        scratch_shapes=[pltpu.VMEM((n, b, k), F32), pltpu.SemaphoreType.DMA((n,))],
-        compiler_params=params(4),
-        cost_estimate=cost(4),
+        input_output_aliases={3: 0},
+        scratch_shapes=[
+            pltpu.VMEM((n, b, k), F32),
+            pltpu.VMEM((b, 2 * b), BF16),
+            pltpu.VMEM((b, 2 * b), BF16),
+            pltpu.SemaphoreType.DMA((n,)),
+        ],
+        compiler_params=params(5),
+        cost_estimate=cost(0.01),
         name="second_back",
-    )(*in_vmem(y, left_u))
+    )(places, *in_vmem(y, u), *in_hbm(x_of_3))
 
 
 def charge_kernel(places, weight, x, high, low, probe, in_1, in_2, out_1, out_2, ended, *outs):
@@ -370,9 +473,10 @@
     outflow = jnp.where(at == 0, ended[...], outflow)
     flows = jnp.concatenate(halves(jnp.concatenate([inflow, outflow], axis=0)), axis=1)
     terms = outs[-1]
-    for i in range(n):
-        value = x[i] + apply_maps(high, low, i, flows)
-        terms[i : i + 1, :] = jnp.sum((value * probe[i]).T, axis=0, keepdims=True) * weight[0]
+    for i in range(0, n, 2):
+        for j, value in enumerate(add_flows(x, high, low, i, flows)):
+            charges = jnp.sum((value * probe[i + j]).T, axis=0, keepdims=True)
+            terms[i + j : i + j + 1, :] = charges * weight[0]
     if len(outs) > 1:
         blocks = outs[0]
         owners, _, rows = blocks.shape
@@ -433,10 +537,12 @@
         pivots, lower, upper, probes
     )
 
+    if by_swaps:
+        last_y, even[0] = together(last_y, even[0])
     in_1 = send(last_y, (0, 1))
     from_3 = send(first_xw, (3, 2))
     if by_swaps:
-        in_1, *even = together(in_1, *even)
+        in_1, even[1], even[2] = together(in_1, even[1], even[2])
     out_1 = last_y + mm(last_t, in_1)
     in_2 = send(out_1, (1, 2))
     if by_swaps:
@@ -445,30 +551,35 @@
         pieces = [block for pair in zip(even, odd) for block in pair]
     else:
         pieces = [lax.all_gather(potential, "energy", axis=1, tiled=True)]
-    driver = drive(me, grain_scale, pivots, pieces)
-    in_2, from_3, driver = together(in_2, from_3, driver)
+    drive_a = drive(0, n // 2, me, grain_scale, pivots, pieces)
+    in_2, from_3, drive_a = together(in_2, from_3, drive_a)
     out_2 = last_y + mm(last_t, in_2)
     base = first_x + mm(first_w, in_1 + in_2)
     outflow_2 = from_3[:, :k] + mm(from_3[:, k:], out_2)
     turn = base + mm(first_s, outflow_2)
     outflow_1 = send(turn, (2, 1))
-    from_3, out_2, _ = together(from_3, out_2, turn)
+    from_3, out_2, scale, _ = together(from_3, out_2, grain_scale, turn)
     in_3 = send(out_2, (2, 3))
+    drive_b = drive(n // 2, n, me, scale, pivots, pieces)
     w_3 = from_3[:, k:]
     around = first_w + mm(first_s, mm(w_3, last_t))
-    outflow_1, around = together(outflow_1, around)
+    outflow_1, drive_b, around = together(outflow_1, drive_b, around)
     around = send(around, (2, 1))
     outflow_0 = send(base + mm(first_s, outflow_1), (1, 0))
 
-    ahead, last_y, left_u = second_ahead(
-        lower, upper, x, high, low, driver, probes,
-        in_1, in_2, in_3, outflow_0, outflow_1, outflow_2,
+    x_of_3, first_of_3 = second_of_3(
+        places, lower, upper, x, high, low, drive_a, drive_b, probes, in_3
     )
+    x_3 = send(first_of_3, (3, 2))
+    outflow_0, x_of_3 = together(outflow_0, x_of_3)
+    ahead, u, last_y = second_ahead(
+        places, lower, upper, x, high, low, drive_a, drive_b,
+        in_1, in_2, outflow_0, outflow_1, outflow_2,
+    )
 
     in_1 = send(last_y, (0, 1))
-    x, first_x = second_back(ahead, left_u)
+    x, first_x = second_back(places, ahead, u, x_of_3)
     in_1, first_x, around = together(in_1, first_x, around)
-    x_3 = send(first_x, (3, 2))
     base = first_x + mm(first_s, mm(w_3, last_y))
     x_3, base = together(x_3, base)
     joined = jnp.where(domain == 1, last_y + mm(last_t, in_1), base + mm(first_s, x_3))

time: 103 us -> 97.7 us (0.949)
  waiting for transfers between devices: 31.9 us -> 23.9 us
  Pallas kernels: 38.7 us -> 41.5 us
    ppermute x11, waiting for transfers between devices: 27.1 us -> 15.7 us  [send(): return lax.ppermute(x, 'dom', list(pairs))]
    ppermute x11, waiting for transfers between devices: 4.81 us -> 8.11 us  [near(): lax.ppermute(x, 'energy', [(i, i ^ way) for i in range(peers)])]
    pallas_call x3 -> x5, Pallas kernels: 21.4 us -> 23.9 us  [the longest x2 9.45 us: drive(): pl.pallas_call(functools.partial(drive_kernel, start), grid=(stop - start...]
  transfers between devices with their start and end apart: 22 -> 22, of which waited for: 8 -> 8; matrix products, arithmetic and copies ran while one was open for 5% -> 5% of each run, Pallas kernels for 35% -> 40%
where the time goes in v4:
time: 97.7 us; the launch traced here: 97.4 us
  Pallas kernels  41.5 us (42%)
  waiting for transfers between devices  23.9 us (24%)
  starting transfers between devices  22.2 us (23%)
  matrix products  6.87 us (7%)
  between operations  1.13 us (1%)
    ppermute x11, waiting for transfers between devices, send(): return lax.ppermute(x, 'dom', list(pairs))  15.7 us
    pallas_call x1, Pallas kernels, local_maps(): pl.pallas_call(local_kernel, in_specs=[HBM] * 4, out_specs=[HBM] * 3 + [V...  14.6 us
    ppermute x11, starting transfers between devices, send(): return lax.ppermute(x, 'dom', list(pairs))  13.4 us
    pallas_call x2, Pallas kernels, drive(): pl.pallas_call(functools.partial(drive_kernel, start), grid=(stop - start...  9.45 us
    pallas_call x1, Pallas kernels, second_ahead(): pl.pallas_call(second_ahead_kernel, in_specs=[SMEM] + [HBM] * 2 + [VMEM]...  9.44 us
    ppermute x11, starting transfers between devices, near(): lax.ppermute(x, 'energy', [(i, i ^ way) for i in range(peers)])  8.73 us
    ppermute x11, waiting for transfers between devices, near(): lax.ppermute(x, 'energy', [(i, i ^ way) for i in range(peers)])  8.11 us
    dot_general x17, matrix products, mm(): return jnp.dot(a, b, precision=HIGH)  6.87 us
  transfers between devices with their start and end apart: 22, of which 8 were waited for; matrix products, arithmetic and copies ran while one was open for 5% of the time, Pallas kernels for 40%

profile of v4, /device:TPU:0, one launch (start us, length us, event | category | flops | bytes accessed | tf_op | source)
XLA Modules:
  0.0 97.4 jit_solution(6870480106703200374)
XLA Ops:
  0.0 2.9 %collective-permute-start = (f32[8,40,320]{2,1,0:T(8,128)}, f32[8,40,320]{2,1,0:T(8,128)}, u32[]{:S(2)}, u32[]{:S(2)}) collective-permute-start(f32[8,40,320]{2,1,0:T(8,128)} %rest_0_.3), channel_id=1, source_target_pairs={{0,8},{4,12},{8,0},{12,4},{16,24},{20,28},{24,16},{28,20},{1,9},{5... | collective-permute-start | bytes 1228808 | tf_op jit(solution)/shard_map/ppermute | solution.py:512
  2.9 1.5 %collective-permute-start.2 = (f32[8,40,320]{2,1,0:T(8,128)}, f32[8,40,320]{2,1,0:T(8,128)}, u32[]{:S(2)}, u32[]{:S(2)}) collective-permute-start(f32[8,40,320]{2,1,0:T(8,128)} %rest_0_.3), channel_id=1, source_target_pairs={{0,16},{4,20},{8,24},{12,28},{16,0},{20,4},{24,8},{28,12},{1,17},{... | collective-permute-start | bytes 1228808 | tf_op jit(solution)/shard_map/ppermute | solution.py:512
  4.5 14.6 %local_maps.1 = (f32[8,320,128]{2,1,0:T(8,128)}, bf16[8,320,768]{2,1,0:T(8,128)(2,1)}, bf16[8,320,768]{2,1,0:T(8,128)(2,1)}, f32[320,128]{1,0:T(8,128)S(1)}, f32...) custom-call(f32[8,320,320]{2,1,0:T(8,128)} %bitcast.48, ...), custom_call_target="tpu_custom_call" | custom-call | flops 15000000512 | tf_op jit(solution)/shard_map/local_maps/pallas_call | solution.py:193
  19.1 4.0 %collective-permute-start.1 = (f32[320,128]{1,0:T(8,128)S(1)}, f32[320,128]{1,0:T(8,128)S(1)}, u32[]{:S(2)}, u32[]{:S(2)}) collective-permute-start(f32[320,128]{1,0:T(8,128)S(1)} %get-tuple-element.50), channel_id=1, source_target_pairs={{0,1},{4,5},{8,9},{12,13},{16,17},{20,21},{24,25},{28,29}} | collective-permute-start | bytes 491528 | tf_op jit(solution)/shard_map/ppermute | solution.py:507
  23.2 0.7 collective-permute-start.5
  23.9 2.6 %collective-permute-done.2.rest_4_ = f32[8,40,320]{2,1,0:T(8,128)} collective-permute-done((f32[8,40,320]{2,1,0:T(8,128)}, f32[8,40,320]{2,1,0:T(8,128)}, u32[]{:S(2)}, u32[]{:S(2)}) %collective-permute-start.2) | collective-permute-done | bytes 409632 | tf_op jit(solution)/shard_map/ppermute | solution.py:512
  26.5 0.5 collective-permute-start.8
  27.1 1.0 %convolution_add_fusion.9 = f32[320,128]{1,0:T(8,128)} fusion(f32[320,128]{1,0:T(8,128)S(1)} %get-tuple-element.50, f32[320,320]{1,0:T(8,128)S(1)} %get-tuple-element.51, f32[320,128]{1,0:T(8,128)S(1)} %collective-permute-done.1.in_1), kind=kOutput, calls=%fused_computation.11 | convolution fusion | flops 78684160 | bytes 901120 | tf_op jit(solution)/shard_map/dot_general | solution.py:503
  28.1 0.8 copy-done.6
  28.9 0.7 collective-permute-start.4
  30.1 4.4 %drive_maps.2.drive_a = bf16[4,320,640]{2,1,0:T(8,128)(2,1)S(1)} custom-call(s32[1]{0:T(128)} %bitcast.1.me, f32[8]{0:T(128)S(1)} %select_reduce_fusion.scale, f32[8,320,320]{2,1,0:T(8,128)} %bitcast.49, f32[8,40,320]{2,1,0:T(8,128)} %rest_0_.3, f32[8,40,320]{2,1,0:T(8,128)} %copy-done.6, f32[8,40,320]{2,1,0:T(8,128)} %collective-permute-done.rest_2_, ...), custom_call_target="tpu_custom_call" | custom-call | flops 10000000 | tf_op jit(solution)/shard_map/drive_maps/pallas_call | solution.py:250
  34.5 0.3 convolution_add_fusion.7
  34.8 0.3 slice_add_fusion.out_2
  35.2 0.3 convolution_add_fusion.8
  35.5 0.3 convolution_add_fusion.6
  35.9 0.7 collective-permute-start.10
  36.5 0.6 fusion.8
  37.1 0.7 collective-permute-start.12
  37.9 5.1 %drive_maps.3.drive_b = bf16[4,320,640]{2,1,0:T(8,128)(2,1)S(1)} custom-call(s32[1]{0:T(128)} %bitcast.1.me, f32[8]{0:T(128)S(1)} %select_reduce_fusion.scale, f32[8,320,320]{2,1,0:T(8,128)} %bitcast.50, f32[8,40,320]{2,1,0:T(8,128)} %rest_0_.3, f32[8,40,320]{2,1,0:T(8,128)} %copy-done.6, f32[8,40,320]{2,1,0:T(8,128)} %collective-permute-done.rest_2_, ...), custom_call_target="tpu_custom_call" | custom-call | flops 10000000 | tf_op jit(solution)/shard_map/drive_maps/pallas_call | solution.py:250
  42.9 0.6 convolution_add_fusion
  43.6 0.3 convolution_add_fusion.5
  43.9 1.4 %collective-permute-start.11 = (f32[320,128]{1,0:T(8,128)S(1)}, f32[320,128]{1,0:T(8,128)S(1)}, u32[]{:S(2)}, u32[]{:S(2)}) collective-permute-start(f32[320,128]{1,0:T(8,128)S(1)} %convolution_add_fusion.5), channel_id=1, source_target_pairs={{1,0},{5,4},{9,8},{13,12},{17,16},{21,20},{25,24},{29,28}} | collective-permute-start | bytes 491528 | tf_op jit(solution)/shard_map/ppermute | solution.py:507
  45.3 0.7 collective-permute-start.14
  46.9 1.0 second_of_3.1
  47.8 0.7 collective-permute-start.15
  48.5 6.0 %collective-permute-done.11.out_0 = f32[320,128]{1,0:T(8,128)S(1)} collective-permute-done((f32[320,128]{1,0:T(8,128)S(1)}, f32[320,128]{1,0:T(8,128)S(1)}, u32[]{:S(2)}, u32[]{:S(2)}) %collective-permute-start.11) | collective-permute-done | bytes 163872 | tf_op jit(solution)/shard_map/ppermute | solution.py:507
  54.5 9.4 %second_ahead.1 = (f32[8,320,128]{2,1,0:T(8,128)S(1)}, f32[8,320,320]{2,1,0:T(8,128)S(1)}, f32[320,128]{1,0:T(8,128)S(1)}) custom-call(s32[2]{0:T(128)S(1)} %pad_add_fusion.places, f32[8,320,320]{2,1,0:T(8,128)} %bitcast.53, f32[8,320,320]{2,1,0:T(8,128)} %bitcast.56, f32[8,320,128]{2,1,0:T(8,128)S(1)} %copy-done.2, bf16[8,320,768]{2,1,0:T(8,128)(2,1)S(1)} %copy-done, ...), custom_call_target="tpu_custom_call" | custom-call | flops 10000000 | tf_op jit(solution)/shard_map/second_ahead/pallas_call | solution.py:418
  64.0 2.0 %collective-permute-start.13 = (f32[320,128]{1,0:T(8,128)S(1)}, f32[320,128]{1,0:T(8,128)S(1)}, u32[]{:S(2)}, u32[]{:S(2)}) collective-permute-start(f32[320,128]{1,0:T(8,128)S(1)} %get-tuple-element.74), channel_id=1, source_target_pairs={{0,1},{4,5},{8,9},{12,13},{16,17},{20,21},{24,25},{28,29}} | collective-permute-start | bytes 491528 | tf_op jit(solution)/shard_map/ppermute | solution.py:507
  66.0 4.1 %second_back.1 = (f32[8,320,128]{2,1,0:T(8,128)}, f32[320,128]{1,0:T(8,128)S(1)}) custom-call(s32[2]{0:T(128)S(1)} %pad_add_fusion.places, f32[8,320,128]{2,1,0:T(8,128)S(1)} %get-tuple-element.70.y, f32[8,320,320]{2,1,0:T(8,128)S(1)} %get-tuple-element.71.u, f32[8,320,128]{2,1,0:T(8,128)} %get-tuple-element.72.x_of_3), custom_call_target="tpu_custom_call", output_to_operand_aliasing={{0}: (3, {})} | custom-call | flops 10000000 | tf_op jit(solution)/shard_map/second_back/pallas_call | solution.py:448
  70.1 0.3 fusion.6
  70.5 0.3 convolution_add_fusion.3
  70.8 0.3 fusion.14
  71.2 0.3 fusion.1
  71.5 0.7 collective-permute-start.16
  72.2 0.3 fusion.15
  72.9 0.3 fusion.2
  73.2 0.3 fusion.17
  73.6 1.3 %collective-permute-start.17 = (f32[320,128]{1,0:T(8,128)S(1)}, f32[320,128]{1,0:T(8,128)S(1)}, u32[]{:S(2)}, u32[]{:S(2)}) collective-permute-start(f32[320,128]{1,0:T(8,128)S(1)} %add.74), channel_id=1, source_target_pairs={{1,0},{2,3},{5,4},{6,7},{9,8},{10,11},{13,12},{14,15},{17,16},{18,... | collective-permute-start | bytes 491528 | tf_op jit(solution)/shard_map/ppermute | solution.py:507
  74.9 0.3 convolution_add_fusion.1.out_2
  75.3 9.7 %collective-permute-done.17.ended = f32[320,128]{1,0:T(8,128)S(1)} collective-permute-done((f32[320,128]{1,0:T(8,128)S(1)}, f32[320,128]{1,0:T(8,128)S(1)}, u32[]{:S(2)}, u32[]{:S(2)}) %collective-permute-start.17) | collective-permute-done | bytes 163872 | tf_op jit(solution)/shard_map/ppermute | solution.py:507
  84.9 3.0 %charge_terms.1 = f32[8,8,40]{2,1,0:T(8,128)S(1)} custom-call(s32[2]{0:T(128)S(1)} %pad_add_fusion.places, f32[1]{0:T(128)S(6)} %div.3.weight, f32[8,320,128]{2,1,0:T(8,128)S(1)} %copy-done.4, bf16[8,320,768]{2,1,0:T(8,128)(2,1)S(1)} %copy-done, bf16[8,320,768]{2,1,0:T(8,128)(2,1)S(1)} %copy-done.1, f32[8,320,128]{2,1,0:T(8,128)S(1)} %copy-done.3, ...), custom_call_target="tpu_custom_call" | custom-call | tf_op jit(solution)/shard_map/charge_terms/pallas_call | solution.py:491
  88.0 1.2 %collective-permute-done.18 = f32[4,8,40]{2,1,0:T(8,128)S(1)} collective-permute-done((f32[4,8,40]{2,1,0:T(8,128)S(1)}, f32[4,8,40]{2,1,0:T(8,128)S(1)}, u32[]{:S(2)}, u32[]{:S(2)}) %collective-permute-start.18) | collective-permute-done | bytes 5152 | tf_op jit(solution)/shard_map/ppermute | solution.py:512
  89.2 1.6 %collective-permute-start.19 = (f32[8,40]{1,0:T(8,128)S(1)}, f32[8,40]{1,0:T(8,128)S(1)}, u32[]{:S(2)}, u32[]{:S(2)}) collective-permute-start(f32[8,40]{1,0:T(8,128)S(1)} %get-tuple-element.87), channel_id=1, source_target_pairs={{0,8},{4,12},{8,0},{12,4},{16,24},{20,28},{24,16},{28,20},{1,9},{5... | collective-permute-start | bytes 3848 | tf_op jit(solution)/shard_map/ppermute | solution.py:512
  90.7 1.5 %collective-permute-start.20 = (f32[8,40]{1,0:T(8,128)S(1)}, f32[8,40]{1,0:T(8,128)S(1)}, u32[]{:S(2)}, u32[]{:S(2)}) collective-permute-start(f32[8,40]{1,0:T(8,128)S(1)} %get-tuple-element.89), channel_id=1, source_target_pairs={{0,16},{4,20},{8,24},{12,28},{16,0},{20,4},{24,8},{28,12},{1,17},{... | collective-permute-start | bytes 3848 | tf_op jit(solution)/shard_map/ppermute | solution.py:512
  92.3 0.5 collective-permute-start.21
  92.9 1.5 %collective-permute-done.20 = f32[8,40]{1,0:T(8,128)S(1)} collective-permute-done((f32[8,40]{1,0:T(8,128)S(1)}, f32[8,40]{1,0:T(8,128)S(1)}, u32[]{:S(2)}, u32[]{:S(2)}) %collective-permute-start.20) | collective-permute-done | bytes 1312 | tf_op jit(solution)/shard_map/ppermute | solution.py:512
  94.4 2.4 %collective-permute-done.21 = f32[8,40]{1,0:T(8,128)S(1)} collective-permute-done((f32[8,40]{1,0:T(8,128)S(1)}, f32[8,40]{1,0:T(8,128)S(1)}, u32[]{:S(2)}, u32[]{:S(2)}) %collective-permute-start.21) | collective-permute-done | bytes 1312 | tf_op jit(solution)/shard_map/ppermute | solution.py:512
  96.8 0.6 fusion.13
  (47 shorter events, 1.4 us)
Async XLA Ops:
  0.0 19.1 %collective-permute-start = (f32[8,40,320]{2,1,0:T(8,128)}, f32[8,40,320]{2,1,0:T(8,128)}, u32[]{:S(2)}, u32[]{:S(2)}) collective-permute-start(f32[8,40,320]{2,1,0:T(8,128)} %rest_0_.3), channel_id=1, source_target_pairs={{0,8},{4,12},{8,0},{12,4},{16,24},{20,28},{24,16},{28,20},{1,9},{5... | collective-permute-start | bytes 1228808 | tf_op jit(solution)/shard_map/ppermute | solution.py:512
  2.9 23.5 %collective-permute-start.2 = (f32[8,40,320]{2,1,0:T(8,128)}, f32[8,40,320]{2,1,0:T(8,128)}, u32[]{:S(2)}, u32[]{:S(2)}) collective-permute-start(f32[8,40,320]{2,1,0:T(8,128)} %rest_0_.3), channel_id=1, source_target_pairs={{0,16},{4,20},{8,24},{12,28},{16,0},{20,4},{24,8},{28,12},{1,17},{... | collective-permute-start | bytes 1228808 | tf_op jit(solution)/shard_map/ppermute | solution.py:512
  4.5 22.0 %collective-permute-start.3 = (f32[8,40,320]{2,1,0:T(8,128)}, f32[8,40,320]{2,1,0:T(8,128)}, u32[]{:S(2)}, u32[]{:S(2)}) collective-permute-start(f32[8,40,320]{2,1,0:T(8,128)} %rest_0_.3), channel_id=1, source_target_pairs={{0,24},{4,28},{8,16},{12,20},{16,8},{20,12},{24,0},{28,4},{1,25},{... | collective-permute-start | bytes 1228808 | tf_op jit(solution)/shard_map/ppermute | solution.py:512
  4.5 18.6 %copy-start.5 = (f32[8,40,320]{2,1,0:T(8,128)S(1)}, f32[8,40,320]{2,1,0:T(8,128)}, u32[]{:S(2)}) copy-start(f32[8,40,320]{2,1,0:T(8,128)} %rest_0_.3) | copy-start | bytes 1228804
  4.5 25.1 %copy-start.7 = (f32[32]{0:T(128)S(1)}, f32[32]{0:T(128)}, u32[]{:S(2)}) copy-start(f32[32]{0:T(128)} %param.13) | copy-start | bytes 388
  4.5 25.1 %copy-start.8 = (s32[8]{0:T(128)S(1)}, s32[8]{0:T(128)}, u32[]{:S(2)}) copy-start(s32[8]{0:T(128)} %param.12) | copy-start | bytes 100
  19.1 7.3 %collective-permute-start.1 = (f32[320,128]{1,0:T(8,128)S(1)}, f32[320,128]{1,0:T(8,128)S(1)}, u32[]{:S(2)}, u32[]{:S(2)}) collective-permute-start(f32[320,128]{1,0:T(8,128)S(1)} %get-tuple-element.50), channel_id=1, source_target_pairs={{0,1},{4,5},{8,9},{12,13},{16,17},{20,21},{24,25},{28,29}} | collective-permute-start | bytes 491528 | tf_op jit(solution)/shard_map/ppermute | solution.py:507
  23.1 5.0 %collective-permute-start.6 = (f32[8,40,320]{2,1,0:T(8,128)S(1)}, f32[8,40,320]{2,1,0:T(8,128)S(1)}, u32[]{:S(2)}, u32[]{:S(2)}) collective-permute-start(f32[8,40,320]{2,1,0:T(8,128)S(1)} %copy-done.5), channel_id=1, source_target_pairs={{0,4},{4,0},{8,12},{12,8},{16,20},{20,16},{24,28},{28,24},{1,5},{5... | collective-permute-start | bytes 1228808 | tf_op jit(solution)/shard_map/ppermute | solution.py:512
  23.2 11.3 %collective-permute-start.5 = (f32[320,448]{1,0:T(8,128)S(1)}, f32[320,448]{1,0:T(8,128)S(1)}, u32[]{:S(2)}, u32[]{:S(2)}) collective-permute-start(f32[320,448]{1,0:T(8,128)S(1)} %get-tuple-element.53), channel_id=1, source_target_pairs={{3,2},{7,6},{11,10},{15,14},{19,18},{23,22},{27,26},{31,30}} | collective-permute-start | bytes 1720328 | tf_op jit(solution)/shard_map/ppermute | solution.py:507
  26.5 3.3 %collective-permute-start.7 = (f32[8,40,320]{2,1,0:T(8,128)}, f32[8,40,320]{2,1,0:T(8,128)}, u32[]{:S(2)}, u32[]{:S(2)}) collective-permute-start(f32[8,40,320]{2,1,0:T(8,128)} %collective-permute-done.rest_2_), channel_id=1, source_target_pairs={{0,4},{4,0},{8,12},{12,8},{16,20},{20,16},{24,28},{28,24},{1,5},{5... | collective-permute-start | bytes 1228808 | tf_op jit(solution)/shard_map/ppermute | solution.py:512
  26.5 3.3 %collective-permute-start.8 = (f32[8,40,320]{2,1,0:T(8,128)}, f32[8,40,320]{2,1,0:T(8,128)}, u32[]{:S(2)}, u32[]{:S(2)}) collective-permute-start(f32[8,40,320]{2,1,0:T(8,128)} %collective-permute-done.2.rest_4_), channel_id=1, source_target_pairs={{0,4},{4,0},{8,12},{12,8},{16,20},{20,16},{24,28},{28,24},{1,5},{5... | collective-permute-start | bytes 1228808 | tf_op jit(solution)/shard_map/ppermute | solution.py:512
  27.0 3.1 %collective-permute-start.9 = (f32[8,40,320]{2,1,0:T(8,128)}, f32[8,40,320]{2,1,0:T(8,128)}, u32[]{:S(2)}, u32[]{:S(2)}) collective-permute-start(f32[8,40,320]{2,1,0:T(8,128)} %collective-permute-done.3.rest_6_), channel_id=1, source_target_pairs={{0,4},{4,0},{8,12},{12,8},{16,20},{20,16},{24,28},{28,24},{1,5},{5... | collective-permute-start | bytes 1228808 | tf_op jit(solution)/shard_map/ppermute | solution.py:512
  28.1 0.8 copy-start.6
  28.9 5.6 %collective-permute-start.4 = (f32[320,128]{1,0:T(8,128)}, f32[320,128]{1,0:T(8,128)S(1)}, u32[]{:S(2)}, u32[]{:S(2)}) collective-permute-start(f32[320,128]{1,0:T(8,128)} %convolution_add_fusion.9), channel_id=1, source_target_pairs={{1,2},{5,6},{9,10},{13,14},{17,18},{21,22},{25,26},{29,30}} | collective-permute-start | bytes 491528 | tf_op jit(solution)/shard_map/ppermute | solution.py:507
  35.9 7.7 %collective-permute-start.10 = (f32[320,128]{1,0:T(8,128)S(1)}, f32[320,128]{1,0:T(8,128)S(1)}, u32[]{:S(2)}, u32[]{:S(2)}) collective-permute-start(f32[320,128]{1,0:T(8,128)S(1)} %convolution_add_fusion.6), channel_id=1, source_target_pairs={{2,1},{6,5},{10,9},{14,13},{18,17},{22,21},{26,25},{30,29}} | collective-permute-start | bytes 491528 | tf_op jit(solution)/shard_map/ppermute | solution.py:507
  37.1 9.7 %collective-permute-start.12 = (f32[320,128]{1,0:T(8,128)S(1)}, f32[320,128]{1,0:T(8,128)S(1)}, u32[]{:S(2)}, u32[]{:S(2)}) collective-permute-start(f32[320,128]{1,0:T(8,128)S(1)} %convolution_add_fusion.7), channel_id=1, source_target_pairs={{2,3},{6,7},{10,11},{14,15},{18,19},{22,23},{26,27},{30,31}} | collective-permute-start | bytes 491528 | tf_op jit(solution)/shard_map/ppermute | solution.py:507
  37.8 9.0 %copy-start.1 = (bf16[8,320,768]{2,1,0:T(8,128)(2,1)S(1)}, bf16[8,320,768]{2,1,0:T(8,128)(2,1)}, u32[]{:S(2)}) copy-start(bf16[8,320,768]{2,1,0:T(8,128)(2,1)} %get-tuple-element.48.low) | copy-start | bytes 11796484
  37.8 9.0 %copy-start.2 = (f32[8,320,128]{2,1,0:T(8,128)S(1)}, f32[8,320,128]{2,1,0:T(8,128)}, u32[]{:S(2)}) copy-start(f32[8,320,128]{2,1,0:T(8,128)} %get-tuple-element.46.x) | copy-start | bytes 3932164
  37.8 9.0 %copy-start.3 = (f32[8,320,128]{2,1,0:T(8,128)S(1)}, f32[8,320,128]{2,1,0:T(8,128)}, u32[]{:S(2)}) copy-start(f32[8,320,128]{2,1,0:T(8,128)} %probe.3) | copy-start | bytes 3932164
  42.9 3.9 %copy-start = (bf16[8,320,768]{2,1,0:T(8,128)(2,1)S(1)}, bf16[8,320,768]{2,1,0:T(8,128)(2,1)}, u32[]{:S(2)}) copy-start(bf16[8,320,768]{2,1,0:T(8,128)(2,1)} %get-tuple-element.47.high) | copy-start | bytes 11796484
  43.9 10.6 %collective-permute-start.11 = (f32[320,128]{1,0:T(8,128)S(1)}, f32[320,128]{1,0:T(8,128)S(1)}, u32[]{:S(2)}, u32[]{:S(2)}) collective-permute-start(f32[320,128]{1,0:T(8,128)S(1)} %convolution_add_fusion.5), channel_id=1, source_target_pairs={{1,0},{5,4},{9,8},{13,12},{17,16},{21,20},{25,24},{29,28}} | collective-permute-start | bytes 491528 | tf_op jit(solution)/shard_map/ppermute | solution.py:507
  45.3 25.1 %collective-permute-start.14 = (f32[320,320]{1,0:T(8,128)S(1)}, f32[320,320]{1,0:T(8,128)S(1)}, u32[]{:S(2)}, u32[]{:S(2)}) collective-permute-start(f32[320,320]{1,0:T(8,128)S(1)} %convolution_add_fusion), channel_id=1, source_target_pairs={{2,1},{6,5},{10,9},{14,13},{18,17},{22,21},{26,25},{30,29}} | collective-permute-start | bytes 1228808 | tf_op jit(solution)/shard_map/ppermute | solution.py:507
  47.8 23.0 %collective-permute-start.15 = (f32[320,128]{1,0:T(8,128)S(1)}, f32[320,128]{1,0:T(8,128)S(1)}, u32[]{:S(2)}, u32[]{:S(2)}) collective-permute-start(f32[320,128]{1,0:T(8,128)S(1)} %get-tuple-element.78), channel_id=1, source_target_pairs={{3,2},{7,6},{11,10},{15,14},{19,18},{23,22},{27,26},{31,30}} | collective-permute-start | bytes 491528 | tf_op jit(solution)/shard_map/ppermute | solution.py:507
  64.0 6.5 %collective-permute-start.13 = (f32[320,128]{1,0:T(8,128)S(1)}, f32[320,128]{1,0:T(8,128)S(1)}, u32[]{:S(2)}, u32[]{:S(2)}) collective-permute-start(f32[320,128]{1,0:T(8,128)S(1)} %get-tuple-element.74), channel_id=1, source_target_pairs={{0,1},{4,5},{8,9},{12,13},{16,17},{20,21},{24,25},{28,29}} | collective-permute-start | bytes 491528 | tf_op jit(solution)/shard_map/ppermute | solution.py:507
  71.5 1.7 %collective-permute-start.16 = (f32[320,128]{1,0:T(8,128)S(1)}, f32[320,128]{1,0:T(8,128)S(1)}, u32[]{:S(2)}, u32[]{:S(2)}) collective-permute-start(f32[320,128]{1,0:T(8,128)S(1)} %fusion.1), channel_id=1, source_target_pairs={{1,2},{2,1},{5,6},{6,5},{9,10},{10,9},{13,14},{14,13},{17,18},{18,... | collective-permute-start | bytes 491528 | tf_op jit(solution)/shard_map/ppermute | solution.py:507
  73.2 11.7 %copy-start.4 = (f32[8,320,128]{2,1,0:T(8,128)S(1)}, f32[8,320,128]{2,1,0:T(8,128)}, u32[]{:S(2)}) copy-start(f32[8,320,128]{2,1,0:T(8,128)} %get-tuple-element.73.x) | copy-start | bytes 3932164
  73.6 11.3 %collective-permute-start.17 = (f32[320,128]{1,0:T(8,128)S(1)}, f32[320,128]{1,0:T(8,128)S(1)}, u32[]{:S(2)}, u32[]{:S(2)}) collective-permute-start(f32[320,128]{1,0:T(8,128)S(1)} %add.74), channel_id=1, source_target_pairs={{1,0},{2,3},{5,4},{6,7},{9,8},{10,11},{13,12},{14,15},{17,16},{18,... | collective-permute-start | bytes 491528 | tf_op jit(solution)/shard_map/ppermute | solution.py:507
  87.9 1.2 %collective-permute-start.18 = (f32[4,8,40]{2,1,0:T(8,128)S(1)}, f32[4,8,40]{2,1,0:T(8,128)S(1)}, u32[]{:S(2)}, u32[]{:S(2)}) collective-permute-start(f32[4,8,40]{2,1,0:T(8,128)S(1)} %slice.37), channel_id=1, source_target_pairs={{0,4},{4,0},{8,12},{12,8},{16,20},{20,16},{24,28},{28,24},{1,5},{5... | collective-permute-start | bytes 15368 | tf_op jit(solution)/shard_map/ppermute | solution.py:512
  89.2 3.7 %collective-permute-start.19 = (f32[8,40]{1,0:T(8,128)S(1)}, f32[8,40]{1,0:T(8,128)S(1)}, u32[]{:S(2)}, u32[]{:S(2)}) collective-permute-start(f32[8,40]{1,0:T(8,128)S(1)} %get-tuple-element.87), channel_id=1, source_target_pairs={{0,8},{4,12},{8,0},{12,4},{16,24},{20,28},{24,16},{28,20},{1,9},{5... | collective-permute-start | bytes 3848 | tf_op jit(solution)/shard_map/ppermute | solution.py:512
  90.7 3.6 %collective-permute-start.20 = (f32[8,40]{1,0:T(8,128)S(1)}, f32[8,40]{1,0:T(8,128)S(1)}, u32[]{:S(2)}, u32[]{:S(2)}) collective-permute-start(f32[8,40]{1,0:T(8,128)S(1)} %get-tuple-element.89), channel_id=1, source_target_pairs={{0,16},{4,20},{8,24},{12,28},{16,0},{20,4},{24,8},{28,12},{1,17},{... | collective-permute-start | bytes 3848 | tf_op jit(solution)/shard_map/ppermute | solution.py:512
  92.3 4.5 %collective-permute-start.21 = (f32[8,40]{1,0:T(8,128)S(1)}, f32[8,40]{1,0:T(8,128)S(1)}, u32[]{:S(2)}, u32[]{:S(2)}) collective-permute-start(f32[8,40]{1,0:T(8,128)S(1)} %get-tuple-element.88), channel_id=1, source_target_pairs={{0,24},{4,28},{8,16},{12,20},{16,8},{20,12},{24,0},{28,4},{1,25},{... | collective-permute-start | bytes 3848 | tf_op jit(solution)/shard_map/ppermute | solution.py:512

commit v5 on v4

--- a/solution.py
+++ b/solution.py
@@ -232,30 +232,32 @@
 def drive_kernel(start, me, scale, pivot, *rest):
     pieces, out, gathered = rest[:-2], rest[-2], rest[-1]
     step = pl.program_id(0)
-    if len(pieces) > 1:
-        rows = pieces[0].shape[1]
-        for j, piece in enumerate(pieces):
-            owner = lax.bitwise_xor(me[0], j)
-            gathered[pl.ds(pl.multiple_of(owner * rows, 8), rows), :] = piece[0]
-        potential = gathered[...]
-    else:
-        potential = pieces[0][0]
-    out[step] = left_two(apply_three(left_three(pivot[0]), *halves(potential * scale[step + start])))
+    for i in range(2):
+        if len(pieces) > 1:
+            rows = pieces[0].shape[1]
+            for j, piece in enumerate(pieces):
+                owner = lax.bitwise_xor(me[0], j)
+                gathered[i, pl.ds(pl.multiple_of(owner * rows, 8), rows), :] = piece[i]
+            potential = gathered[i]
+        else:
+            potential = pieces[0][i]
+        potential = potential * scale[2 * step + i + start]
+        out[2 * step + i] = left_two(apply_three(left_three(pivot[i]), *halves(potential)))
 
 
 def drive(start, stop, me, scale, pivots, pieces):
     b = pivots.shape[1]
     rows = pieces[0].shape[1]
-    at = lambda i: (i + start, 0, 0)
+    at = lambda i: (i + start // 2, 0, 0)
     return pl.pallas_call(
         functools.partial(drive_kernel, start),
-        grid=(stop - start,),
-        in_specs=[SMEM, SMEM, pl.BlockSpec((1, b, b), at)]
-        + [pl.BlockSpec((1, rows, b), at)] * len(pieces),
+        grid=((stop - start) // 2,),
+        in_specs=[SMEM, SMEM, pl.BlockSpec((2, b, b), at)]
+        + [pl.BlockSpec((2, rows, b), at)] * len(pieces),
         out_specs=VMEM,
         out_shape=pltpu.VMEM((stop - start, b, 2 * b), BF16),
-        scratch_shapes=[pltpu.VMEM((b, b), F32)],
-        compiler_params=params(10),
+        scratch_shapes=[pltpu.VMEM((2, b, b), F32)],
+        compiler_params=params(14),
         cost_estimate=cost(0.01),
         name="drive_maps",
     )(me, scale, *in_hbm(pivots, *pieces))
@@ -463,37 +465,36 @@
     )(places, *in_vmem(y, u), *in_hbm(x_of_3))
 
 
-def charge_kernel(places, weight, x, high, low, probe, in_1, in_2, out_1, out_2, ended, *outs):
+def charge_kernel(places, weight, x, high, low, probe, in_1, in_2, out_1, out_2, ended, blocks, terms):
     n, b, k = x.shape
-    at, energy = places[0], places[1]
+    at = places[0]
     none = jnp.zeros_like(ended)
     inflow = jnp.where(at == 1, in_1[...], jnp.where(at == 2, in_2[...], none))
     inflow = jnp.where(at == 3, ended[...], inflow)
     outflow = jnp.where(at == 1, out_1[...], jnp.where(at == 2, out_2[...], none))
     outflow = jnp.where(at == 0, ended[...], outflow)
     flows = jnp.concatenate(halves(jnp.concatenate([inflow, outflow], axis=0)), axis=1)
-    terms = outs[-1]
-    for i in range(0, n, 2):
-        for j, value in enumerate(add_flows(x, high, low, i, flows)):
-            charges = jnp.sum((value * probe[i + j]).T, axis=0, keepdims=True)
-            terms[i + j : i + j + 1, :] = charges * weight[0]
-    if len(outs) > 1:
-        blocks = outs[0]
-        owners, _, rows = blocks.shape
-        for owner in range(owners):
-            j = lax.bitwise_xor(energy, owner)
-            blocks[lax.div(j, 2) + lax.rem(j, 2) * (owners // 2)] = terms[:, owner * rows : (owner + 1) * rows]
+    skip = high.shape[2] - flows.shape[0]
+    for i in range(n):
+        maps = jnp.concatenate([high[i, :, skip:], low[i, :, skip:]], axis=1)
+        out = dot(maps, jnp.concatenate([flows, flows], axis=0))
+        value = x[i] + out[:, :k] + out[:, k:]
+        terms[i : i + 1, :] = jnp.sum((value * probe[i]).T, axis=0, keepdims=True) * weight[0]
+    owners = blocks.shape[0]
+    rows = b // owners
+    for owner in range(owners):
+        blocks[owner, :, :rows] = terms[:, owner * rows : (owner + 1) * rows]
 
 
 def charge(places, weight, energies, x, high, low, probes, *flows):
     n, b, k = probes.shape
-    by_swaps = energies == 8
+    wide = -(-(b // energies) // 128) * 128
     return pl.pallas_call(
         charge_kernel,
         in_specs=[SMEM] * 2 + [VMEM] * (4 + len(flows)),
         out_specs=VMEM,
-        out_shape=pltpu.VMEM((energies, n, b // energies) if by_swaps else (n, b), F32),
-        scratch_shapes=[pltpu.VMEM((n, b), F32)] if by_swaps else [],
+        out_shape=pltpu.VMEM((energies, n, wide), F32),
+        scratch_shapes=[pltpu.VMEM((n, b), F32)],
         compiler_params=params(10),
         name="charge_terms",
     )(places, weight, *in_vmem(x, high, low, probes), *flows)
@@ -596,13 +597,8 @@
 
     weight = weights / (k * energies)
     terms = charge(places, weight, energies, x, high, low, probes, in_1, swapped, swapped + past, beyond, ended)
-    if energies == 8:
-        half = energies // 2
-        total = terms[:half] + near(terms[half:], (1,))[0]
-        parts = [near(total[j], (2 * j,))[0] for j in range(1, half)]
-        return total[0] + parts[0] + parts[1] + parts[2]
-    split = terms.reshape(n, energies, b // energies).transpose(1, 0, 2)
-    return jnp.sum(lax.all_to_all(split, "energy", 0, 0, tiled=True), axis=0)
+    summed = jnp.sum(lax.all_to_all(terms, "energy", 0, 0, tiled=True), axis=0)
+    return summed[:, : b // energies]
 
 
 def solution(mesh):

time: 97.7 us -> 96.4 us (0.987)
  blocking collectives: 0 us -> 8.36 us
  waiting for transfers between devices: 23.9 us -> 20.1 us
  starting transfers between devices: 22.2 us -> 18.8 us
  Pallas kernels: 41.5 us -> 39.1 us
    all_to_all x0 -> x1, blocking collectives: none -> 8.36 us  [per_device(): summed = jnp.sum(lax.all_to_all(terms, 'energy', 0, 0, tiled=True), axis=0)]
    ppermute x11 -> x7, waiting for transfers between devices: 8.11 us -> 2.9 us  [near(): lax.ppermute(x, 'energy', [(i, i ^ way) for i in range(peers)])]
    ppermute x11 -> x7, starting transfers between devices: 8.73 us -> 5.11 us  [near(): lax.ppermute(x, 'energy', [(i, i ^ way) for i in range(peers)])]
    pallas_call x2, Pallas kernels: 9.45 us -> 7.38 us  [drive(): pl.pallas_call(functools.partial(drive_kernel, start), grid=((stop - star...]
    ppermute x11, waiting for transfers between devices: 15.7 us -> 17.2 us  [send(): return lax.ppermute(x, 'dom', list(pairs))]
  transfers between devices with their start and end apart: 22 -> 18, of which waited for: 8 -> 4; matrix products, arithmetic and copies ran while one was open for 5% -> 5% of each run, Pallas kernels for 40% -> 38%
where the time goes in v5:
time: 96.4 us; the launch traced here: 96.1 us
  Pallas kernels  39.1 us (41%)
  waiting for transfers between devices  20.1 us (21%)
  starting transfers between devices  18.8 us (20%)
  blocking collectives  8.36 us (9%)
  matrix products  6.87 us (7%)
  between operations  1.11 us (1%)
    ppermute x11, waiting for transfers between devices, send(): return lax.ppermute(x, 'dom', list(pairs))  17.2 us
    pallas_call x1, Pallas kernels, local_maps(): pl.pallas_call(local_kernel, in_specs=[HBM] * 4, out_specs=[HBM] * 3 + [V...  14.6 us
    ppermute x11, starting transfers between devices, send(): return lax.ppermute(x, 'dom', list(pairs))  13.6 us
    pallas_call x1, Pallas kernels, second_ahead(): pl.pallas_call(second_ahead_kernel, in_specs=[SMEM] + [HBM] * 2 + [VMEM]...  9.44 us
    all_to_all x1, blocking collectives, per_device(): summed = jnp.sum(lax.all_to_all(terms, 'energy', 0, 0, tiled=True), axis=0)  8.36 us
    pallas_call x2, Pallas kernels, drive(): pl.pallas_call(functools.partial(drive_kernel, start), grid=((stop - star...  7.38 us
    dot_general x17, matrix products, mm(): return jnp.dot(a, b, precision=HIGH)  6.87 us
    ppermute x7, starting transfers between devices, near(): lax.ppermute(x, 'energy', [(i, i ^ way) for i in range(peers)])  5.11 us
  transfers between devices with their start and end apart: 18, of which 4 were waited for; matrix products, arithmetic and copies ran while one was open for 5% of the time, Pallas kernels for 38%

profile of v5, /device:TPU:0, one launch (start us, length us, event | category | flops | bytes accessed | tf_op | source)
XLA Modules:
  0.0 96.1 jit_solution(3661475999576676374)
XLA Ops:
  0.0 2.9 %collective-permute-start = (f32[8,40,320]{2,1,0:T(8,128)}, f32[8,40,320]{2,1,0:T(8,128)}, u32[]{:S(2)}, u32[]{:S(2)}) collective-permute-start(f32[8,40,320]{2,1,0:T(8,128)} %rest_0_.3), channel_id=1, source_target_pairs={{0,8},{4,12},{8,0},{12,4},{16,24},{20,28},{24,16},{28,20},{1,9},{5... | collective-permute-start | bytes 1228808 | tf_op jit(solution)/shard_map/ppermute | solution.py:513
  2.9 1.5 %collective-permute-start.2 = (f32[8,40,320]{2,1,0:T(8,128)}, f32[8,40,320]{2,1,0:T(8,128)}, u32[]{:S(2)}, u32[]{:S(2)}) collective-permute-start(f32[8,40,320]{2,1,0:T(8,128)} %rest_0_.3), channel_id=1, source_target_pairs={{0,16},{4,20},{8,24},{12,28},{16,0},{20,4},{24,8},{28,12},{1,17},{... | collective-permute-start | bytes 1228808 | tf_op jit(solution)/shard_map/ppermute | solution.py:513
  4.5 14.6 %local_maps.1 = (f32[8,320,128]{2,1,0:T(8,128)}, bf16[8,320,768]{2,1,0:T(8,128)(2,1)}, bf16[8,320,768]{2,1,0:T(8,128)(2,1)}, f32[320,128]{1,0:T(8,128)S(1)}, f32...) custom-call(f32[8,320,320]{2,1,0:T(8,128)} %bitcast.35, ...), custom_call_target="tpu_custom_call" | custom-call | flops 15000000512 | tf_op jit(solution)/shard_map/local_maps/pallas_call | solution.py:193
  19.1 4.0 %collective-permute-start.1 = (f32[320,128]{1,0:T(8,128)S(1)}, f32[320,128]{1,0:T(8,128)S(1)}, u32[]{:S(2)}, u32[]{:S(2)}) collective-permute-start(f32[320,128]{1,0:T(8,128)S(1)} %get-tuple-element.50), channel_id=1, source_target_pairs={{0,1},{4,5},{8,9},{12,13},{16,17},{20,21},{24,25},{28,29}} | collective-permute-start | bytes 491528 | tf_op jit(solution)/shard_map/ppermute | solution.py:508
  23.2 0.7 collective-permute-start.5
  23.9 2.6 %collective-permute-done.2.rest_4_ = f32[8,40,320]{2,1,0:T(8,128)} collective-permute-done((f32[8,40,320]{2,1,0:T(8,128)}, f32[8,40,320]{2,1,0:T(8,128)}, u32[]{:S(2)}, u32[]{:S(2)}) %collective-permute-start.2) | collective-permute-done | bytes 409632 | tf_op jit(solution)/shard_map/ppermute | solution.py:513
  26.5 0.5 collective-permute-start.8
  27.0 0.1 collective-permute-start.9
  27.1 1.0 %convolution_add_fusion.9 = f32[320,128]{1,0:T(8,128)} fusion(f32[320,128]{1,0:T(8,128)S(1)} %get-tuple-element.50, f32[320,320]{1,0:T(8,128)S(1)} %get-tuple-element.51, f32[320,128]{1,0:T(8,128)S(1)} %collective-permute-done.1.in_1), kind=kOutput, calls=%fused_computation.11 | convolution fusion | flops 78684160 | bytes 901120 | tf_op jit(solution)/shard_map/dot_general | solution.py:504
  28.1 0.8 copy-done.6
  28.9 0.7 collective-permute-start.4
  29.6 0.2 select_reduce_fusion.scale
  29.8 0.3 collective-permute-done.9.rest_7_
  30.1 3.6 %drive_maps.2.drive_a = bf16[4,320,640]{2,1,0:T(8,128)(2,1)S(1)} custom-call(s32[1]{0:T(128)} %bitcast.1.me, f32[8]{0:T(128)S(1)} %select_reduce_fusion.scale, f32[8,320,320]{2,1,0:T(8,128)} %bitcast.36, f32[8,40,320]{2,1,0:T(8,128)} %rest_0_.3, f32[8,40,320]{2,1,0:T(8,128)} %copy-done.6, f32[8,40,320]{2,1,0:T(8,128)} %collective-permute-done.rest_2_, ...), custom_call_target="tpu_custom_call" | custom-call | flops 10000000 | tf_op jit(solution)/shard_map/drive_maps/pallas_call | solution.py:252
  33.7 0.3 convolution_add_fusion.7
  34.1 0.3 slice_add_fusion.out_2
  34.4 0.3 convolution_add_fusion.8
  34.7 0.3 convolution_add_fusion.6
  35.1 0.7 collective-permute-start.10
  35.8 0.6 fusion.8
  36.4 0.7 collective-permute-start.12
  37.1 3.8 %drive_maps.3.drive_b = bf16[4,320,640]{2,1,0:T(8,128)(2,1)S(1)} custom-call(s32[1]{0:T(128)} %bitcast.1.me, f32[8]{0:T(128)S(1)} %select_reduce_fusion.scale, f32[8,320,320]{2,1,0:T(8,128)} %bitcast.37, f32[8,40,320]{2,1,0:T(8,128)} %rest_0_.3, f32[8,40,320]{2,1,0:T(8,128)} %copy-done.6, f32[8,40,320]{2,1,0:T(8,128)} %collective-permute-done.rest_2_, ...), custom_call_target="tpu_custom_call" | custom-call | flops 10000000 | tf_op jit(solution)/shard_map/drive_maps/pallas_call | solution.py:252
  40.9 0.6 convolution_add_fusion
  41.5 0.3 convolution_add_fusion.5
  41.8 1.4 %collective-permute-start.11 = (f32[320,128]{1,0:T(8,128)S(1)}, f32[320,128]{1,0:T(8,128)S(1)}, u32[]{:S(2)}, u32[]{:S(2)}) collective-permute-start(f32[320,128]{1,0:T(8,128)S(1)} %convolution_add_fusion.5), channel_id=1, source_target_pairs={{1,0},{5,4},{9,8},{13,12},{17,16},{21,20},{25,24},{29,28}} | collective-permute-start | bytes 491528 | tf_op jit(solution)/shard_map/ppermute | solution.py:508
  43.3 0.7 collective-permute-start.14
  44.7 0.1 pad_add_fusion.places
  44.8 1.0 %second_of_3.1 = (f32[8,320,128]{2,1,0:T(8,128)}, f32[320,128]{1,0:T(8,128)S(1)}) custom-call(s32[2]{0:T(128)S(1)} %pad_add_fusion.places, f32[8,320,320]{2,1,0:T(8,128)} %bitcast.39, f32[8,320,320]{2,1,0:T(8,128)} %bitcast.42, f32[8,320,128]{2,1,0:T(8,128)S(1)} %copy-done.2, bf16[8,320,768]{2,1,0:T(8,128)(2,1)S(1)} %copy-done, ...), custom_call_target="tpu_custom_call" | custom-call | flops 10000000 | tf_op jit(solution)/shard_map/second_of_3/pallas_call | solution.py:378
  45.8 0.7 collective-permute-start.15
  46.4 7.9 %collective-permute-done.11.out_0 = f32[320,128]{1,0:T(8,128)S(1)} collective-permute-done((f32[320,128]{1,0:T(8,128)S(1)}, f32[320,128]{1,0:T(8,128)S(1)}, u32[]{:S(2)}, u32[]{:S(2)}) %collective-permute-start.11) | collective-permute-done | bytes 163872 | tf_op jit(solution)/shard_map/ppermute | solution.py:508
  54.4 9.4 %second_ahead.1 = (f32[8,320,128]{2,1,0:T(8,128)S(1)}, f32[8,320,320]{2,1,0:T(8,128)S(1)}, f32[320,128]{1,0:T(8,128)S(1)}) custom-call(s32[2]{0:T(128)S(1)} %pad_add_fusion.places, f32[8,320,320]{2,1,0:T(8,128)} %bitcast.40, f32[8,320,320]{2,1,0:T(8,128)} %bitcast.43, f32[8,320,128]{2,1,0:T(8,128)S(1)} %copy-done.2, bf16[8,320,768]{2,1,0:T(8,128)(2,1)S(1)} %copy-done, ...), custom_call_target="tpu_custom_call" | custom-call | flops 10000000 | tf_op jit(solution)/shard_map/second_ahead/pallas_call | solution.py:420
  63.8 2.2 %collective-permute-start.13 = (f32[320,128]{1,0:T(8,128)S(1)}, f32[320,128]{1,0:T(8,128)S(1)}, u32[]{:S(2)}, u32[]{:S(2)}) collective-permute-start(f32[320,128]{1,0:T(8,128)S(1)} %get-tuple-element.74), channel_id=1, source_target_pairs={{0,1},{4,5},{8,9},{12,13},{16,17},{20,21},{24,25},{28,29}} | collective-permute-start | bytes 491528 | tf_op jit(solution)/shard_map/ppermute | solution.py:508
  66.0 4.1 %second_back.1 = (f32[8,320,128]{2,1,0:T(8,128)}, f32[320,128]{1,0:T(8,128)S(1)}) custom-call(s32[2]{0:T(128)S(1)} %pad_add_fusion.places, f32[8,320,128]{2,1,0:T(8,128)S(1)} %get-tuple-element.70.y, f32[8,320,320]{2,1,0:T(8,128)S(1)} %get-tuple-element.71.u, f32[8,320,128]{2,1,0:T(8,128)} %get-tuple-element.72.x_of_3), custom_call_target="tpu_custom_call", output_to_operand_aliasing={{0}: (3, {})} | custom-call | flops 10000000 | tf_op jit(solution)/shard_map/second_back/pallas_call | solution.py:450
  70.1 0.3 fusion.6
  70.5 0.3 convolution_add_fusion.3
  70.8 0.3 fusion.11
  71.2 0.3 fusion.1
  71.5 0.7 collective-permute-start.16
  72.2 0.3 fusion.12
  72.5 0.3 fusion.13
  72.9 0.3 fusion.2
  73.2 0.3 fusion.14
  73.6 1.3 %collective-permute-start.17 = (f32[320,128]{1,0:T(8,128)S(1)}, f32[320,128]{1,0:T(8,128)S(1)}, u32[]{:S(2)}, u32[]{:S(2)}) collective-permute-start(f32[320,128]{1,0:T(8,128)S(1)} %add.62), channel_id=1, source_target_pairs={{1,0},{2,3},{5,4},{6,7},{9,8},{10,11},{13,12},{14,15},{17,16},{18,... | collective-permute-start | bytes 491528 | tf_op jit(solution)/shard_map/ppermute | solution.py:508
  74.9 0.3 convolution_add_fusion.1.out_2
  75.3 9.3 %collective-permute-done.17.ended = f32[320,128]{1,0:T(8,128)S(1)} collective-permute-done((f32[320,128]{1,0:T(8,128)S(1)}, f32[320,128]{1,0:T(8,128)S(1)}, u32[]{:S(2)}, u32[]{:S(2)}) %collective-permute-start.17) | collective-permute-done | bytes 163872 | tf_op jit(solution)/shard_map/ppermute | solution.py:508
  84.5 2.6 %charge_terms.1 = f32[8,8,128]{2,1,0:T(8,128)S(1)} custom-call(s32[2]{0:T(128)S(1)} %pad_add_fusion.places, f32[1]{0:T(128)S(6)} %div.3.weight, f32[8,320,128]{2,1,0:T(8,128)S(1)} %copy-done.4, bf16[8,320,768]{2,1,0:T(8,128)(2,1)S(1)} %copy-done, bf16[8,320,768]{2,1,0:T(8,128)(2,1)S(1)} %copy-done.1, f32[8,320,128]{2,1,0:T(8,128)S(1)} %copy-done.3, ...), custom_call_target="tpu_custom_call" | custom-call | tf_op jit(solution)/shard_map/charge_terms/pallas_call | solution.py:492
  87.2 8.4 %all_to_all.5 = f32[8,8,128]{2,1,0:T(8,128)S(1)} all-to-all(f32[8,8,128]{2,1,0:T(8,128)S(1)} %charge_terms.1), channel_id=1, replica_groups=mesh['energy'=8,'dom'=4] {'energy'}, dimensions={0} | all-to-all | bytes 65536 | tf_op jit(solution)/shard_map/all_to_all | solution.py:600
  95.5 0.6 reduce_sum.19
  (37 shorter events, 0.2 us)
Async XLA Ops:
  0.0 19.1 %collective-permute-start = (f32[8,40,320]{2,1,0:T(8,128)}, f32[8,40,320]{2,1,0:T(8,128)}, u32[]{:S(2)}, u32[]{:S(2)}) collective-permute-start(f32[8,40,320]{2,1,0:T(8,128)} %rest_0_.3), channel_id=1, source_target_pairs={{0,8},{4,12},{8,0},{12,4},{16,24},{20,28},{24,16},{28,20},{1,9},{5... | collective-permute-start | bytes 1228808 | tf_op jit(solution)/shard_map/ppermute | solution.py:513
  2.9 23.5 %collective-permute-start.2 = (f32[8,40,320]{2,1,0:T(8,128)}, f32[8,40,320]{2,1,0:T(8,128)}, u32[]{:S(2)}, u32[]{:S(2)}) collective-permute-start(f32[8,40,320]{2,1,0:T(8,128)} %rest_0_.3), channel_id=1, source_target_pairs={{0,16},{4,20},{8,24},{12,28},{16,0},{20,4},{24,8},{28,12},{1,17},{... | collective-permute-start | bytes 1228808 | tf_op jit(solution)/shard_map/ppermute | solution.py:513
  4.5 22.0 %collective-permute-start.3 = (f32[8,40,320]{2,1,0:T(8,128)}, f32[8,40,320]{2,1,0:T(8,128)}, u32[]{:S(2)}, u32[]{:S(2)}) collective-permute-start(f32[8,40,320]{2,1,0:T(8,128)} %rest_0_.3), channel_id=1, source_target_pairs={{0,24},{4,28},{8,16},{12,20},{16,8},{20,12},{24,0},{28,4},{1,25},{... | collective-permute-start | bytes 1228808 | tf_op jit(solution)/shard_map/ppermute | solution.py:513
  4.5 18.6 %copy-start.5 = (f32[8,40,320]{2,1,0:T(8,128)S(1)}, f32[8,40,320]{2,1,0:T(8,128)}, u32[]{:S(2)}) copy-start(f32[8,40,320]{2,1,0:T(8,128)} %rest_0_.3) | copy-start | bytes 1228804
  4.5 25.1 %copy-start.7 = (f32[32]{0:T(128)S(1)}, f32[32]{0:T(128)}, u32[]{:S(2)}) copy-start(f32[32]{0:T(128)} %param.13) | copy-start | bytes 388
  4.5 25.1 %copy-start.8 = (s32[8]{0:T(128)S(1)}, s32[8]{0:T(128)}, u32[]{:S(2)}) copy-start(s32[8]{0:T(128)} %param.12) | copy-start | bytes 100
  19.1 7.3 %collective-permute-start.1 = (f32[320,128]{1,0:T(8,128)S(1)}, f32[320,128]{1,0:T(8,128)S(1)}, u32[]{:S(2)}, u32[]{:S(2)}) collective-permute-start(f32[320,128]{1,0:T(8,128)S(1)} %get-tuple-element.50), channel_id=1, source_target_pairs={{0,1},{4,5},{8,9},{12,13},{16,17},{20,21},{24,25},{28,29}} | collective-permute-start | bytes 491528 | tf_op jit(solution)/shard_map/ppermute | solution.py:508
  23.1 5.0 %collective-permute-start.6 = (f32[8,40,320]{2,1,0:T(8,128)S(1)}, f32[8,40,320]{2,1,0:T(8,128)S(1)}, u32[]{:S(2)}, u32[]{:S(2)}) collective-permute-start(f32[8,40,320]{2,1,0:T(8,128)S(1)} %copy-done.5), channel_id=1, source_target_pairs={{0,4},{4,0},{8,12},{12,8},{16,20},{20,16},{24,28},{28,24},{1,5},{5... | collective-permute-start | bytes 1228808 | tf_op jit(solution)/shard_map/ppermute | solution.py:513
  23.2 10.5 %collective-permute-start.5 = (f32[320,448]{1,0:T(8,128)S(1)}, f32[320,448]{1,0:T(8,128)S(1)}, u32[]{:S(2)}, u32[]{:S(2)}) collective-permute-start(f32[320,448]{1,0:T(8,128)S(1)} %get-tuple-element.53), channel_id=1, source_target_pairs={{3,2},{7,6},{11,10},{15,14},{19,18},{23,22},{27,26},{31,30}} | collective-permute-start | bytes 1720328 | tf_op jit(solution)/shard_map/ppermute | solution.py:508
  26.5 3.3 %collective-permute-start.7 = (f32[8,40,320]{2,1,0:T(8,128)}, f32[8,40,320]{2,1,0:T(8,128)}, u32[]{:S(2)}, u32[]{:S(2)}) collective-permute-start(f32[8,40,320]{2,1,0:T(8,128)} %collective-permute-done.rest_2_), channel_id=1, source_target_pairs={{0,4},{4,0},{8,12},{12,8},{16,20},{20,16},{24,28},{28,24},{1,5},{5... | collective-permute-start | bytes 1228808 | tf_op jit(solution)/shard_map/ppermute | solution.py:513
  26.5 3.3 %collective-permute-start.8 = (f32[8,40,320]{2,1,0:T(8,128)}, f32[8,40,320]{2,1,0:T(8,128)}, u32[]{:S(2)}, u32[]{:S(2)}) collective-permute-start(f32[8,40,320]{2,1,0:T(8,128)} %collective-permute-done.2.rest_4_), channel_id=1, source_target_pairs={{0,4},{4,0},{8,12},{12,8},{16,20},{20,16},{24,28},{28,24},{1,5},{5... | collective-permute-start | bytes 1228808 | tf_op jit(solution)/shard_map/ppermute | solution.py:513
  27.0 3.1 %collective-permute-start.9 = (f32[8,40,320]{2,1,0:T(8,128)}, f32[8,40,320]{2,1,0:T(8,128)}, u32[]{:S(2)}, u32[]{:S(2)}) collective-permute-start(f32[8,40,320]{2,1,0:T(8,128)} %collective-permute-done.3.rest_6_), channel_id=1, source_target_pairs={{0,4},{4,0},{8,12},{12,8},{16,20},{20,16},{24,28},{28,24},{1,5},{5... | collective-permute-start | bytes 1228808 | tf_op jit(solution)/shard_map/ppermute | solution.py:513
  28.1 0.8 copy-start.6
  28.9 4.8 %collective-permute-start.4 = (f32[320,128]{1,0:T(8,128)}, f32[320,128]{1,0:T(8,128)S(1)}, u32[]{:S(2)}, u32[]{:S(2)}) collective-permute-start(f32[320,128]{1,0:T(8,128)} %convolution_add_fusion.9), channel_id=1, source_target_pairs={{1,2},{5,6},{9,10},{13,14},{17,18},{21,22},{25,26},{29,30}} | collective-permute-start | bytes 491528 | tf_op jit(solution)/shard_map/ppermute | solution.py:508
  35.1 6.4 %collective-permute-start.10 = (f32[320,128]{1,0:T(8,128)S(1)}, f32[320,128]{1,0:T(8,128)S(1)}, u32[]{:S(2)}, u32[]{:S(2)}) collective-permute-start(f32[320,128]{1,0:T(8,128)S(1)} %convolution_add_fusion.6), channel_id=1, source_target_pairs={{2,1},{6,5},{10,9},{14,13},{18,17},{22,21},{26,25},{30,29}} | collective-permute-start | bytes 491528 | tf_op jit(solution)/shard_map/ppermute | solution.py:508
  36.4 8.4 %collective-permute-start.12 = (f32[320,128]{1,0:T(8,128)S(1)}, f32[320,128]{1,0:T(8,128)S(1)}, u32[]{:S(2)}, u32[]{:S(2)}) collective-permute-start(f32[320,128]{1,0:T(8,128)S(1)} %convolution_add_fusion.7), channel_id=1, source_target_pairs={{2,3},{6,7},{10,11},{14,15},{18,19},{22,23},{26,27},{30,31}} | collective-permute-start | bytes 491528 | tf_op jit(solution)/shard_map/ppermute | solution.py:508
  37.1 7.7 %copy-start.1 = (bf16[8,320,768]{2,1,0:T(8,128)(2,1)S(1)}, bf16[8,320,768]{2,1,0:T(8,128)(2,1)}, u32[]{:S(2)}) copy-start(bf16[8,320,768]{2,1,0:T(8,128)(2,1)} %get-tuple-element.48.low) | copy-start | bytes 11796484
  37.1 7.7 %copy-start.2 = (f32[8,320,128]{2,1,0:T(8,128)S(1)}, f32[8,320,128]{2,1,0:T(8,128)}, u32[]{:S(2)}) copy-start(f32[8,320,128]{2,1,0:T(8,128)} %get-tuple-element.46.x) | copy-start | bytes 3932164
  37.1 7.7 %copy-start.3 = (f32[8,320,128]{2,1,0:T(8,128)S(1)}, f32[8,320,128]{2,1,0:T(8,128)}, u32[]{:S(2)}) copy-start(f32[8,320,128]{2,1,0:T(8,128)} %probe.3) | copy-start | bytes 3932164
  40.9 3.9 %copy-start = (bf16[8,320,768]{2,1,0:T(8,128)(2,1)S(1)}, bf16[8,320,768]{2,1,0:T(8,128)(2,1)}, u32[]{:S(2)}) copy-start(bf16[8,320,768]{2,1,0:T(8,128)(2,1)} %get-tuple-element.47.high) | copy-start | bytes 11796484
  41.8 12.5 %collective-permute-start.11 = (f32[320,128]{1,0:T(8,128)S(1)}, f32[320,128]{1,0:T(8,128)S(1)}, u32[]{:S(2)}, u32[]{:S(2)}) collective-permute-start(f32[320,128]{1,0:T(8,128)S(1)} %convolution_add_fusion.5), channel_id=1, source_target_pairs={{1,0},{5,4},{9,8},{13,12},{17,16},{21,20},{25,24},{29,28}} | collective-permute-start | bytes 491528 | tf_op jit(solution)/shard_map/ppermute | solution.py:508
  43.3 27.2 %collective-permute-start.14 = (f32[320,320]{1,0:T(8,128)S(1)}, f32[320,320]{1,0:T(8,128)S(1)}, u32[]{:S(2)}, u32[]{:S(2)}) collective-permute-start(f32[320,320]{1,0:T(8,128)S(1)} %convolution_add_fusion), channel_id=1, source_target_pairs={{2,1},{6,5},{10,9},{14,13},{18,17},{22,21},{26,25},{30,29}} | collective-permute-start | bytes 1228808 | tf_op jit(solution)/shard_map/ppermute | solution.py:508
  45.8 25.1 %collective-permute-start.15 = (f32[320,128]{1,0:T(8,128)S(1)}, f32[320,128]{1,0:T(8,128)S(1)}, u32[]{:S(2)}, u32[]{:S(2)}) collective-permute-start(f32[320,128]{1,0:T(8,128)S(1)} %get-tuple-element.78), channel_id=1, source_target_pairs={{3,2},{7,6},{11,10},{15,14},{19,18},{23,22},{27,26},{31,30}} | collective-permute-start | bytes 491528 | tf_op jit(solution)/shard_map/ppermute | solution.py:508
  63.8 6.7 %collective-permute-start.13 = (f32[320,128]{1,0:T(8,128)S(1)}, f32[320,128]{1,0:T(8,128)S(1)}, u32[]{:S(2)}, u32[]{:S(2)}) collective-permute-start(f32[320,128]{1,0:T(8,128)S(1)} %get-tuple-element.74), channel_id=1, source_target_pairs={{0,1},{4,5},{8,9},{12,13},{16,17},{20,21},{24,25},{28,29}} | collective-permute-start | bytes 491528 | tf_op jit(solution)/shard_map/ppermute | solution.py:508
  71.5 1.7 %collective-permute-start.16 = (f32[320,128]{1,0:T(8,128)S(1)}, f32[320,128]{1,0:T(8,128)S(1)}, u32[]{:S(2)}, u32[]{:S(2)}) collective-permute-start(f32[320,128]{1,0:T(8,128)S(1)} %fusion.1), channel_id=1, source_target_pairs={{1,2},{2,1},{5,6},{6,5},{9,10},{10,9},{13,14},{14,13},{17,18},{18,... | collective-permute-start | bytes 491528 | tf_op jit(solution)/shard_map/ppermute | solution.py:508
  73.2 11.3 %copy-start.4 = (f32[8,320,128]{2,1,0:T(8,128)S(1)}, f32[8,320,128]{2,1,0:T(8,128)}, u32[]{:S(2)}) copy-start(f32[8,320,128]{2,1,0:T(8,128)} %get-tuple-element.73.x) | copy-start | bytes 3932164
  73.6 10.9 %collective-permute-start.17 = (f32[320,128]{1,0:T(8,128)S(1)}, f32[320,128]{1,0:T(8,128)S(1)}, u32[]{:S(2)}, u32[]{:S(2)}) collective-permute-start(f32[320,128]{1,0:T(8,128)S(1)} %add.62), channel_id=1, source_target_pairs={{1,0},{2,3},{5,4},{6,7},{9,8},{10,11},{13,12},{14,15},{17,16},{18,... | collective-permute-start | bytes 491528 | tf_op jit(solution)/shard_map/ppermute | solution.py:508

commit v6 on v5

--- a/solution.py
+++ b/solution.py
@@ -397,29 +397,23 @@
 
 
 def second_ahead_kernel(
-    places, lower, upper, x, high, low, drive_a, drive_b, in_1, in_2, out_0, out_1, out_2,
+    lower, upper, x, high, low, drive_a, drive_b, in_1, in_2, out_0, out_1, out_2,
     y, u, last, l, left_a, left_b, sem,
 ):
-    @pl.when(places[0] != 3)
-    def _():
-        inflow = in_1[...] + in_2[...]
-        outflow = out_0[...] + out_1[...] + out_2[...]
-        sweep_ahead(
-            lower, upper, x, high, low, drive_a, drive_b, inflow, outflow,
-            y, u, l, left_a, left_b, sem,
-        )
-        last[...] = y[y.shape[0] - 1]
-
-    @pl.when(places[0] == 3)
-    def _():
-        last[...] = jnp.zeros_like(last)
-
-
-def second_ahead(places, lower, upper, x, high, low, drive_a, drive_b, *flows):
+    inflow = in_1[...] + in_2[...]
+    outflow = out_0[...] + out_1[...] + out_2[...]
+    sweep_ahead(
+        lower, upper, x, high, low, drive_a, drive_b, inflow, outflow,
+        y, u, l, left_a, left_b, sem,
+    )
+    last[...] = y[y.shape[0] - 1]
+
+
+def second_ahead(lower, upper, x, high, low, drive_a, drive_b, *flows):
     n, b, k = x.shape
     return pl.pallas_call(
         second_ahead_kernel,
-        in_specs=[SMEM] + [HBM] * 2 + [VMEM] * (5 + len(flows)),
+        in_specs=[HBM] * 2 + [VMEM] * (5 + len(flows)),
         out_specs=[VMEM] * 3,
         out_shape=pinned(((n, b, k), F32), ((n, b, b), F32), ((b, k), F32)),
         scratch_shapes=[
@@ -431,7 +425,7 @@
         compiler_params=params(12),
         cost_estimate=cost(0.01),
         name="second_ahead",
-    )(places, *in_hbm(lower, upper), *in_vmem(x, high, low, drive_a, drive_b), *flows)
+    )(*in_hbm(lower, upper), *in_vmem(x, high, low, drive_a, drive_b), *flows)
 
 
 def second_back_kernel(places, y, u, x_of_3, x_out, first, out, left_a, left_b, sem):
@@ -574,7 +568,7 @@
     x_3 = send(first_of_3, (3, 2))
     outflow_0, x_of_3 = together(outflow_0, x_of_3)
     ahead, u, last_y = second_ahead(
-        places, lower, upper, x, high, low, drive_a, drive_b,
+        lower, upper, x, high, low, drive_a, drive_b,
         in_1, in_2, outflow_0, outflow_1, outflow_2,
     )
 

time: 96.4 us -> 95.9 us (level)
  no operation moved by 1% of the time
where the time goes in v6:
time: 95.9 us; the launch traced here: 95.6 us
  Pallas kernels  38.6 us (40%)
  waiting for transfers between devices  20.1 us (21%)
  starting transfers between devices  18.8 us (20%)
  blocking collectives  8.36 us (9%)
  matrix products  6.87 us (7%)
  between operations  1.11 us (1%)
  other arithmetic  0.96 us (1%)
    ppermute x11, waiting for transfers between devices, send(): return lax.ppermute(x, 'dom', list(pairs))  17.2 us
    pallas_call x1, Pallas kernels, local_maps(): pl.pallas_call(local_kernel, in_specs=[HBM] * 4, out_specs=[HBM] * 3 + [V...  14.6 us
    ppermute x11, starting transfers between devices, send(): return lax.ppermute(x, 'dom', list(pairs))  13.6 us
    pallas_call x1, Pallas kernels, second_ahead(): pl.pallas_call(second_ahead_kernel, in_specs=[HBM] * 2 + [VMEM] * (5 + le...  8.88 us
    all_to_all x1, blocking collectives, per_device(): summed = jnp.sum(lax.all_to_all(terms, 'energy', 0, 0, tiled=True), axis=0)  8.36 us
    pallas_call x2, Pallas kernels, drive(): pl.pallas_call(functools.partial(drive_kernel, start), grid=((stop - star...  7.39 us
    dot_general x17, matrix products, mm(): return jnp.dot(a, b, precision=HIGH)  6.87 us
    ppermute x7, starting transfers between devices, near(): lax.ppermute(x, 'energy', [(i, i ^ way) for i in range(peers)])  5.11 us
  transfers between devices with their start and end apart: 18, of which 4 were waited for; matrix products, arithmetic and copies ran while one was open for 5% of the time, Pallas kernels for 38%

profile of v6, /device:TPU:0, one launch (start us, length us, event | category | flops | bytes accessed | tf_op | source)
XLA Modules:
  0.0 95.6 jit_solution(14282219912249647965)
XLA Ops:
  0.0 2.9 %collective-permute-start = (f32[8,40,320]{2,1,0:T(8,128)}, f32[8,40,320]{2,1,0:T(8,128)}, u32[]{:S(2)}, u32[]{:S(2)}) collective-permute-start(f32[8,40,320]{2,1,0:T(8,128)} %rest_0_.3), channel_id=1, source_target_pairs={{0,8},{4,12},{8,0},{12,4},{16,24},{20,28},{24,16},{28,20},{1,9},{5... | collective-permute-start | bytes 1228808 | tf_op jit(solution)/shard_map/ppermute | solution.py:507
  2.9 1.5 %collective-permute-start.2 = (f32[8,40,320]{2,1,0:T(8,128)}, f32[8,40,320]{2,1,0:T(8,128)}, u32[]{:S(2)}, u32[]{:S(2)}) collective-permute-start(f32[8,40,320]{2,1,0:T(8,128)} %rest_0_.3), channel_id=1, source_target_pairs={{0,16},{4,20},{8,24},{12,28},{16,0},{20,4},{24,8},{28,12},{1,17},{... | collective-permute-start | bytes 1228808 | tf_op jit(solution)/shard_map/ppermute | solution.py:507
  4.5 14.6 %local_maps.1 = (f32[8,320,128]{2,1,0:T(8,128)}, bf16[8,320,768]{2,1,0:T(8,128)(2,1)}, bf16[8,320,768]{2,1,0:T(8,128)(2,1)}, f32[320,128]{1,0:T(8,128)S(1)}, f32...) custom-call(f32[8,320,320]{2,1,0:T(8,128)} %bitcast.41, ...), custom_call_target="tpu_custom_call" | custom-call | flops 15000000512 | tf_op jit(solution)/shard_map/local_maps/pallas_call | solution.py:193
  19.1 4.0 %collective-permute-start.1 = (f32[320,128]{1,0:T(8,128)S(1)}, f32[320,128]{1,0:T(8,128)S(1)}, u32[]{:S(2)}, u32[]{:S(2)}) collective-permute-start(f32[320,128]{1,0:T(8,128)S(1)} %get-tuple-element.50), channel_id=1, source_target_pairs={{0,1},{4,5},{8,9},{12,13},{16,17},{20,21},{24,25},{28,29}} | collective-permute-start | bytes 491528 | tf_op jit(solution)/shard_map/ppermute | solution.py:502
  23.2 0.7 collective-permute-start.5
  23.9 2.6 %collective-permute-done.2.rest_4_ = f32[8,40,320]{2,1,0:T(8,128)} collective-permute-done((f32[8,40,320]{2,1,0:T(8,128)}, f32[8,40,320]{2,1,0:T(8,128)}, u32[]{:S(2)}, u32[]{:S(2)}) %collective-permute-start.2) | collective-permute-done | bytes 409632 | tf_op jit(solution)/shard_map/ppermute | solution.py:507
  26.5 0.5 collective-permute-start.8
  27.0 0.1 collective-permute-start.9
  27.1 1.0 %convolution_add_fusion.9 = f32[320,128]{1,0:T(8,128)} fusion(f32[320,128]{1,0:T(8,128)S(1)} %get-tuple-element.50, f32[320,320]{1,0:T(8,128)S(1)} %get-tuple-element.51, f32[320,128]{1,0:T(8,128)S(1)} %collective-permute-done.1.in_1), kind=kOutput, calls=%fused_computation.11 | convolution fusion | flops 78684160 | bytes 901120 | tf_op jit(solution)/shard_map/dot_general | solution.py:498
  28.1 0.8 copy-done.6
  28.9 0.7 collective-permute-start.4
  29.6 0.2 select_reduce_fusion.scale
  29.8 0.3 collective-permute-done.9.rest_7_
  30.1 3.6 %drive_maps.2.drive_a = bf16[4,320,640]{2,1,0:T(8,128)(2,1)S(1)} custom-call(s32[1]{0:T(128)} %bitcast.1.me, f32[8]{0:T(128)S(1)} %select_reduce_fusion.scale, f32[8,320,320]{2,1,0:T(8,128)} %bitcast.42, f32[8,40,320]{2,1,0:T(8,128)} %rest_0_.3, f32[8,40,320]{2,1,0:T(8,128)} %copy-done.6, f32[8,40,320]{2,1,0:T(8,128)} %collective-permute-done.rest_2_, ...), custom_call_target="tpu_custom_call" | custom-call | flops 10000000 | tf_op jit(solution)/shard_map/drive_maps/pallas_call | solution.py:252
  33.7 0.3 convolution_add_fusion.7
  34.1 0.3 slice_add_fusion.out_2
  34.4 0.3 convolution_add_fusion.8
  34.7 0.3 convolution_add_fusion.6
  35.1 0.7 collective-permute-start.10
  35.8 0.6 fusion.8
  36.4 0.7 collective-permute-start.12
  37.1 3.8 %drive_maps.3.drive_b = bf16[4,320,640]{2,1,0:T(8,128)(2,1)S(1)} custom-call(s32[1]{0:T(128)} %bitcast.1.me, f32[8]{0:T(128)S(1)} %select_reduce_fusion.scale, f32[8,320,320]{2,1,0:T(8,128)} %bitcast.43, f32[8,40,320]{2,1,0:T(8,128)} %rest_0_.3, f32[8,40,320]{2,1,0:T(8,128)} %copy-done.6, f32[8,40,320]{2,1,0:T(8,128)} %collective-permute-done.rest_2_, ...), custom_call_target="tpu_custom_call" | custom-call | flops 10000000 | tf_op jit(solution)/shard_map/drive_maps/pallas_call | solution.py:252
  40.9 0.6 convolution_add_fusion
  41.5 0.3 convolution_add_fusion.5
  41.8 1.4 %collective-permute-start.11 = (f32[320,128]{1,0:T(8,128)S(1)}, f32[320,128]{1,0:T(8,128)S(1)}, u32[]{:S(2)}, u32[]{:S(2)}) collective-permute-start(f32[320,128]{1,0:T(8,128)S(1)} %convolution_add_fusion.5), channel_id=1, source_target_pairs={{1,0},{5,4},{9,8},{13,12},{17,16},{21,20},{25,24},{29,28}} | collective-permute-start | bytes 491528 | tf_op jit(solution)/shard_map/ppermute | solution.py:502
  43.3 0.7 collective-permute-start.14
  44.7 0.1 pad_add_fusion.places
  44.8 1.0 %second_of_3.1 = (f32[8,320,128]{2,1,0:T(8,128)}, f32[320,128]{1,0:T(8,128)S(1)}) custom-call(s32[2]{0:T(128)S(1)} %pad_add_fusion.places, f32[8,320,320]{2,1,0:T(8,128)} %bitcast.36, f32[8,320,320]{2,1,0:T(8,128)} %bitcast.39, f32[8,320,128]{2,1,0:T(8,128)S(1)} %copy-done.2, bf16[8,320,768]{2,1,0:T(8,128)(2,1)S(1)} %copy-done, ...), custom_call_target="tpu_custom_call" | custom-call | flops 10000000 | tf_op jit(solution)/shard_map/second_of_3/pallas_call | solution.py:378
  45.8 0.7 collective-permute-start.15
  46.4 7.9 %collective-permute-done.11.out_0 = f32[320,128]{1,0:T(8,128)S(1)} collective-permute-done((f32[320,128]{1,0:T(8,128)S(1)}, f32[320,128]{1,0:T(8,128)S(1)}, u32[]{:S(2)}, u32[]{:S(2)}) %collective-permute-start.11) | collective-permute-done | bytes 163872 | tf_op jit(solution)/shard_map/ppermute | solution.py:502
  54.4 8.9 %second_ahead.1 = (f32[8,320,128]{2,1,0:T(8,128)S(1)}, f32[8,320,320]{2,1,0:T(8,128)S(1)}, f32[320,128]{1,0:T(8,128)S(1)}) custom-call(f32[8,320,320]{2,1,0:T(8,128)} %bitcast.37, f32[8,320,320]{2,1,0:T(8,128)} %bitcast.40, f32[8,320,128]{2,1,0:T(8,128)S(1)} %copy-done.2, bf16[8,320,768]{2,1,0:T(8,128)(2,1)S(1)} %copy-done, ...), custom_call_target="tpu_custom_call" | custom-call | flops 10000000 | tf_op jit(solution)/shard_map/second_ahead/pallas_call | solution.py:414
  63.2 2.2 %collective-permute-start.13 = (f32[320,128]{1,0:T(8,128)S(1)}, f32[320,128]{1,0:T(8,128)S(1)}, u32[]{:S(2)}, u32[]{:S(2)}) collective-permute-start(f32[320,128]{1,0:T(8,128)S(1)} %get-tuple-element.74), channel_id=1, source_target_pairs={{0,1},{4,5},{8,9},{12,13},{16,17},{20,21},{24,25},{28,29}} | collective-permute-start | bytes 491528 | tf_op jit(solution)/shard_map/ppermute | solution.py:502
  65.5 4.0 %second_back.1 = (f32[8,320,128]{2,1,0:T(8,128)}, f32[320,128]{1,0:T(8,128)S(1)}) custom-call(s32[2]{0:T(128)S(1)} %pad_add_fusion.places, f32[8,320,128]{2,1,0:T(8,128)S(1)} %get-tuple-element.70.y, f32[8,320,320]{2,1,0:T(8,128)S(1)} %get-tuple-element.71.u, f32[8,320,128]{2,1,0:T(8,128)} %get-tuple-element.72.x_of_3), custom_call_target="tpu_custom_call", output_to_operand_aliasing={{0}: (3, {})} | custom-call | flops 10000000 | tf_op jit(solution)/shard_map/second_back/pallas_call | solution.py:444
  69.5 0.3 fusion.6
  69.9 0.3 convolution_add_fusion.3
  70.2 0.3 fusion.11
  70.6 0.3 fusion.1
  70.9 0.7 collective-permute-start.16
  71.6 0.3 fusion.12
  71.9 0.3 fusion.13
  72.3 0.3 fusion.2
  72.6 0.3 fusion.14
  73.0 1.3 %collective-permute-start.17 = (f32[320,128]{1,0:T(8,128)S(1)}, f32[320,128]{1,0:T(8,128)S(1)}, u32[]{:S(2)}, u32[]{:S(2)}) collective-permute-start(f32[320,128]{1,0:T(8,128)S(1)} %add.62), channel_id=1, source_target_pairs={{1,0},{2,3},{5,4},{6,7},{9,8},{10,11},{13,12},{14,15},{17,16},{18,... | collective-permute-start | bytes 491528 | tf_op jit(solution)/shard_map/ppermute | solution.py:502
  74.3 0.3 convolution_add_fusion.1.out_2
  74.7 9.3 %collective-permute-done.17.ended = f32[320,128]{1,0:T(8,128)S(1)} collective-permute-done((f32[320,128]{1,0:T(8,128)S(1)}, f32[320,128]{1,0:T(8,128)S(1)}, u32[]{:S(2)}, u32[]{:S(2)}) %collective-permute-start.17) | collective-permute-done | bytes 163872 | tf_op jit(solution)/shard_map/ppermute | solution.py:502
  84.0 2.7 %charge_terms.1 = f32[8,8,128]{2,1,0:T(8,128)S(1)} custom-call(s32[2]{0:T(128)S(1)} %pad_add_fusion.places, f32[1]{0:T(128)S(6)} %div.3.weight, f32[8,320,128]{2,1,0:T(8,128)S(1)} %copy-done.4, bf16[8,320,768]{2,1,0:T(8,128)(2,1)S(1)} %copy-done, bf16[8,320,768]{2,1,0:T(8,128)(2,1)S(1)} %copy-done.1, f32[8,320,128]{2,1,0:T(8,128)S(1)} %copy-done.3, ...), custom_call_target="tpu_custom_call" | custom-call | tf_op jit(solution)/shard_map/charge_terms/pallas_call | solution.py:486
  86.6 8.4 %all_to_all.5 = f32[8,8,128]{2,1,0:T(8,128)S(1)} all-to-all(f32[8,8,128]{2,1,0:T(8,128)S(1)} %charge_terms.1), channel_id=1, replica_groups=mesh['energy'=8,'dom'=4] {'energy'}, dimensions={0} | all-to-all | bytes 65536 | tf_op jit(solution)/shard_map/all_to_all | solution.py:594
  95.0 0.6 reduce_sum.19
  (37 shorter events, 0.2 us)
Async XLA Ops:
  0.0 19.1 %collective-permute-start = (f32[8,40,320]{2,1,0:T(8,128)}, f32[8,40,320]{2,1,0:T(8,128)}, u32[]{:S(2)}, u32[]{:S(2)}) collective-permute-start(f32[8,40,320]{2,1,0:T(8,128)} %rest_0_.3), channel_id=1, source_target_pairs={{0,8},{4,12},{8,0},{12,4},{16,24},{20,28},{24,16},{28,20},{1,9},{5... | collective-permute-start | bytes 1228808 | tf_op jit(solution)/shard_map/ppermute | solution.py:507
  2.9 23.5 %collective-permute-start.2 = (f32[8,40,320]{2,1,0:T(8,128)}, f32[8,40,320]{2,1,0:T(8,128)}, u32[]{:S(2)}, u32[]{:S(2)}) collective-permute-start(f32[8,40,320]{2,1,0:T(8,128)} %rest_0_.3), channel_id=1, source_target_pairs={{0,16},{4,20},{8,24},{12,28},{16,0},{20,4},{24,8},{28,12},{1,17},{... | collective-permute-start | bytes 1228808 | tf_op jit(solution)/shard_map/ppermute | solution.py:507
  4.5 22.0 %collective-permute-start.3 = (f32[8,40,320]{2,1,0:T(8,128)}, f32[8,40,320]{2,1,0:T(8,128)}, u32[]{:S(2)}, u32[]{:S(2)}) collective-permute-start(f32[8,40,320]{2,1,0:T(8,128)} %rest_0_.3), channel_id=1, source_target_pairs={{0,24},{4,28},{8,16},{12,20},{16,8},{20,12},{24,0},{28,4},{1,25},{... | collective-permute-start | bytes 1228808 | tf_op jit(solution)/shard_map/ppermute | solution.py:507
  4.5 18.6 %copy-start.5 = (f32[8,40,320]{2,1,0:T(8,128)S(1)}, f32[8,40,320]{2,1,0:T(8,128)}, u32[]{:S(2)}) copy-start(f32[8,40,320]{2,1,0:T(8,128)} %rest_0_.3) | copy-start | bytes 1228804
  4.5 25.1 %copy-start.7 = (f32[32]{0:T(128)S(1)}, f32[32]{0:T(128)}, u32[]{:S(2)}) copy-start(f32[32]{0:T(128)} %param.13) | copy-start | bytes 388
  4.5 25.1 %copy-start.8 = (s32[8]{0:T(128)S(1)}, s32[8]{0:T(128)}, u32[]{:S(2)}) copy-start(s32[8]{0:T(128)} %param.12) | copy-start | bytes 100
  19.1 7.3 %collective-permute-start.1 = (f32[320,128]{1,0:T(8,128)S(1)}, f32[320,128]{1,0:T(8,128)S(1)}, u32[]{:S(2)}, u32[]{:S(2)}) collective-permute-start(f32[320,128]{1,0:T(8,128)S(1)} %get-tuple-element.50), channel_id=1, source_target_pairs={{0,1},{4,5},{8,9},{12,13},{16,17},{20,21},{24,25},{28,29}} | collective-permute-start | bytes 491528 | tf_op jit(solution)/shard_map/ppermute | solution.py:502
  23.1 5.0 %collective-permute-start.6 = (f32[8,40,320]{2,1,0:T(8,128)S(1)}, f32[8,40,320]{2,1,0:T(8,128)S(1)}, u32[]{:S(2)}, u32[]{:S(2)}) collective-permute-start(f32[8,40,320]{2,1,0:T(8,128)S(1)} %copy-done.5), channel_id=1, source_target_pairs={{0,4},{4,0},{8,12},{12,8},{16,20},{20,16},{24,28},{28,24},{1,5},{5... | collective-permute-start | bytes 1228808 | tf_op jit(solution)/shard_map/ppermute | solution.py:507
  23.2 10.5 %collective-permute-start.5 = (f32[320,448]{1,0:T(8,128)S(1)}, f32[320,448]{1,0:T(8,128)S(1)}, u32[]{:S(2)}, u32[]{:S(2)}) collective-permute-start(f32[320,448]{1,0:T(8,128)S(1)} %get-tuple-element.53), channel_id=1, source_target_pairs={{3,2},{7,6},{11,10},{15,14},{19,18},{23,22},{27,26},{31,30}} | collective-permute-start | bytes 1720328 | tf_op jit(solution)/shard_map/ppermute | solution.py:502
  26.5 3.3 %collective-permute-start.7 = (f32[8,40,320]{2,1,0:T(8,128)}, f32[8,40,320]{2,1,0:T(8,128)}, u32[]{:S(2)}, u32[]{:S(2)}) collective-permute-start(f32[8,40,320]{2,1,0:T(8,128)} %collective-permute-done.rest_2_), channel_id=1, source_target_pairs={{0,4},{4,0},{8,12},{12,8},{16,20},{20,16},{24,28},{28,24},{1,5},{5... | collective-permute-start | bytes 1228808 | tf_op jit(solution)/shard_map/ppermute | solution.py:507
  26.5 3.3 %collective-permute-start.8 = (f32[8,40,320]{2,1,0:T(8,128)}, f32[8,40,320]{2,1,0:T(8,128)}, u32[]{:S(2)}, u32[]{:S(2)}) collective-permute-start(f32[8,40,320]{2,1,0:T(8,128)} %collective-permute-done.2.rest_4_), channel_id=1, source_target_pairs={{0,4},{4,0},{8,12},{12,8},{16,20},{20,16},{24,28},{28,24},{1,5},{5... | collective-permute-start | bytes 1228808 | tf_op jit(solution)/shard_map/ppermute | solution.py:507
  27.0 3.1 %collective-permute-start.9 = (f32[8,40,320]{2,1,0:T(8,128)}, f32[8,40,320]{2,1,0:T(8,128)}, u32[]{:S(2)}, u32[]{:S(2)}) collective-permute-start(f32[8,40,320]{2,1,0:T(8,128)} %collective-permute-done.3.rest_6_), channel_id=1, source_target_pairs={{0,4},{4,0},{8,12},{12,8},{16,20},{20,16},{24,28},{28,24},{1,5},{5... | collective-permute-start | bytes 1228808 | tf_op jit(solution)/shard_map/ppermute | solution.py:507
  28.1 0.8 copy-start.6
  28.9 4.8 %collective-permute-start.4 = (f32[320,128]{1,0:T(8,128)}, f32[320,128]{1,0:T(8,128)S(1)}, u32[]{:S(2)}, u32[]{:S(2)}) collective-permute-start(f32[320,128]{1,0:T(8,128)} %convolution_add_fusion.9), channel_id=1, source_target_pairs={{1,2},{5,6},{9,10},{13,14},{17,18},{21,22},{25,26},{29,30}} | collective-permute-start | bytes 491528 | tf_op jit(solution)/shard_map/ppermute | solution.py:502
  35.1 6.4 %collective-permute-start.10 = (f32[320,128]{1,0:T(8,128)S(1)}, f32[320,128]{1,0:T(8,128)S(1)}, u32[]{:S(2)}, u32[]{:S(2)}) collective-permute-start(f32[320,128]{1,0:T(8,128)S(1)} %convolution_add_fusion.6), channel_id=1, source_target_pairs={{2,1},{6,5},{10,9},{14,13},{18,17},{22,21},{26,25},{30,29}} | collective-permute-start | bytes 491528 | tf_op jit(solution)/shard_map/ppermute | solution.py:502
  36.4 8.4 %collective-permute-start.12 = (f32[320,128]{1,0:T(8,128)S(1)}, f32[320,128]{1,0:T(8,128)S(1)}, u32[]{:S(2)}, u32[]{:S(2)}) collective-permute-start(f32[320,128]{1,0:T(8,128)S(1)} %convolution_add_fusion.7), channel_id=1, source_target_pairs={{2,3},{6,7},{10,11},{14,15},{18,19},{22,23},{26,27},{30,31}} | collective-permute-start | bytes 491528 | tf_op jit(solution)/shard_map/ppermute | solution.py:502
  37.0 7.7 %copy-start.1 = (bf16[8,320,768]{2,1,0:T(8,128)(2,1)S(1)}, bf16[8,320,768]{2,1,0:T(8,128)(2,1)}, u32[]{:S(2)}) copy-start(bf16[8,320,768]{2,1,0:T(8,128)(2,1)} %get-tuple-element.48.low) | copy-start | bytes 11796484
  37.1 7.7 %copy-start.2 = (f32[8,320,128]{2,1,0:T(8,128)S(1)}, f32[8,320,128]{2,1,0:T(8,128)}, u32[]{:S(2)}) copy-start(f32[8,320,128]{2,1,0:T(8,128)} %get-tuple-element.46.x) | copy-start | bytes 3932164
  37.1 7.7 %copy-start.3 = (f32[8,320,128]{2,1,0:T(8,128)S(1)}, f32[8,320,128]{2,1,0:T(8,128)}, u32[]{:S(2)}) copy-start(f32[8,320,128]{2,1,0:T(8,128)} %probe.3) | copy-start | bytes 3932164
  40.9 3.9 %copy-start = (bf16[8,320,768]{2,1,0:T(8,128)(2,1)S(1)}, bf16[8,320,768]{2,1,0:T(8,128)(2,1)}, u32[]{:S(2)}) copy-start(bf16[8,320,768]{2,1,0:T(8,128)(2,1)} %get-tuple-element.47.high) | copy-start | bytes 11796484
  41.8 12.5 %collective-permute-start.11 = (f32[320,128]{1,0:T(8,128)S(1)}, f32[320,128]{1,0:T(8,128)S(1)}, u32[]{:S(2)}, u32[]{:S(2)}) collective-permute-start(f32[320,128]{1,0:T(8,128)S(1)} %convolution_add_fusion.5), channel_id=1, source_target_pairs={{1,0},{5,4},{9,8},{13,12},{17,16},{21,20},{25,24},{29,28}} | collective-permute-start | bytes 491528 | tf_op jit(solution)/shard_map/ppermute | solution.py:502
  43.3 26.6 %collective-permute-start.14 = (f32[320,320]{1,0:T(8,128)S(1)}, f32[320,320]{1,0:T(8,128)S(1)}, u32[]{:S(2)}, u32[]{:S(2)}) collective-permute-start(f32[320,320]{1,0:T(8,128)S(1)} %convolution_add_fusion), channel_id=1, source_target_pairs={{2,1},{6,5},{10,9},{14,13},{18,17},{22,21},{26,25},{30,29}} | collective-permute-start | bytes 1228808 | tf_op jit(solution)/shard_map/ppermute | solution.py:502
  45.8 24.5 %collective-permute-start.15 = (f32[320,128]{1,0:T(8,128)S(1)}, f32[320,128]{1,0:T(8,128)S(1)}, u32[]{:S(2)}, u32[]{:S(2)}) collective-permute-start(f32[320,128]{1,0:T(8,128)S(1)} %get-tuple-element.78), channel_id=1, source_target_pairs={{3,2},{7,6},{11,10},{15,14},{19,18},{23,22},{27,26},{31,30}} | collective-permute-start | bytes 491528 | tf_op jit(solution)/shard_map/ppermute | solution.py:502
  63.2 6.6 %collective-permute-start.13 = (f32[320,128]{1,0:T(8,128)S(1)}, f32[320,128]{1,0:T(8,128)S(1)}, u32[]{:S(2)}, u32[]{:S(2)}) collective-permute-start(f32[320,128]{1,0:T(8,128)S(1)} %get-tuple-element.74), channel_id=1, source_target_pairs={{0,1},{4,5},{8,9},{12,13},{16,17},{20,21},{24,25},{28,29}} | collective-permute-start | bytes 491528 | tf_op jit(solution)/shard_map/ppermute | solution.py:502
  70.9 1.7 %collective-permute-start.16 = (f32[320,128]{1,0:T(8,128)S(1)}, f32[320,128]{1,0:T(8,128)S(1)}, u32[]{:S(2)}, u32[]{:S(2)}) collective-permute-start(f32[320,128]{1,0:T(8,128)S(1)} %fusion.1), channel_id=1, source_target_pairs={{1,2},{2,1},{5,6},{6,5},{9,10},{10,9},{13,14},{14,13},{17,18},{18,... | collective-permute-start | bytes 491528 | tf_op jit(solution)/shard_map/ppermute | solution.py:502
  72.6 11.3 %copy-start.4 = (f32[8,320,128]{2,1,0:T(8,128)S(1)}, f32[8,320,128]{2,1,0:T(8,128)}, u32[]{:S(2)}) copy-start(f32[8,320,128]{2,1,0:T(8,128)} %get-tuple-element.73.x) | copy-start | bytes 3932164
  73.0 11.0 %collective-permute-start.17 = (f32[320,128]{1,0:T(8,128)S(1)}, f32[320,128]{1,0:T(8,128)S(1)}, u32[]{:S(2)}, u32[]{:S(2)}) collective-permute-start(f32[320,128]{1,0:T(8,128)S(1)} %add.62), channel_id=1, source_target_pairs={{1,0},{2,3},{5,4},{6,7},{9,8},{10,11},{13,12},{14,15},{17,16},{18,... | collective-permute-start | bytes 491528 | tf_op jit(solution)/shard_map/ppermute | solution.py:502
